TPU v7x, 32 devices: a whole 2x2x4 slice. The times are simulated.
32 devices in a mesh: design: 2 (over y), leaf: 4 (over z), vec: 2 (over x), sub: 2 (over core).
Axes of the slice: x: 2, y: 2, z: 4, core: 2. Of those that a mesh axis runs over, the one named last changes fastest.
Arguments:
- adjoint: bfloat16 [64, 32, 256], P(('design', 'leaf', 'vec'), 'sub'), parts along dimension 0, may hold values from -6 to 6
- leaf_basis_out: bfloat16 [64, 64, 256], P(('design', 'leaf', 'vec')), parts along dimension 0, may hold values from -0.375 to 0.375
- leaf_basis_in: bfloat16 [64, 64, 256], P(('design', 'leaf', 'vec')), parts along dimension 0, may hold values from -0.75 to 0.75
- transfer_up: bfloat16 [16, 64, 256], P(('design', 'leaf', 'vec')), parts along dimension 0, may hold values from -0.375 to 0.375
- transfer_down: bfloat16 [16, 64, 256], P(('design', 'leaf', 'vec')), parts along dimension 0, may hold values from -0.75 to 0.75
- far_coupling: bfloat16 [64, 64, 512], P(('design', 'leaf', 'vec')), parts along dimension 0, may hold values from -0.25 to 0.25
- top_coupling: bfloat16 [16, 64, 1024], P(('design', 'leaf', 'vec')), parts along dimension 0, may hold values from -0.1875 to 0.1875
- near_tiles: bfloat16 [64, 768, 256], P(('design', 'leaf', 'vec')), parts along dimension 0, may hold values from -0.21875 to 0.21875
- near_src: int32 [64, 3], P(('design', 'leaf', 'vec')), parts along dimension 0, may hold values from 0 to 31, as said below
- far_dst: int32 [64, 8], P(('design', 'leaf', 'vec')), parts along dimension 0, may hold values from 0 to 31, as said below
- top_src: int32 [16, 16], P(('design', 'leaf', 'vec')), parts along dimension 0, may hold values from 0 to 7, as said below
Outputs:
- response: float32 [64, 32, 256], P(('design', 'leaf', 'vec'), 'sub'), parts along dimension 0
There are 2 independent parts, one for each index of `design`. A program takes and returns all parts, laid end to end along the dimension named above; each array names one. Nothing has to cross between parts.
Inputs may be any that keep to these rules, and one draw needn't show every extreme that they name: `near_src`: entry 0 of row j is j itself; the other entries lie in j's aligned block of 4 leaves or in the aligned blocks just before and after it. `far_dst`: entry [i, k] lies in an aligned block of 4 leaves that is 1 to 4 blocks away from i's block. The targets that the rows of one block name within any one other block are at most 2 distinct leaves; every block reaches 2 in some other block. `top_src`: entry [D, k] differs from D by 1 to 8 - 1 modulo 8; entry [D, 0] is D - 1 modulo 8.
All inputs are finite; a program needn't handle non-finite values.
Results may differ from a plain program's by a relative error of at most 0.0042.
Values may be sent and summed in bfloat16 or wider, within the bound.
No kernel may reach another device: no remote copies, remote signals or barrier semaphores. Data moves between devices by JAX's collectives and lax.ppermute only.
A program may use at most 64 MiB of HBM per device.

v0:
```python
import jax
import jax.numpy as jnp
from jax import lax
from jax.sharding import PartitionSpec as P


def padded_2(cells, sides, width):
    for axis, dim in sides:
        count = lax.axis_size(axis)
        ends = count - 1
        head = lax.slice_in_dim(cells, 0, width, axis=dim)
        tail = lax.slice_in_dim(cells, cells.shape[dim] - width, cells.shape[dim], axis=dim)
        cells = jnp.concatenate(
            [
                lax.ppermute(tail, axis, [(i, (i + 1) % count) for i in range(ends)]),
                cells,
                lax.ppermute(head, axis, [((i + 1) % count, i) for i in range(ends)]),
            ],
            axis=dim,
        )
    return cells


def on_device(
    adjoint,
    leaf_basis_out,
    leaf_basis_in,
    transfer_up,
    transfer_down,
    far_coupling,
    top_coupling,
    near_tiles,
    near_src,
    far_dst,
    top_src,
):
    f32 = jnp.float32
    bf16 = jnp.bfloat16
    highest = lax.Precision.HIGHEST
    leaf_dev, vectors, cells = adjoint.shape
    rank = leaf_basis_out.shape[1]
    far_count = far_dst.shape[1]
    top_count = top_src.shape[1]
    near_count = near_src.shape[1]
    width = vectors * rank
    nodes = lax.axis_size(("leaf", "vec"))
    myself = lax.axis_index(("leaf", "vec"))
    first = myself * leaf_dev
    total_leaves = nodes * leaf_dev
    leaf_coef = jnp.einsum(
        "jvc,jrc->jvr", adjoint, leaf_basis_out, preferred_element_type=f32
    ).astype(bf16)
    side = leaf_coef.transpose(1, 0, 2).reshape(vectors, leaf_dev * rank)
    node_coef = jnp.einsum("vm,rm->vr", side, transfer_up[0], preferred_element_type=f32).astype(
        bf16
    )
    everyone = lax.all_gather(node_coef.reshape(1, width), ("leaf", "vec"), axis=0, tiled=True)
    picked = jnp.take(everyone, top_src[0], axis=0)
    picked = (
        picked.reshape(top_count, vectors, rank)
        .transpose(1, 0, 2)
        .reshape(vectors, top_count * rank)
    )
    top_in = jnp.einsum("vm,rm->vr", picked, top_coupling[0], preferred_element_type=f32).astype(
        bf16
    )
    down = jnp.dot(top_in, transfer_down[0], preferred_element_type=f32)
    down = down.reshape(vectors, leaf_dev, rank).transpose(1, 0, 2)
    contrib = jnp.einsum("ivr,irm->ivm", leaf_coef, far_coupling, preferred_element_type=f32)
    contrib = (
        contrib.reshape(leaf_dev, vectors, far_count, rank)
        .transpose(0, 2, 1, 3)
        .reshape(leaf_dev * far_count, width)
    )
    targets = far_dst.reshape(-1)
    every_leaf = jnp.arange(total_leaves, dtype=jnp.int32)
    named = (targets[:, None] == every_leaf[None, :]).astype(f32)
    accum = jnp.einsum("et,ew->tw", named, contrib, precision=highest)
    leaf_in = lax.psum_scatter(accum, ("leaf", "vec"), scatter_dimension=0, tiled=True)
    mixed = (leaf_in.reshape(leaf_dev, vectors, rank) + down).astype(bf16)
    far_out = jnp.einsum("jvr,jrc->jvc", mixed, leaf_basis_in, preferred_element_type=f32)
    padded = padded_2(adjoint, ((("leaf", "vec"), 0),), leaf_dev)
    local_source = near_src - (first - leaf_dev)
    blocks = jnp.take(padded, local_source.reshape(-1), axis=0).reshape(
        leaf_dev, near_count, vectors, cells
    )
    tiles = near_tiles.reshape(leaf_dev, near_count, cells, cells)
    near_out = jnp.einsum("jkvc,jkcd->jvd", blocks, tiles, preferred_element_type=f32)
    return far_out + near_out


def solution(mesh):
    in_specs = (
        P(("design", "leaf", "vec"), "sub", None),
        P(("design", "leaf", "vec"), None, None),
        P(("design", "leaf", "vec"), None, None),
        P(("design", "leaf", "vec"), None, None),
        P(("design", "leaf", "vec"), None, None),
        P(("design", "leaf", "vec"), None, None),
        P(("design", "leaf", "vec"), None, None),
        P(("design", "leaf", "vec"), None, None),
        P(("design", "leaf", "vec"), None),
        P(("design", "leaf", "vec"), None),
        P(("design", "leaf", "vec"), None),
    )
    out_specs = P(("design", "leaf", "vec"), "sub", None)
    return jax.shard_map(
        on_device, mesh=mesh, in_specs=in_specs, out_specs=out_specs, check_vma=False
    )
```

profile of v0, /device:TPU:0, one launch (start us, length us, event | category | flops | bytes accessed | tf_op | source)
XLA Modules:
  0.0 97.8 jit_solution(16214450385330026660)
XLA Ops:
  6.5 0.0 copy-start
  6.5 0.0 copy-start.6
  6.5 0.0 copy-start.8
  6.5 0.0 copy-start.2
  6.6 0.0 all-reduce.3.cloned.1.call-start
  6.6 1.4 %collective-permute-start.1 = (bf16[4,16,256]{2,1,0:T(8,128)(2,1)}, bf16[4,16,256]{2,1,0:T(8,128)(2,1)S(1)}, u32[]{:S(2)}, u32[]{:S(2)}) collective-permute-start(bf16[4,16,256]{2,1,0:T(8,128)(2,1)} %param.11), channel_id=1, source_target_pairs={{2,0},{4,2},{6,4},{8,6},{10,8},{12,10},{14,12},{3,1},{5,3},{7,5},{... | collective-permute-start | bytes 98312 | tf_op jit(solution)/shard_map/ppermute | solution.py:17
  8.0 5.5 %collective-permute-start = (bf16[4,16,256]{2,1,0:T(8,128)(2,1)}, bf16[4,16,256]{2,1,0:T(8,128)(2,1)S(1)}, u32[]{:S(2)}, u32[]{:S(2)}) collective-permute-start(bf16[4,16,256]{2,1,0:T(8,128)(2,1)} %param.11), channel_id=1, source_target_pairs={{0,2},{2,4},{4,6},{6,8},{8,10},{10,12},{12,14},{1,3},{3,5},{5,7},{... | collective-permute-start | bytes 98312 | tf_op jit(solution)/shard_map/ppermute | solution.py:15
  13.5 1.1 %convolution_convert_fusion = bf16[4,16,64]{2,1,0:T(8,128)(2,1)S(1)} fusion(bf16[4,16,256]{2,1,0:T(8,128)(2,1)} %param.11, bf16[4,64,256]{2,1,0:T(8,128)(2,1)} %param.12), kind=kOutput, calls=%fused_computation.7 | convolution fusion | flops 2101248 | bytes 172032 | tf_op jit(solution)/shard_map/jvc,jrc->jvr/dot_general | solution.py:50
  14.6 0.0 copy-start.4
  14.6 0.0 copy-start.9
  14.6 0.0 copy-start.3
  14.6 1.1 %fusion.16 = f32[4,16,512]{2,1,0:T(8,128)S(1)} fusion(bf16[4,16,64]{2,1,0:T(8,128)(2,1)S(1)} %convolution_convert_fusion, bf16[4,64,512]{2,1,0:T(8,128)(2,1)} %param.16), kind=kOutput, calls=%fused_computation.38 | convolution fusion | flops 4194304 | bytes 401408 | tf_op jit(solution)/shard_map/ivr,irm->ivm/dot_general | solution.py:69
  15.7 0.1 reshape.104
  15.9 0.0 copy-start.1
  15.9 0.1 reshape.105
  16.1 0.0 copy-done.6
  16.1 0.1 eq.15
  16.1 1.0 fusion.11
  17.1 0.0 all-reduce.3.cloned.1.call-update
  17.1 0.0 copy-done.8
  17.2 0.1 reshape.107
  17.3 0.0 copy-done.5
  17.3 0.1 convolution_convert_fusion.2
  17.4 0.1 reshape.128
  17.5 31.4 %all-gather = bf16[8,1,1024]{2,1,0:T(2,128)(2,1)S(1)} all-gather(bf16[1,1,1024]{2,1,0:T(2,128)(2,1)S(1)} %reshape.128), channel_id=1, replica_groups=mesh['design'=2,'leaf'=4,'vec'=2,'sub'=2] {'leaf','vec'}, dimensions={0}, use_global_device_ids=true | all-gather | bytes 18432 | tf_op jit(solution)/shard_map/all_gather | solution.py:57
  48.9 0.6 gather_fusion
  49.5 0.1 gather.13
  49.6 0.1 fusion.8
  49.7 0.1 reshape.109
  49.8 0.0 copy-done.7
  49.8 0.1 reshape.110
  49.9 0.0 copy-done.2
  49.9 0.1 fusion.4
  50.1 0.0 copy-done.4
  50.1 0.1 copy.26
  50.2 0.0 copy-done.9
  50.2 0.6 dynamic-slice
  51.4 0.0 collective-permute-done.1
  51.5 0.0 collective-permute-done
  51.5 0.0 copy-done.3
  51.5 0.6 gather_fusion.1
  52.1 36.7 %all-reduce.3.cloned.1.call-done = f32[32,1024]{1,0:T(8,128)} async-done(((f32[32,1024]{1,0:T(8,128)}), f32[32,1024]{1,0:T(8,128)}) %all-reduce.3.cloned.1.call-update) | async-done | bytes 131088
  88.8 0.8 constant_dynamic-slice_fusion
  89.6 0.1 reshape.106
  89.6 0.0 copy-done.1
  89.6 0.3 fusion.3
  89.9 0.0 copy-done
  89.9 1.0 %fusion = f32[4,16,256]{2,1,0:T(8,128)} fusion(f32[4,16,256]{2,1,0:T(8,128)S(1)} %fusion.3, bf16[4,3,256,256]{3,2,1,0:T(8,128)(2,1)S(1)} %bitcast.58, bf16[4,3,16,256]{3,2,1,0:T(8,128)(2,1)S(1)} %bitcast.61, pred[4,3]{1,0:T(4,128)(4,1)S(1)} %get-tuple-element.5), kind=kOutput, calls=%fused_computation.3 | convolution fusion | flops 25231360 | bytes 1802252 | tf_op jit(solution)/shard_map/jkvc,jkcd->jvd/dot_general | solution.py:88
  (12 shorter events, 0.1 us)
Async XLA Ops:
  6.5 83.4 %copy-start = (bf16[4,768,256]{2,1,0:T(8,128)(2,1)S(1)}, bf16[4,768,256]{2,1,0:T(8,128)(2,1)}, u32[]{:S(2)}) copy-start(bf16[4,768,256]{2,1,0:T(8,128)(2,1)} %param.18) | copy-start | bytes 4718596
  6.5 9.5 %copy-start.6 = (s32[4,8]{1,0:T(4,128)S(1)}, s32[4,8]{1,0:T(4,128)}, u32[]{:S(2)}) copy-start(s32[4,8]{1,0:T(4,128)} %param.20) | copy-start | bytes 388
  6.5 10.6 %copy-start.8 = (s32[1,16]{1,0:T(1,128)S(1)}, s32[1,16]{1,0:T(1,128)}, u32[]{:S(2)}) copy-start(s32[1,16]{1,0:T(1,128)} %param.21) | copy-start | bytes 196
  6.5 10.7 %copy-start.5 = (bf16[1,64,256]{2,1,0:T(8,128)(2,1)S(1)}, bf16[1,64,256]{2,1,0:T(8,128)(2,1)}, u32[]{:S(2)}) copy-start(bf16[1,64,256]{2,1,0:T(8,128)(2,1)} %param.14) | copy-start | bytes 98308
  6.5 43.2 %copy-start.7 = (s32[4,3]{1,0:T(4,128)S(1)}, s32[4,3]{1,0:T(4,128)}, u32[]{:S(2)}) copy-start(s32[4,3]{1,0:T(4,128)} %param.19) | copy-start | bytes 148
  6.5 43.4 %copy-start.2 = (bf16[1,64,1024]{2,1,0:T(8,128)(2,1)S(1)}, bf16[1,64,1024]{2,1,0:T(8,128)(2,1)}, u32[]{:S(2)}) copy-start(bf16[1,64,1024]{2,1,0:T(8,128)(2,1)} %param.17) | copy-start | bytes 393220
  6.6 82.2 %all-reduce.3.cloned.1.call-start = ((), (), s32[]{:S(2)}) async-start(), calls=%async_computation | async-start | bytes 262144
  6.6 44.8 %collective-permute-start.1 = (bf16[4,16,256]{2,1,0:T(8,128)(2,1)}, bf16[4,16,256]{2,1,0:T(8,128)(2,1)S(1)}, u32[]{:S(2)}, u32[]{:S(2)}) collective-permute-start(bf16[4,16,256]{2,1,0:T(8,128)(2,1)} %param.11), channel_id=1, source_target_pairs={{2,0},{4,2},{6,4},{8,6},{10,8},{12,10},{14,12},{3,1},{5,3},{7,5},{... | collective-permute-start | bytes 98312 | tf_op jit(solution)/shard_map/ppermute | solution.py:17
  8.0 43.4 %collective-permute-start = (bf16[4,16,256]{2,1,0:T(8,128)(2,1)}, bf16[4,16,256]{2,1,0:T(8,128)(2,1)S(1)}, u32[]{:S(2)}, u32[]{:S(2)}) collective-permute-start(bf16[4,16,256]{2,1,0:T(8,128)(2,1)} %param.11), channel_id=1, source_target_pairs={{0,2},{2,4},{4,6},{6,8},{8,10},{10,12},{12,14},{1,3},{3,5},{5,7},{... | collective-permute-start | bytes 98312 | tf_op jit(solution)/shard_map/ppermute | solution.py:15
  14.6 35.5 %copy-start.4 = (bf16[1,64,256]{2,1,0:T(8,128)(2,1)S(1)}, bf16[1,64,256]{2,1,0:T(8,128)(2,1)}, u32[]{:S(2)}) copy-start(bf16[1,64,256]{2,1,0:T(8,128)(2,1)} %param.15) | copy-start | bytes 98308
  14.6 35.6 %copy-start.9 = (u32[32]{0:T(128)S(1)}, u32[32]{0:T(128)}, u32[]{:S(2)}) copy-start(u32[32]{0:T(128)} %constant.58) | copy-start | bytes 388
  14.6 36.9 %copy-start.3 = (bf16[4,16,256]{2,1,0:T(8,128)(2,1)S(1)}, bf16[4,16,256]{2,1,0:T(8,128)(2,1)}, u32[]{:S(2)}) copy-start(bf16[4,16,256]{2,1,0:T(8,128)(2,1)} %param.11) | copy-start | bytes 98308
  15.9 73.8 %copy-start.1 = (bf16[4,64,256]{2,1,0:T(8,128)(2,1)S(1)}, bf16[4,64,256]{2,1,0:T(8,128)(2,1)}, u32[]{:S(2)}) copy-start(bf16[4,64,256]{2,1,0:T(8,128)(2,1)} %param.13) | copy-start | bytes 393220
Sparse Core Ops, SparseCore 0:
  17.3 71.4 all-reduce.2
where the time goes:
time: 98.1 us; the launch traced here: 97.8 us
  waiting for transfers between devices  36.8 us (38%)
  blocking collectives  31.4 us (32%)
  between operations  14.3 us (15%)
  starting transfers between devices  6.94 us (7%)
  matrix products  4.7 us (5%)
  local copies, waits for them, and re-layouts  3.61 us (4%)
    unnamed x2, waiting for transfers between devices  36.8 us
    all_gather x1, blocking collectives, on_device(): lax.all_gather(node_coef.reshape(1, width), ('leaf', 'vec'), axis=0, tile...  31.4 us
    ppermute x1, starting transfers between devices, padded_2(): lax.ppermute(tail, axis, [(i, (i + 1) % count) for i in range(ends)])  5.48 us
  transfers between devices with their start and end apart: 3, of which 1 were waited for; matrix products, arithmetic and copies ran while one was open for 6% of the time, Pallas kernels for 0%

commit v1 on v0

v1 whole, which is shorter than its diff:
```python
import functools

import jax
import jax.numpy as jnp
from jax import lax
from jax.experimental import pallas as pl
from jax.experimental.pallas import tpu as pltpu
from jax.sharding import PartitionSpec as P

F32 = jnp.float32
BF16 = jnp.bfloat16
NODE_AXES = ("leaf", "vec")
NT = (((1,), (1,)), ((), ()))


def bits_of(count):
    return count.bit_length() - 1


def reversed_bits(value, width):
    return sum(((value >> bit) & 1) << (width - 1 - bit) for bit in range(width))


def lane_half(shape):
    return lax.broadcasted_iota(jnp.int32, shape, 1) // (shape[1] // 2)


def source_kernel(nodes, me_ref, dst_ref, adj_ref, out_ref, up_ref, far_ref, send_ref, keep_ref, sums):
    leaf_dev, vectors, _ = adj_ref.shape
    rank = out_ref.shape[1]
    far_count = dst_ref.shape[1]
    pairs = leaf_dev // 2
    wide = 2 * rank
    me = me_ref[0]
    sums[...] = jnp.zeros_like(sums)
    half = lane_half((vectors, wide))
    coefs = []
    for j in range(leaf_dev):
        coef = lax.dot_general(adj_ref[j], out_ref[j], NT, preferred_element_type=F32).astype(BF16)
        coefs.append(coef)
        contrib = jnp.dot(coef, far_ref[j], preferred_element_type=F32)
        for g in range(far_count // 2):
            straight = contrib[:, g * wide : (g + 1) * wide]
            turned = pltpu.roll(straight, rank, 1)
            for h in range(2):
                target = dst_ref[j, 2 * g + h]
                place = ((target // leaf_dev) ^ me) * pairs + (target % leaf_dev) // 2
                side = target % 2
                value = jnp.where(jnp.full(half.shape, side) == h, straight, turned)
                sums[place] += jnp.where(half == side, value, 0.0)
    side = jnp.concatenate(coefs, axis=1)
    node = lax.dot_general(side, up_ref[0], NT, preferred_element_type=F32).astype(BF16)
    rows = pairs * vectors
    width = bits_of(nodes)
    for r in range(nodes):
        d = reversed_bits(r, width)
        block = sums[d * pairs : (d + 1) * pairs].reshape(rows, wide)
        if r < nodes // 2:
            keep_ref[r * rows : (r + 1) * rows] = block
        else:
            at = (r - nodes // 2) * rows
            send_ref[at : at + rows] = block.astype(BF16)
    send_ref[nodes // 2 * rows :] = jnp.concatenate([node, node], axis=1)


def near_kernel(me_ref, src_ref, adj_ref, a_ref, b_ref, tiles_ref, near_ref, around):
    leaf_dev, _, cells = adj_ref.shape
    near_count = src_ref.shape[1]
    me = me_ref[0]
    around[:leaf_dev] = adj_ref[...]
    around[leaf_dev : 2 * leaf_dev] = a_ref[...]
    around[2 * leaf_dev :] = b_ref[...]
    for j in range(leaf_dev):
        total = None
        for k in range(near_count):
            source = src_ref[j, k]
            node = source // leaf_dev
            base = jnp.where(node == me, 0, jnp.where(node == (me ^ 1), leaf_dev, 2 * leaf_dev))
            block = around[base + source % leaf_dev]
            part = jnp.dot(block, tiles_ref[j, k * cells : (k + 1) * cells], preferred_element_type=F32)
            total = part if total is None else total + part
        near_ref[j] = total


def final_kernel(me_ref, src_ref, keep_ref, got_ref, *refs):
    *coef_refs, top_ref, down_ref, in_ref, near_ref, out_ref, held = refs
    leaf_dev, vectors, cells = near_ref.shape
    rank = in_ref.shape[1]
    wide = 2 * rank
    me = me_ref[0]
    at = 0
    for ref in coef_refs:
        count = ref.shape[0] // vectors
        held[at : at + count] = ref[...].astype(F32).reshape(count, vectors, wide)
        at += count
    half = lane_half((vectors, wide))
    top_count = src_ref.shape[1]
    picked = []
    for q in range(top_count // 2):
        sides = []
        for h in range(2):
            distance = src_ref[0, 2 * q + h] ^ me
            block = held[distance // 2]
            turned = pltpu.roll(block, rank, 1)
            sides.append(jnp.where(jnp.full(half.shape, distance % 2) == h, block, turned))
        picked.append(jnp.where(half == 0, sides[0], sides[1]).astype(BF16))
    picked = jnp.concatenate(picked, axis=1)
    top_in = lax.dot_general(picked, top_ref[0], NT, preferred_element_type=F32).astype(BF16)
    down = jnp.dot(top_in, down_ref[0], preferred_element_type=F32)
    leaf_in = keep_ref[...] + got_ref[...].astype(F32)
    leaf_in = jnp.concatenate([leaf_in[p * vectors : (p + 1) * vectors] for p in range(leaf_dev // 2)], axis=1)
    mixed = (leaf_in + down).astype(BF16)
    for j in range(leaf_dev):
        far = jnp.dot(mixed[:, j * rank : (j + 1) * rank], in_ref[j], preferred_element_type=F32)
        out_ref[j] = near_ref[j] + far


VMEM = pl.BlockSpec(memory_space=pltpu.VMEM)
SMEM = pl.BlockSpec(memory_space=pltpu.SMEM)


def on_device(
    adjoint, leaf_basis_out, leaf_basis_in, transfer_up, transfer_down, far_coupling, top_coupling, near_tiles, near_src, far_dst, top_src
):
    leaf_dev, vectors, cells = adjoint.shape
    rank = leaf_basis_out.shape[1]
    wide = 2 * rank
    pairs = leaf_dev // 2
    rows = pairs * vectors
    nodes = lax.axis_size(NODE_AXES)
    steps = bits_of(nodes)
    me = lax.axis_index(NODE_AXES).astype(jnp.int32).reshape(1)

    def exchange(x, distance):
        return lax.ppermute(x, NODE_AXES, [(i, i ^ distance) for i in range(nodes)])

    send, keep = pl.pallas_call(
        functools.partial(source_kernel, nodes),
        out_shape=(
            jax.ShapeDtypeStruct((nodes // 2 * rows + vectors, wide), BF16),
            jax.ShapeDtypeStruct((nodes // 2 * rows, wide), F32),
        ),
        in_specs=[SMEM, SMEM] + [VMEM] * 4,
        out_specs=(VMEM, VMEM),
        scratch_shapes=[pltpu.VMEM((nodes * pairs, vectors, wide), F32)],
        name="source",
    )(me, far_dst, adjoint, leaf_basis_out, transfer_up, far_coupling)

    other = [pair for i in range(1, nodes - 1, 2) for pair in ((i, i + 1), (i + 1, i))]
    a = exchange(adjoint, 1)
    b = lax.ppermute(adjoint, NODE_AXES, other)

    coefs = [send[nodes // 2 * rows :]]
    for step in range(steps):
        got = exchange(send, 1 << step)
        half = nodes >> (step + 1)
        arrived = got[half * rows :]
        if step == 0:
            left = jnp.arange(wide) < rank
            coefs = [jnp.where(left, coefs[0], arrived)]
        else:
            coefs.append(arrived)
        if step < steps - 1:
            keep = keep + got[: half * rows].astype(F32)
            send = jnp.concatenate([keep[half // 2 * rows :].astype(BF16)] + coefs, axis=0)
            keep = keep[: half // 2 * rows]

    near = pl.pallas_call(
        near_kernel,
        out_shape=jax.ShapeDtypeStruct((leaf_dev, vectors, cells), F32),
        in_specs=[SMEM, SMEM] + [VMEM] * 4,
        out_specs=VMEM,
        scratch_shapes=[pltpu.VMEM((3 * leaf_dev, vectors, cells), BF16)],
        name="near",
    )(me, near_src, adjoint, a, b, near_tiles)

    return pl.pallas_call(
        final_kernel,
        out_shape=jax.ShapeDtypeStruct((leaf_dev, vectors, cells), F32),
        in_specs=[SMEM, SMEM] + [VMEM] * (6 + len(coefs)),
        out_specs=VMEM,
        scratch_shapes=[pltpu.VMEM((nodes // 2, vectors, wide), F32)],
        name="final",
    )(me, top_src, keep, got[:rows], *coefs, top_coupling, transfer_down, leaf_basis_in, near)


def solution(mesh):
    split = P(("design", "leaf", "vec"), None, None)
    in_specs = (P(("design", "leaf", "vec"), "sub", None),) + (split,) * 7 + (P(("design", "leaf", "vec"), None),) * 3
    out_specs = P(("design", "leaf", "vec"), "sub", None)
    return jax.shard_map(on_device, mesh=mesh, in_specs=in_specs, out_specs=out_specs, check_vma=False)
```

time: 98.1 us -> 24.9 us (0.25)
  waiting for transfers between devices: 36.8 us -> 2.15 us
  blocking collectives: 31.4 us -> 0 us
  between operations: 14.3 us -> 0.07 us
  Pallas kernels: 0 us -> 7.05 us
  matrix products: 4.7 us -> 0 us
  starting transfers between devices: 6.94 us -> 11.2 us
  other arithmetic: 0.13 us -> 1.55 us
  local copies, waits for them, and re-layouts: 3.61 us -> 2.44 us
    unnamed x2 -> x0, waiting for transfers between devices: 36.8 us -> none
    all_gather x1 -> x0, blocking collectives: 31.4 us -> none  [on_device(): lax.all_gather(node_coef.reshape(1, width), ('leaf', 'vec'), axis=0, tile...]
    pallas_call x0 -> x3, Pallas kernels: none -> 7.05 us  [the longest x1 2.42 us: on_device(): pl.pallas_call(near_kernel, out_shape=jax.ShapeDtypeStruct((leaf_dev, vec...]
    dot_general x7 -> x0, matrix products: 4.7 us -> none  [the longest x1 1.13 us: on_device(): jnp.einsum('ivr,irm->ivm', leaf_coef, far_coupling, preferred_element_typ...]
    ppermute x2 -> x5, starting transfers between devices: 6.9 us -> 11.2 us  [the longest x4 10.5 us: exchange(): return lax.ppermute(x, NODE_AXES, [(i, i ^ distance) for i in range(nodes)])]
    ppermute x2 -> x5, waiting for transfers between devices: 0.01 us -> 2.15 us  [the longest x4 2.15 us: exchange(): return lax.ppermute(x, NODE_AXES, [(i, i ^ distance) for i in range(nodes)])]
    gather x3 -> x0, local copies, waits for them, and re-layouts: 1.26 us -> none  [the longest x2 0.7 us: on_device(): picked = jnp.take(everyone, top_src[0], axis=0)]
    slice x0 -> x5, local copies, waits for them, and re-layouts: none -> 1.21 us  [the longest x2 0.6 us: on_device(): arrived = got[half * rows:]]
  transfers between devices with their start and end apart: 3 -> 5, of which waited for: 1 -> 1; matrix products, arithmetic and copies ran while one was open for 6% -> 3% of each run, Pallas kernels for 0% -> 10%
where the time goes in v1:
time: 24.9 us; the launch traced here: 24.4 us
  starting transfers between devices  11.2 us (45%)
  Pallas kernels  7.05 us (28%)
  local copies, waits for them, and re-layouts  2.44 us (10%)
  waiting for transfers between devices  2.15 us (9%)
  other arithmetic  1.55 us (6%)
    ppermute x4, starting transfers between devices, exchange(): return lax.ppermute(x, NODE_AXES, [(i, i ^ distance) for i in range(nodes)])  10.5 us
    pallas_call x1, Pallas kernels, on_device(): pl.pallas_call(near_kernel, out_shape=jax.ShapeDtypeStruct((leaf_dev, vec...  2.42 us
    pallas_call x1, Pallas kernels, on_device(): pl.pallas_call(functools.partial(source_kernel, nodes), out_shape=(jax.Sh...  2.35 us
    pallas_call x1, Pallas kernels, on_device(): pl.pallas_call(final_kernel, out_shape=jax.ShapeDtypeStruct((leaf_dev, ve...  2.27 us
    ppermute x4, waiting for transfers between devices, exchange(): return lax.ppermute(x, NODE_AXES, [(i, i ^ distance) for i in range(nodes)])  2.15 us
    unnamed x8, local copies, waits for them, and re-layouts  1.23 us
    add x2, other arithmetic, on_device(): keep = keep + got[:half * rows].astype(F32)  0.86 us
    select_n x1, other arithmetic, on_device(): coefs = [jnp.where(left, coefs[0], arrived)]  0.68 us
  transfers between devices with their start and end apart: 5, of which 1 were waited for; matrix products, arithmetic and copies ran while one was open for 3% of the time, Pallas kernels for 10%

profile of v1, /device:TPU:0, one launch (start us, length us, event | category | flops | bytes accessed | tf_op | source)
XLA Modules:
  0.0 24.4 jit_solution(16776722185224628881)
XLA Ops:
  0.0 2.4 %source.1 = (bf16[144,128]{1,0:T(8,128)(2,1)}, f32[128,128]{1,0:T(8,128)}) custom-call(s32[1]{0:T(128)} %bitcast.me_ref, s32[4,8]{1,0:T(4,128)} %dst_ref.1, bf16[4,16,256]{2,1,0:T(8,128)(2,1)} %adj_ref.3, bf16[4,64,256]{2,1,0:T(8,128)(2,1)} %out_ref.1, bf16[1,64,256]{2,1,0:T(8,128)(2,1)} %up_ref.1, bf16[4,64,512]{2,1,0:T(8,128)(2,1)} %far_ref.1), custom_call_target="tpu_custom_call" | custom-call | tf_op jit(solution)/shard_map/source/pallas_call | solution.py:137
  2.4 2.9 %collective-permute-start = (bf16[144,128]{1,0:T(8,128)(2,1)}, bf16[144,128]{1,0:T(8,128)(2,1)S(1)}, u32[]{:S(2)}, u32[]{:S(2)}) collective-permute-start(bf16[144,128]{1,0:T(8,128)(2,1)} %get-tuple-element.8), channel_id=1, source_target_pairs={{0,2},{2,0},{4,6},{6,4},{8,10},{10,8},{12,14},{14,12},{1,3},{3,1},... | collective-permute-start | bytes 110600 | tf_op jit(solution)/shard_map/ppermute | solution.py:135
  5.3 2.1 %collective-permute-done = bf16[144,128]{1,0:T(8,128)(2,1)S(1)} collective-permute-done((bf16[144,128]{1,0:T(8,128)(2,1)}, bf16[144,128]{1,0:T(8,128)(2,1)S(1)}, u32[]{:S(2)}, u32[]{:S(2)}) %collective-permute-start) | collective-permute-done | bytes 36896 | tf_op jit(solution)/shard_map/ppermute | solution.py:135
  7.4 0.8 %convert_add_fusion = f32[128,128]{1,0:T(8,128)S(1)} fusion(f32[128,128]{1,0:T(8,128)} %get-tuple-element.7, bf16[144,128]{1,0:T(8,128)(2,1)S(1)} %collective-permute-done), kind=kLoop, calls=%fused_computation | loop fusion | flops 32768 | bytes 163840 | tf_op jit(solution)/shard_map/add | solution.py:164
  8.3 0.7 %slice_select_fusion.refs_0_ = bf16[16,128]{1,0:T(8,128)(2,1)S(1)} fusion(bf16[144,128]{1,0:T(8,128)(2,1)S(1)} %collective-permute-done, bf16[144,128]{1,0:T(8,128)(2,1)} %get-tuple-element.8, pred[128]{0:T(512)(128)(4,1)S(1)} %iota_compare_fusion), kind=kLoop, calls=%fused_computation.6 | loop fusion | flops 2048 | bytes 12416 | tf_op jit(solution)/shard_map/jit(_where)/select_n | solution.py:160
  9.0 0.0 copy-start
  9.0 2.2 %collective-permute-start.1 = (bf16[80,128]{1,0:T(8,128)(2,1)S(1)}, bf16[80,128]{1,0:T(8,128)(2,1)S(1)}, u32[]{:S(2)}, u32[]{:S(2)}) collective-permute-start(bf16[80,128]{1,0:T(8,128)(2,1)S(1)} %pad_maximum_fusion), channel_id=1, source_target_pairs={{0,4},{2,6},{4,0},{6,2},{8,12},{10,14},{12,8},{14,10},{1,5},{3,7},... | collective-permute-start | bytes 61448 | tf_op jit(solution)/shard_map/ppermute | solution.py:135
  11.2 1.5 %collective-permute-start.3 = (bf16[4,16,256]{2,1,0:T(8,128)(2,1)}, bf16[4,16,256]{2,1,0:T(8,128)(2,1)S(1)}, u32[]{:S(2)}, u32[]{:S(2)}) collective-permute-start(bf16[4,16,256]{2,1,0:T(8,128)(2,1)} %adj_ref.3), channel_id=1, source_target_pairs={{0,2},{2,0},{4,6},{6,4},{8,10},{10,8},{12,14},{14,12},{1,3},{3,1},... | collective-permute-start | bytes 98312 | tf_op jit(solution)/shard_map/ppermute | solution.py:135
  12.6 0.7 %collective-permute-start.4 = (bf16[4,16,256]{2,1,0:T(8,128)(2,1)}, bf16[4,16,256]{2,1,0:T(8,128)(2,1)S(1)}, u32[]{:S(2)}, u32[]{:S(2)}) collective-permute-start(bf16[4,16,256]{2,1,0:T(8,128)(2,1)} %adj_ref.3), channel_id=1, source_target_pairs={{2,4},{4,2},{6,8},{8,6},{10,12},{12,10},{3,5},{5,3},{7,9},{9,7},{1... | collective-permute-start | bytes 98312 | tf_op jit(solution)/shard_map/ppermute | solution.py:151
  13.3 0.0 collective-permute-done.1
  13.4 0.0 copy-start.1
  13.4 3.9 %collective-permute-start.2 = (bf16[64,128]{1,0:T(8,128)(2,1)S(1)}, bf16[64,128]{1,0:T(8,128)(2,1)S(1)}, u32[]{:S(2)}, u32[]{:S(2)}) collective-permute-start(bf16[64,128]{1,0:T(8,128)(2,1)S(1)} %pad_maximum_fusion.1), channel_id=1, source_target_pairs={{0,8},{2,10},{4,12},{6,14},{8,0},{10,2},{12,4},{14,6},{1,9},{3,11}... | collective-permute-start | bytes 49160 | tf_op jit(solution)/shard_map/ppermute | solution.py:135
  17.3 0.0 collective-permute-done.3.a_ref
  17.3 0.0 copy-start.2
  17.3 0.0 collective-permute-done.4.b_ref
  17.3 0.6 %copy-done.2 = bf16[4,16,256]{2,1,0:T(8,128)(2,1)} copy-done((bf16[4,16,256]{2,1,0:T(8,128)(2,1)}, bf16[4,16,256]{2,1,0:T(8,128)(2,1)S(1)}, u32[]{:S(2)}) %copy-start.2) | copy-done | bytes 32792
  17.9 0.0 copy-start.3
  17.9 0.6 %copy-done.3 = bf16[4,16,256]{2,1,0:T(8,128)(2,1)} copy-done((bf16[4,16,256]{2,1,0:T(8,128)(2,1)}, bf16[4,16,256]{2,1,0:T(8,128)(2,1)S(1)}, u32[]{:S(2)}) %copy-start.3) | copy-done | bytes 32792
  18.5 2.4 %near.1.refs_6_ = f32[4,16,256]{2,1,0:T(8,128)} custom-call(s32[1]{0:T(128)} %bitcast.me_ref, s32[4,3]{1,0:T(4,128)} %src_ref.2, bf16[4,16,256]{2,1,0:T(8,128)(2,1)} %adj_ref.3, bf16[4,16,256]{2,1,0:T(8,128)(2,1)} %copy-done.2, bf16[4,16,256]{2,1,0:T(8,128)(2,1)} %copy-done.3, bf16[4,768,256]{2,1,0:T(8,128)(2,1)} %tiles_ref.1), custom_call_target="tpu_custom_call" | custom-call | tf_op jit(solution)/shard_map/near/pallas_call | solution.py:168
  20.9 0.6 %slice.51.keep_ref = f32[32,128]{1,0:T(8,128)} slice(f32[64,128]{1,0:T(8,128)S(1)} %slice_add_fusion), slice={[0:32], [0:128]} | slice | bytes 32768 | tf_op jit(solution)/shard_map/slice | solution.py:166
  21.5 0.0 collective-permute-done.2
  21.5 0.6 %fusion = (bf16[32,128]{1,0:T(8,128)(2,1)}, bf16[32,128]{1,0:T(8,128)(2,1)}) fusion(bf16[64,128]{1,0:T(8,128)(2,1)S(1)} %collective-permute-done.2), kind=kLoop, calls=%fused_computation.8 | loop fusion | bytes 32768 | tf_op jit(solution)/shard_map/slice | solution.py:157
  22.2 0.0 copy-done
  22.2 0.0 copy-done.1
  22.2 2.3 %final.1 = f32[4,16,256]{2,1,0:T(8,128)} custom-call(s32[1]{0:T(128)} %bitcast.me_ref, s32[1,16]{1,0:T(1,128)} %src_ref.3, f32[32,128]{1,0:T(8,128)} %slice.51.keep_ref, bf16[32,128]{1,0:T(8,128)(2,1)} %get-tuple-element.10.got_ref, bf16[16,128]{1,0:T(8,128)(2,1)} %copy-done, bf16[16,128]{1,0:T(8,128)(2,1)} %copy-done.1, ...), custom_call_target="tpu_custom_call" | custom-call | tf_op jit(solution)/shard_map/final/pallas_call | solution.py:177
  (7 shorter events, 0.0 us)
Async XLA Ops:
  2.4 5.1 %collective-permute-start = (bf16[144,128]{1,0:T(8,128)(2,1)}, bf16[144,128]{1,0:T(8,128)(2,1)S(1)}, u32[]{:S(2)}, u32[]{:S(2)}) collective-permute-start(bf16[144,128]{1,0:T(8,128)(2,1)} %get-tuple-element.8), channel_id=1, source_target_pairs={{0,2},{2,0},{4,6},{6,4},{8,10},{10,8},{12,14},{14,12},{1,3},{3,1},... | collective-permute-start | bytes 110600 | tf_op jit(solution)/shard_map/ppermute | solution.py:135
  9.0 13.2 %copy-start = (bf16[16,128]{1,0:T(8,128)(2,1)}, bf16[16,128]{1,0:T(8,128)(2,1)S(1)}, u32[]{:S(2)}) copy-start(bf16[16,128]{1,0:T(8,128)(2,1)S(1)} %slice_select_fusion.refs_0_) | copy-start | bytes 12292
  9.0 4.3 %collective-permute-start.1 = (bf16[80,128]{1,0:T(8,128)(2,1)S(1)}, bf16[80,128]{1,0:T(8,128)(2,1)S(1)}, u32[]{:S(2)}, u32[]{:S(2)}) collective-permute-start(bf16[80,128]{1,0:T(8,128)(2,1)S(1)} %pad_maximum_fusion), channel_id=1, source_target_pairs={{0,4},{2,6},{4,0},{6,2},{8,12},{10,14},{12,8},{14,10},{1,5},{3,7},... | collective-permute-start | bytes 61448 | tf_op jit(solution)/shard_map/ppermute | solution.py:135
  11.2 6.1 %collective-permute-start.3 = (bf16[4,16,256]{2,1,0:T(8,128)(2,1)}, bf16[4,16,256]{2,1,0:T(8,128)(2,1)S(1)}, u32[]{:S(2)}, u32[]{:S(2)}) collective-permute-start(bf16[4,16,256]{2,1,0:T(8,128)(2,1)} %adj_ref.3), channel_id=1, source_target_pairs={{0,2},{2,0},{4,6},{6,4},{8,10},{10,8},{12,14},{14,12},{1,3},{3,1},... | collective-permute-start | bytes 98312 | tf_op jit(solution)/shard_map/ppermute | solution.py:135
  12.6 4.7 %collective-permute-start.4 = (bf16[4,16,256]{2,1,0:T(8,128)(2,1)}, bf16[4,16,256]{2,1,0:T(8,128)(2,1)S(1)}, u32[]{:S(2)}, u32[]{:S(2)}) collective-permute-start(bf16[4,16,256]{2,1,0:T(8,128)(2,1)} %adj_ref.3), channel_id=1, source_target_pairs={{2,4},{4,2},{6,8},{8,6},{10,12},{12,10},{3,5},{5,3},{7,9},{9,7},{1... | collective-permute-start | bytes 98312 | tf_op jit(solution)/shard_map/ppermute | solution.py:151
  13.4 8.8 %copy-start.1 = (bf16[16,128]{1,0:T(8,128)(2,1)}, bf16[16,128]{1,0:T(8,128)(2,1)S(1)}, u32[]{:S(2)}) copy-start(bf16[16,128]{1,0:T(8,128)(2,1)S(1)} %slice.53.refs_1_) | copy-start | bytes 12292
  13.4 8.2 %collective-permute-start.2 = (bf16[64,128]{1,0:T(8,128)(2,1)S(1)}, bf16[64,128]{1,0:T(8,128)(2,1)S(1)}, u32[]{:S(2)}, u32[]{:S(2)}) collective-permute-start(bf16[64,128]{1,0:T(8,128)(2,1)S(1)} %pad_maximum_fusion.1), channel_id=1, source_target_pairs={{0,8},{2,10},{4,12},{6,14},{8,0},{10,2},{12,4},{14,6},{1,9},{3,11}... | collective-permute-start | bytes 49160 | tf_op jit(solution)/shard_map/ppermute | solution.py:135
  17.3 0.6 %copy-start.2 = (bf16[4,16,256]{2,1,0:T(8,128)(2,1)}, bf16[4,16,256]{2,1,0:T(8,128)(2,1)S(1)}, u32[]{:S(2)}) copy-start(bf16[4,16,256]{2,1,0:T(8,128)(2,1)S(1)} %collective-permute-done.3.a_ref) | copy-start | bytes 98308
  17.9 0.6 %copy-start.3 = (bf16[4,16,256]{2,1,0:T(8,128)(2,1)}, bf16[4,16,256]{2,1,0:T(8,128)(2,1)S(1)}, u32[]{:S(2)}) copy-start(bf16[4,16,256]{2,1,0:T(8,128)(2,1)S(1)} %collective-permute-done.4.b_ref) | copy-start | bytes 98308

commit v2 on v1

v2 whole, which is shorter than its diff:
```python
import functools

import jax
import jax.numpy as jnp
from jax import lax
from jax.experimental import pallas as pl
from jax.experimental.pallas import tpu as pltpu
from jax.sharding import PartitionSpec as P

F32 = jnp.float32
BF16 = jnp.bfloat16
NODE_AXES = ("leaf", "vec")
NT = (((1,), (1,)), ((), ()))
TN = (((0,), (0,)), ((), ()))
VMEM = pl.BlockSpec(memory_space=pltpu.VMEM)
HBM = pl.BlockSpec(memory_space=pltpu.HBM)
PARAMS = pltpu.CompilerParams(vmem_limit_bytes=24 << 20)


def bits_of(count):
    return count.bit_length() - 1


def reversed_bits(value, width):
    return sum(((value >> bit) & 1) << (width - 1 - bit) for bit in range(width))


def lane_half(shape):
    return lax.broadcasted_iota(jnp.int32, shape, 1) // (shape[1] // 2)


def in_hbm(x):
    return pltpu.with_memory_space_constraint(x, pltpu.HBM)


def side_by_side(stacked, rows):
    return jnp.concatenate([stacked[at : at + rows] for at in range(0, stacked.shape[0], rows)], axis=1)


def source_kernel(nodes, *refs):
    inputs, rest = refs[:9], refs[9:]
    dst_hbm, adj_hbm, out_hbm, up_hbm, far_hbm = inputs[:5]
    send_ref, keep_ref, adj_ref = rest[:3]
    later = rest[3:7]
    dst_ref, out_ref, up_ref, far_ref, sums, sems = rest[7:]
    pairs_of_refs = [(dst_hbm, dst_ref), (adj_hbm, adj_ref), (out_hbm, out_ref), (far_hbm, far_ref), (up_hbm, up_ref)]
    pairs_of_refs += list(zip(inputs[5:], later))
    copies = [pltpu.make_async_copy(a, b, sems.at[i]) for i, (a, b) in enumerate(pairs_of_refs)]
    for copy in copies:
        copy.start()
    leaf_dev, vectors, _ = adj_ref.shape
    rank = out_ref.shape[1]
    far_count = dst_ref.shape[1]
    pairs = leaf_dev // 2
    wide = 2 * rank
    me = lax.axis_index(NODE_AXES)
    sums[...] = jnp.zeros_like(sums)
    half = lane_half((vectors, wide))
    for copy in copies[:4]:
        copy.wait()
    coefs = []
    for j in range(leaf_dev):
        coef = lax.dot_general(adj_ref[j], out_ref[j], NT, preferred_element_type=F32).astype(BF16)
        coefs.append(coef)
        contrib = jnp.dot(coef, far_ref[j], preferred_element_type=F32)
        for g in range(far_count // 2):
            straight = contrib[:, g * wide : (g + 1) * wide]
            turned = pltpu.roll(straight, rank, 1)
            for h in range(2):
                target = dst_ref[j, 2 * g + h]
                place = ((target // leaf_dev) ^ me) * pairs + (target % leaf_dev) // 2
                side = target % 2
                value = jnp.where(jnp.full(half.shape, side) == h, straight, turned)
                sums[place] += jnp.where(half == side, value, 0.0)
    copies[4].wait()
    side = jnp.concatenate(coefs, axis=1)
    node = lax.dot_general(side, up_ref[0], NT, preferred_element_type=F32).astype(BF16)
    rows = pairs * vectors
    width = bits_of(nodes)
    for r in range(nodes):
        d = reversed_bits(r, width)
        block = sums[d * pairs : (d + 1) * pairs].reshape(rows, wide)
        if r < nodes // 2:
            keep_ref[r * rows : (r + 1) * rows] = block
        else:
            at = (r - nodes // 2) * rows
            send_ref[at : at + rows] = block.astype(BF16)
    send_ref[nodes // 2 * rows :] = jnp.concatenate([node, node], axis=1)
    for copy in copies[5:]:
        copy.wait()


def near_kernel(nodes, near_hbm, top_hbm, adj_ref, a_ref, b_ref, tiles_ref, top_ref, down_ref, keep_ref, *refs):
    *coef_refs, near_ref, base_ref, rest_ref, near_src, top_src, around, by_node, sems = refs
    copies = [pltpu.make_async_copy(top_hbm, top_src, sems.at[0]), pltpu.make_async_copy(near_hbm, near_src, sems.at[1])]
    for copy in copies:
        copy.start()
    leaf_dev, vectors, cells = adj_ref.shape
    near_count = near_src.shape[1]
    top_count = top_src.shape[1]
    rank = down_ref.shape[1]
    me = lax.axis_index(NODE_AXES)
    around[:leaf_dev] = adj_ref[...]
    around[leaf_dev : 2 * leaf_dev] = a_ref[...]
    around[2 * leaf_dev :] = b_ref[...]
    by_node[...] = jnp.zeros_like(by_node)
    through = lax.dot_general(top_ref[0], down_ref[0], TN, preferred_element_type=F32)
    copies[0].wait()
    for k in range(top_count):
        by_node[top_src[0, k] ^ me] += through[k * rank : (k + 1) * rank]
    copies[1].wait()
    for j in range(leaf_dev):
        total = None
        for k in range(near_count):
            source = near_src[j, k]
            node = source // leaf_dev
            base = jnp.where(node == me, 0, jnp.where(node == (me ^ 1), leaf_dev, 2 * leaf_dev))
            block = around[base + source % leaf_dev]
            part = jnp.dot(block, tiles_ref[j, k * cells : (k + 1) * cells], preferred_element_type=F32)
            total = part if total is None else total + part
        near_ref[j] = total
    known = nodes // 2
    at = 0
    base = side_by_side(keep_ref[...], vectors)
    for ref in coef_refs:
        count = 2 * ref.shape[0] // vectors
        matrix = by_node[at : at + count].reshape(count * rank, leaf_dev * rank).astype(BF16)
        base = base + jnp.dot(side_by_side(ref[...], vectors), matrix, preferred_element_type=F32)
        at += count
    base_ref[...] = base
    rest_ref[...] = by_node[known:].reshape(known * rank, leaf_dev * rank).astype(BF16)


def final_kernel(got_ref, base_ref, rest_ref, in_ref, near_ref, out_ref):
    leaf_dev, vectors, _ = near_ref.shape
    rank = in_ref.shape[1]
    rows = leaf_dev // 2 * vectors
    got = got_ref[...]
    down = jnp.dot(side_by_side(got[rows:], vectors), rest_ref[...], preferred_element_type=F32)
    mixed = (base_ref[...] + side_by_side(got[:rows].astype(F32), vectors) + down).astype(BF16)
    for j in range(leaf_dev):
        far = jnp.dot(mixed[:, j * rank : (j + 1) * rank], in_ref[j], preferred_element_type=F32)
        out_ref[j] = near_ref[j] + far


def on_device(
    adjoint, leaf_basis_out, leaf_basis_in, transfer_up, transfer_down, far_coupling, top_coupling, near_tiles, near_src, far_dst, top_src
):
    leaf_dev, vectors, cells = adjoint.shape
    rank = leaf_basis_out.shape[1]
    wide = 2 * rank
    pairs = leaf_dev // 2
    rows = pairs * vectors
    nodes = lax.axis_size(NODE_AXES)
    steps = bits_of(nodes)

    def exchange(x, distance):
        return lax.ppermute(x, NODE_AXES, [(i, i ^ distance) for i in range(nodes)])

    def like(x):
        return jax.ShapeDtypeStruct(x.shape, x.dtype)

    later = (near_tiles, top_coupling, transfer_down, leaf_basis_in)
    send, keep, adjoint_v, tiles, top, down, basis_in = pl.pallas_call(
        functools.partial(source_kernel, nodes),
        out_shape=(
            jax.ShapeDtypeStruct((nodes // 2 * rows + vectors, wide), BF16),
            jax.ShapeDtypeStruct((nodes // 2 * rows, wide), F32),
            like(adjoint),
            *map(like, later),
        ),
        in_specs=[HBM] * 9,
        out_specs=(VMEM,) * 7,
        scratch_shapes=[
            pltpu.SMEM(far_dst.shape, jnp.int32),
            pltpu.VMEM(leaf_basis_out.shape, BF16),
            pltpu.VMEM(transfer_up.shape, BF16),
            pltpu.VMEM(far_coupling.shape, BF16),
            pltpu.VMEM((nodes * pairs, vectors, wide), F32),
            pltpu.SemaphoreType.DMA((9,)),
        ],
        compiler_params=PARAMS,
        name="source",
    )(*map(in_hbm, (far_dst, adjoint, leaf_basis_out, transfer_up, far_coupling, *later)))

    other = [(i, (i + (1 if i % 2 else -1)) % nodes) for i in range(nodes)]
    a = exchange(adjoint_v, 1)
    b = lax.ppermute(adjoint_v, NODE_AXES, other)

    coefs = [send[nodes // 2 * rows :]]
    for step in range(steps):
        got = exchange(send, 1 << step)
        half = nodes >> (step + 1)
        if step < steps - 1:
            arrived = got[half * rows :]
            if step == 0:
                left = jnp.arange(wide) < rank
                coefs = [jnp.where(left, coefs[0], arrived)]
            else:
                coefs.append(arrived)
            keep = keep + got[: half * rows].astype(F32)
            send = jnp.concatenate([keep[half // 2 * rows :].astype(BF16)] + coefs, axis=0)
            keep = keep[: half // 2 * rows]

    near, base, rest = pl.pallas_call(
        functools.partial(near_kernel, nodes),
        out_shape=(
            jax.ShapeDtypeStruct((leaf_dev, vectors, cells), F32),
            jax.ShapeDtypeStruct((vectors, leaf_dev * rank), F32),
            jax.ShapeDtypeStruct((nodes // 2 * rank, leaf_dev * rank), BF16),
        ),
        in_specs=[HBM] * 2 + [VMEM] * (7 + len(coefs)),
        out_specs=(VMEM,) * 3,
        scratch_shapes=[
            pltpu.SMEM(near_src.shape, jnp.int32),
            pltpu.SMEM(top_src.shape, jnp.int32),
            pltpu.VMEM((3 * leaf_dev, vectors, cells), BF16),
            pltpu.VMEM((nodes, rank, leaf_dev * rank), F32),
            pltpu.SemaphoreType.DMA((2,)),
        ],
        compiler_params=PARAMS,
        name="near",
    )(in_hbm(near_src), in_hbm(top_src), adjoint_v, a, b, tiles, top, down, keep, *coefs)

    return pl.pallas_call(
        final_kernel,
        out_shape=jax.ShapeDtypeStruct((leaf_dev, vectors, cells), F32),
        in_specs=[VMEM] * 5,
        out_specs=VMEM,
        compiler_params=PARAMS,
        name="final",
    )(got, base, rest, basis_in, near)


def solution(mesh):
    split = P(("design", "leaf", "vec"), None, None)
    in_specs = (P(("design", "leaf", "vec"), "sub", None),) + (split,) * 7 + (P(("design", "leaf", "vec"), None),) * 3
    out_specs = P(("design", "leaf", "vec"), "sub", None)
    return jax.shard_map(on_device, mesh=mesh, in_specs=in_specs, out_specs=out_specs, check_vma=False)
```

time: 24.9 us -> 19 us (0.76); the launches traced: 24.4 us -> 18.8 us
  Pallas kernels: 7.05 us -> 4.29 us
  local copies, waits for them, and re-layouts: 2.44 us -> 0.02 us
  waiting for transfers between devices: 2.15 us -> 4.14 us
  other arithmetic: 1.55 us -> 0.04 us
  starting transfers between devices: 11.2 us -> 10.2 us
    ppermute x4, starting transfers between devices: 10.5 us -> 6.84 us  [exchange(): return lax.ppermute(x, NODE_AXES, [(i, i ^ distance) for i in range(nodes)])]
    ppermute x1, starting transfers between devices: 0.65 us -> 3.4 us  [on_device(): b = lax.ppermute(adjoint_v, NODE_AXES, other)]
    ppermute x1, waiting for transfers between devices: 0.01 us -> 1.52 us  [on_device(): b = lax.ppermute(adjoint_v, NODE_AXES, other)]
    pallas_call x1, Pallas kernels: 2.27 us -> 0.98 us  [on_device(): pl.pallas_call(final_kernel, out_shape=jax.ShapeDtypeStruct((leaf_dev, ve...]
    unnamed x8 -> x0, local copies, waits for them, and re-layouts: 1.23 us -> none
    pallas_call x1, Pallas kernels: 2.42 us -> 1.3 us  [on_device(): pl.pallas_call(functools.partial(near_kernel, nodes), out_shape=(jax.Shap...]
    add x2, other arithmetic: 0.86 us -> 0.02 us  [on_device(): keep = keep + got[:half * rows].astype(F32)]
    select_n x1, other arithmetic: 0.68 us -> 0.01 us  [on_device(): coefs = [jnp.where(left, coefs[0], arrived)]]
  transfers between devices with their start and end apart: 5 -> 5, of which waited for: 1 -> 3; matrix products, arithmetic and copies ran while one was open for 3% -> 0% of each run, Pallas kernels for 10% -> 7%
where the time goes in v2:
time: 19 us; the launch traced here: 18.8 us
  starting transfers between devices  10.2 us (54%)
  Pallas kernels  4.29 us (23%)
  waiting for transfers between devices  4.14 us (22%)
    ppermute x4, starting transfers between devices, exchange(): return lax.ppermute(x, NODE_AXES, [(i, i ^ distance) for i in range(nodes)])  6.84 us
    ppermute x1, starting transfers between devices, on_device(): b = lax.ppermute(adjoint_v, NODE_AXES, other)  3.4 us
    ppermute x4, waiting for transfers between devices, exchange(): return lax.ppermute(x, NODE_AXES, [(i, i ^ distance) for i in range(nodes)])  2.62 us
    pallas_call x1, Pallas kernels, on_device(): pl.pallas_call(functools.partial(source_kernel, nodes), out_shape=(jax.Sh...  2.01 us
    ppermute x1, waiting for transfers between devices, on_device(): b = lax.ppermute(adjoint_v, NODE_AXES, other)  1.52 us
    pallas_call x1, Pallas kernels, on_device(): pl.pallas_call(functools.partial(near_kernel, nodes), out_shape=(jax.Shap...  1.3 us
    pallas_call x1, Pallas kernels, on_device(): pl.pallas_call(final_kernel, out_shape=jax.ShapeDtypeStruct((leaf_dev, ve...  0.98 us
  transfers between devices with their start and end apart: 5, of which 3 were waited for; matrix products, arithmetic and copies ran while one was open for 0% of the time, Pallas kernels for 7%

profile of v2, /device:TPU:0, one launch (start us, length us, event | category | flops | bytes accessed | tf_op | source)
XLA Modules:
  0.0 18.8 jit_solution(4185183449831661100)
XLA Ops:
  0.0 2.0 %source.1 = (bf16[144,128]{1,0:T(8,128)(2,1)S(1)}, f32[128,128]{1,0:T(8,128)S(1)}, bf16[4,16,256]{2,1,0:T(8,128)(2,1)S(1)}, bf16[4,768,256]{2,1,0:T(8,128)(2,1)S...) custom-call(s32[4,8]{1,0:T(4,128)} %refs_0_.1, ...), custom_call_target="tpu_custom_call" | custom-call | tf_op jit(solution)/shard_map/source/pallas_call | solution.py:164
  2.0 3.0 %collective-permute-start = (bf16[144,128]{1,0:T(8,128)(2,1)S(1)}, bf16[144,128]{1,0:T(8,128)(2,1)S(1)}, u32[]{:S(2)}, u32[]{:S(2)}) collective-permute-start(bf16[144,128]{1,0:T(8,128)(2,1)S(1)} %get-tuple-element.16), channel_id=1, source_target_pairs={{0,2},{2,0},{4,6},{6,4},{8,10},{10,8},{12,14},{14,12},{1,3},{3,1},... | collective-permute-start | bytes 110600 | tf_op jit(solution)/shard_map/ppermute | solution.py:158
  5.0 1.9 %collective-permute-done = bf16[144,128]{1,0:T(8,128)(2,1)S(1)} collective-permute-done((bf16[144,128]{1,0:T(8,128)(2,1)S(1)}, bf16[144,128]{1,0:T(8,128)(2,1)S(1)}, u32[]{:S(2)}, u32[]{:S(2)}) %collective-permute-start) | collective-permute-done | bytes 36896 | tf_op jit(solution)/shard_map/ppermute | solution.py:158
  7.0 2.2 %collective-permute-start.1 = (bf16[80,128]{1,0:T(8,128)(2,1)S(1)}, bf16[80,128]{1,0:T(8,128)(2,1)S(1)}, u32[]{:S(2)}, u32[]{:S(2)}) collective-permute-start(bf16[80,128]{1,0:T(8,128)(2,1)S(1)} %pad_maximum_fusion), channel_id=1, source_target_pairs={{0,4},{2,6},{4,0},{6,2},{8,12},{10,14},{12,8},{14,10},{1,5},{3,7},... | collective-permute-start | bytes 61448 | tf_op jit(solution)/shard_map/ppermute | solution.py:158
  9.2 3.4 %collective-permute-start.4 = (bf16[4,16,256]{2,1,0:T(8,128)(2,1)S(1)}, bf16[4,16,256]{2,1,0:T(8,128)(2,1)S(1)}, u32[]{:S(2)}, u32[]{:S(2)}) collective-permute-start(bf16[4,16,256]{2,1,0:T(8,128)(2,1)S(1)} %get-tuple-element.17.adj_ref), channel_id=1, source_target_pairs={{0,14},{2,4},{4,2},{6,8},{8,6},{10,12},{12,10},{14,0},{1,15},{3,5}... | collective-permute-start | bytes 98312 | tf_op jit(solution)/shard_map/ppermute | solution.py:188
  12.6 0.0 collective-permute-start.3
  12.6 0.0 collective-permute-done.1
  12.6 1.7 %collective-permute-start.2 = (bf16[64,128]{1,0:T(8,128)(2,1)S(1)}, bf16[64,128]{1,0:T(8,128)(2,1)S(1)}, u32[]{:S(2)}, u32[]{:S(2)}) collective-permute-start(bf16[64,128]{1,0:T(8,128)(2,1)S(1)} %pad_maximum_fusion.1), channel_id=1, source_target_pairs={{0,8},{2,10},{4,12},{6,14},{8,0},{10,2},{12,4},{14,6},{1,9},{3,11}... | collective-permute-start | bytes 49160 | tf_op jit(solution)/shard_map/ppermute | solution.py:158
  14.3 1.5 %collective-permute-done.4.b_ref = bf16[4,16,256]{2,1,0:T(8,128)(2,1)S(1)} collective-permute-done((bf16[4,16,256]{2,1,0:T(8,128)(2,1)S(1)}, bf16[4,16,256]{2,1,0:T(8,128)(2,1)S(1)}, u32[]{:S(2)}, u32[]{:S(2)}) %collective-permute-start.4) | collective-permute-done | bytes 32800 | tf_op jit(solution)/shard_map/ppermute | solution.py:188
  15.8 0.7 %collective-permute-done.3.a_ref = bf16[4,16,256]{2,1,0:T(8,128)(2,1)S(1)} collective-permute-done((bf16[4,16,256]{2,1,0:T(8,128)(2,1)S(1)}, bf16[4,16,256]{2,1,0:T(8,128)(2,1)S(1)}, u32[]{:S(2)}, u32[]{:S(2)}) %collective-permute-start.3) | collective-permute-done | bytes 32800 | tf_op jit(solution)/shard_map/ppermute | solution.py:158
  16.5 1.3 %near.1 = (f32[4,16,256]{2,1,0:T(8,128)S(1)}, f32[16,256]{1,0:T(8,128)S(1)}, bf16[256,256]{1,0:T(8,128)(2,1)S(1)}) custom-call(s32[4,3]{1,0:T(4,128)} %near_hbm.1, s32[1,16]{1,0:T(1,128)} %top_hbm.1, bf16[4,16,256]{2,1,0:T(8,128)(2,1)S(1)} %get-tuple-element.17.adj_ref, bf16[4,16,256]{2,1,0:T(8,128)(2,1)S(1)} %collective-permute-done.3.a_ref, ...), custom_call_target="tpu_custom_call" | custom-call | tf_op jit(solution)/shard_map/near/pallas_call | solution.py:205
  17.8 0.0 collective-permute-done.2.got_ref
  17.8 1.0 %final.1 = f32[4,16,256]{2,1,0:T(8,128)} custom-call(bf16[64,128]{1,0:T(8,128)(2,1)S(1)} %collective-permute-done.2.got_ref, f32[16,256]{1,0:T(8,128)S(1)} %get-tuple-element.21.base_ref, bf16[256,256]{1,0:T(8,128)(2,1)S(1)} %get-tuple-element.22.rest_ref, bf16[4,64,256]{2,1,0:T(8,128)(2,1)S(1)} %get-tuple-element.23.in_ref, ...), custom_call_target="tpu_custom_call" | custom-call | tf_op jit(solution)/shard_map/final/pallas_call | solution.py:225
  (10 shorter events, 0.1 us)
Async XLA Ops:
  2.0 4.9 %collective-permute-start = (bf16[144,128]{1,0:T(8,128)(2,1)S(1)}, bf16[144,128]{1,0:T(8,128)(2,1)S(1)}, u32[]{:S(2)}, u32[]{:S(2)}) collective-permute-start(bf16[144,128]{1,0:T(8,128)(2,1)S(1)} %get-tuple-element.16), channel_id=1, source_target_pairs={{0,2},{2,0},{4,6},{6,4},{8,10},{10,8},{12,14},{14,12},{1,3},{3,1},... | collective-permute-start | bytes 110600 | tf_op jit(solution)/shard_map/ppermute | solution.py:158
  7.0 5.6 %collective-permute-start.1 = (bf16[80,128]{1,0:T(8,128)(2,1)S(1)}, bf16[80,128]{1,0:T(8,128)(2,1)S(1)}, u32[]{:S(2)}, u32[]{:S(2)}) collective-permute-start(bf16[80,128]{1,0:T(8,128)(2,1)S(1)} %pad_maximum_fusion), channel_id=1, source_target_pairs={{0,4},{2,6},{4,0},{6,2},{8,12},{10,14},{12,8},{14,10},{1,5},{3,7},... | collective-permute-start | bytes 61448 | tf_op jit(solution)/shard_map/ppermute | solution.py:158
  9.2 6.6 %collective-permute-start.4 = (bf16[4,16,256]{2,1,0:T(8,128)(2,1)S(1)}, bf16[4,16,256]{2,1,0:T(8,128)(2,1)S(1)}, u32[]{:S(2)}, u32[]{:S(2)}) collective-permute-start(bf16[4,16,256]{2,1,0:T(8,128)(2,1)S(1)} %get-tuple-element.17.adj_ref), channel_id=1, source_target_pairs={{0,14},{2,4},{4,2},{6,8},{8,6},{10,12},{12,10},{14,0},{1,15},{3,5}... | collective-permute-start | bytes 98312 | tf_op jit(solution)/shard_map/ppermute | solution.py:188
  12.6 3.9 %collective-permute-start.3 = (bf16[4,16,256]{2,1,0:T(8,128)(2,1)S(1)}, bf16[4,16,256]{2,1,0:T(8,128)(2,1)S(1)}, u32[]{:S(2)}, u32[]{:S(2)}) collective-permute-start(bf16[4,16,256]{2,1,0:T(8,128)(2,1)S(1)} %get-tuple-element.17.adj_ref), channel_id=1, source_target_pairs={{0,2},{2,0},{4,6},{6,4},{8,10},{10,8},{12,14},{14,12},{1,3},{3,1},... | collective-permute-start | bytes 98312 | tf_op jit(solution)/shard_map/ppermute | solution.py:158
  12.6 5.2 %collective-permute-start.2 = (bf16[64,128]{1,0:T(8,128)(2,1)S(1)}, bf16[64,128]{1,0:T(8,128)(2,1)S(1)}, u32[]{:S(2)}, u32[]{:S(2)}) collective-permute-start(bf16[64,128]{1,0:T(8,128)(2,1)S(1)} %pad_maximum_fusion.1), channel_id=1, source_target_pairs={{0,8},{2,10},{4,12},{6,14},{8,0},{10,2},{12,4},{14,6},{1,9},{3,11}... | collective-permute-start | bytes 49160 | tf_op jit(solution)/shard_map/ppermute | solution.py:158

commit v3 on v2

--- a/solution.py
+++ b/solution.py
@@ -183,9 +183,12 @@
         name="source",
     )(*map(in_hbm, (far_dst, adjoint, leaf_basis_out, transfer_up, far_coupling, *later)))
 
-    other = [(i, (i + (1 if i % 2 else -1)) % nodes) for i in range(nodes)]
+    cores = lax.axis_size("sub")
+    inner = [(i, i + 1 if i % 2 else i - 1) for i in range(1, nodes - 1)]
+    other = [(i * cores + c, j * cores + c) for i, j in inner for c in range(cores)]
+    other += [(i * cores + c, i * cores + (c + 1) % cores) for i in (0, nodes - 1) for c in range(cores)]
     a = exchange(adjoint_v, 1)
-    b = lax.ppermute(adjoint_v, NODE_AXES, other)
+    b = lax.ppermute(adjoint_v, NODE_AXES + ("sub",), other)
 
     coefs = [send[nodes // 2 * rows :]]
     for step in range(steps):

time: 19 us -> 17.2 us (0.905)
  waiting for transfers between devices: 4.14 us -> 2.56 us
  starting transfers between devices: 10.2 us -> 10 us
    ppermute x1, starting transfers between devices: 3.4 us -> 0.01 us  [on_device(): b = lax.ppermute(adjoint_v, NODE_AXES + ('sub',), other)]
    ppermute x4, starting transfers between devices: 6.84 us -> 10 us  [exchange(): return lax.ppermute(x, NODE_AXES, [(i, i ^ distance) for i in range(nodes)])]
    ppermute x1, waiting for transfers between devices: 1.52 us -> 0.01 us  [on_device(): b = lax.ppermute(adjoint_v, NODE_AXES + ('sub',), other)]
  transfers between devices with their start and end apart: 5 -> 5, of which waited for: 3 -> 3; matrix products, arithmetic and copies ran while one was open for 0% -> 0% of each run, Pallas kernels for 7% -> 8%
where the time goes in v3:
time: 17.2 us; the launch traced here: 17 us
  starting transfers between devices  10 us (58%)
  Pallas kernels  4.29 us (25%)
  waiting for transfers between devices  2.56 us (15%)
    ppermute x4, starting transfers between devices, exchange(): return lax.ppermute(x, NODE_AXES, [(i, i ^ distance) for i in range(nodes)])  10 us
    ppermute x4, waiting for transfers between devices, exchange(): return lax.ppermute(x, NODE_AXES, [(i, i ^ distance) for i in range(nodes)])  2.56 us
    pallas_call x1, Pallas kernels, on_device(): pl.pallas_call(functools.partial(source_kernel, nodes), out_shape=(jax.Sh...  2.01 us
    pallas_call x1, Pallas kernels, on_device(): pl.pallas_call(functools.partial(near_kernel, nodes), out_shape=(jax.Shap...  1.3 us
    pallas_call x1, Pallas kernels, on_device(): pl.pallas_call(final_kernel, out_shape=jax.ShapeDtypeStruct((leaf_dev, ve...  0.98 us
  transfers between devices with their start and end apart: 5, of which 3 were waited for; matrix products, arithmetic and copies ran while one was open for 0% of the time, Pallas kernels for 8%

profile of v3, /device:TPU:0, one launch (start us, length us, event | category | flops | bytes accessed | tf_op | source)
XLA Modules:
  0.0 17.0 jit_solution(11738707411306926162)
XLA Ops:
  0.0 2.0 %source.1 = (bf16[144,128]{1,0:T(8,128)(2,1)S(1)}, f32[128,128]{1,0:T(8,128)S(1)}, bf16[4,16,256]{2,1,0:T(8,128)(2,1)S(1)}, bf16[4,768,256]{2,1,0:T(8,128)(2,1)S...) custom-call(s32[4,8]{1,0:T(4,128)} %refs_0_.1, ...), custom_call_target="tpu_custom_call" | custom-call | tf_op jit(solution)/shard_map/source/pallas_call | solution.py:164
  2.0 3.0 %collective-permute-start = (bf16[144,128]{1,0:T(8,128)(2,1)S(1)}, bf16[144,128]{1,0:T(8,128)(2,1)S(1)}, u32[]{:S(2)}, u32[]{:S(2)}) collective-permute-start(bf16[144,128]{1,0:T(8,128)(2,1)S(1)} %get-tuple-element.16), channel_id=1, source_target_pairs={{0,2},{2,0},{4,6},{6,4},{8,10},{10,8},{12,14},{14,12},{1,3},{3,1},... | collective-permute-start | bytes 110600 | tf_op jit(solution)/shard_map/ppermute | solution.py:158
  5.0 1.9 %collective-permute-done = bf16[144,128]{1,0:T(8,128)(2,1)S(1)} collective-permute-done((bf16[144,128]{1,0:T(8,128)(2,1)S(1)}, bf16[144,128]{1,0:T(8,128)(2,1)S(1)}, u32[]{:S(2)}, u32[]{:S(2)}) %collective-permute-start) | collective-permute-done | bytes 36896 | tf_op jit(solution)/shard_map/ppermute | solution.py:158
  7.0 2.2 %collective-permute-start.1 = (bf16[80,128]{1,0:T(8,128)(2,1)S(1)}, bf16[80,128]{1,0:T(8,128)(2,1)S(1)}, u32[]{:S(2)}, u32[]{:S(2)}) collective-permute-start(bf16[80,128]{1,0:T(8,128)(2,1)S(1)} %pad_maximum_fusion), channel_id=1, source_target_pairs={{0,4},{2,6},{4,0},{6,2},{8,12},{10,14},{12,8},{14,10},{1,5},{3,7},... | collective-permute-start | bytes 61448 | tf_op jit(solution)/shard_map/ppermute | solution.py:158
  9.2 0.0 collective-permute-start.4
  9.2 1.5 %collective-permute-start.3 = (bf16[4,16,256]{2,1,0:T(8,128)(2,1)S(1)}, bf16[4,16,256]{2,1,0:T(8,128)(2,1)S(1)}, u32[]{:S(2)}, u32[]{:S(2)}) collective-permute-start(bf16[4,16,256]{2,1,0:T(8,128)(2,1)S(1)} %get-tuple-element.17.adj_ref), channel_id=1, source_target_pairs={{0,2},{2,0},{4,6},{6,4},{8,10},{10,8},{12,14},{14,12},{1,3},{3,1},... | collective-permute-start | bytes 98312 | tf_op jit(solution)/shard_map/ppermute | solution.py:158
  10.7 0.2 %collective-permute-done.1 = bf16[80,128]{1,0:T(8,128)(2,1)S(1)} collective-permute-done((bf16[80,128]{1,0:T(8,128)(2,1)S(1)}, bf16[80,128]{1,0:T(8,128)(2,1)S(1)}, u32[]{:S(2)}, u32[]{:S(2)}) %collective-permute-start.1) | collective-permute-done | bytes 20512 | tf_op jit(solution)/shard_map/ppermute | solution.py:158
  11.0 3.3 %collective-permute-start.2 = (bf16[64,128]{1,0:T(8,128)(2,1)S(1)}, bf16[64,128]{1,0:T(8,128)(2,1)S(1)}, u32[]{:S(2)}, u32[]{:S(2)}) collective-permute-start(bf16[64,128]{1,0:T(8,128)(2,1)S(1)} %pad_maximum_fusion.1), channel_id=1, source_target_pairs={{0,8},{2,10},{4,12},{6,14},{8,0},{10,2},{12,4},{14,6},{1,9},{3,11}... | collective-permute-start | bytes 49160 | tf_op jit(solution)/shard_map/ppermute | solution.py:158
  14.3 0.0 collective-permute-done.4.b_ref
  14.3 0.0 collective-permute-done.3.a_ref
  14.3 1.3 %near.1 = (f32[4,16,256]{2,1,0:T(8,128)S(1)}, f32[16,256]{1,0:T(8,128)S(1)}, bf16[256,256]{1,0:T(8,128)(2,1)S(1)}) custom-call(s32[4,3]{1,0:T(4,128)} %near_hbm.1, s32[1,16]{1,0:T(1,128)} %top_hbm.1, bf16[4,16,256]{2,1,0:T(8,128)(2,1)S(1)} %get-tuple-element.17.adj_ref, bf16[4,16,256]{2,1,0:T(8,128)(2,1)S(1)} %collective-permute-done.3.a_ref, ...), custom_call_target="tpu_custom_call" | custom-call | tf_op jit(solution)/shard_map/near/pallas_call | solution.py:208
  15.6 0.4 %collective-permute-done.2.got_ref = bf16[64,128]{1,0:T(8,128)(2,1)S(1)} collective-permute-done((bf16[64,128]{1,0:T(8,128)(2,1)S(1)}, bf16[64,128]{1,0:T(8,128)(2,1)S(1)}, u32[]{:S(2)}, u32[]{:S(2)}) %collective-permute-start.2) | collective-permute-done | bytes 16416 | tf_op jit(solution)/shard_map/ppermute | solution.py:158
  16.0 1.0 %final.1 = f32[4,16,256]{2,1,0:T(8,128)} custom-call(bf16[64,128]{1,0:T(8,128)(2,1)S(1)} %collective-permute-done.2.got_ref, f32[16,256]{1,0:T(8,128)S(1)} %get-tuple-element.21.base_ref, bf16[256,256]{1,0:T(8,128)(2,1)S(1)} %get-tuple-element.22.rest_ref, bf16[4,64,256]{2,1,0:T(8,128)(2,1)S(1)} %get-tuple-element.23.in_ref, ...), custom_call_target="tpu_custom_call" | custom-call | tf_op jit(solution)/shard_map/final/pallas_call | solution.py:228
  (10 shorter events, 0.1 us)
Async XLA Ops:
  2.0 4.9 %collective-permute-start = (bf16[144,128]{1,0:T(8,128)(2,1)S(1)}, bf16[144,128]{1,0:T(8,128)(2,1)S(1)}, u32[]{:S(2)}, u32[]{:S(2)}) collective-permute-start(bf16[144,128]{1,0:T(8,128)(2,1)S(1)} %get-tuple-element.16), channel_id=1, source_target_pairs={{0,2},{2,0},{4,6},{6,4},{8,10},{10,8},{12,14},{14,12},{1,3},{3,1},... | collective-permute-start | bytes 110600 | tf_op jit(solution)/shard_map/ppermute | solution.py:158
  7.0 3.9 %collective-permute-start.1 = (bf16[80,128]{1,0:T(8,128)(2,1)S(1)}, bf16[80,128]{1,0:T(8,128)(2,1)S(1)}, u32[]{:S(2)}, u32[]{:S(2)}) collective-permute-start(bf16[80,128]{1,0:T(8,128)(2,1)S(1)} %pad_maximum_fusion), channel_id=1, source_target_pairs={{0,4},{2,6},{4,0},{6,2},{8,12},{10,14},{12,8},{14,10},{1,5},{3,7},... | collective-permute-start | bytes 61448 | tf_op jit(solution)/shard_map/ppermute | solution.py:158
  9.2 5.1 %collective-permute-start.4 = (bf16[4,16,256]{2,1,0:T(8,128)(2,1)S(1)}, bf16[4,16,256]{2,1,0:T(8,128)(2,1)S(1)}, u32[]{:S(2)}, u32[]{:S(2)}) collective-permute-start(bf16[4,16,256]{2,1,0:T(8,128)(2,1)S(1)} %get-tuple-element.17.adj_ref), channel_id=1, source_target_pairs={{2,4},{3,5},{4,2},{5,3},{6,8},{7,9},{8,6},{9,7},{10,12},{11,13},{1... | collective-permute-start | bytes 98312 | tf_op jit(solution)/shard_map/ppermute | solution.py:191
  9.2 5.1 %collective-permute-start.3 = (bf16[4,16,256]{2,1,0:T(8,128)(2,1)S(1)}, bf16[4,16,256]{2,1,0:T(8,128)(2,1)S(1)}, u32[]{:S(2)}, u32[]{:S(2)}) collective-permute-start(bf16[4,16,256]{2,1,0:T(8,128)(2,1)S(1)} %get-tuple-element.17.adj_ref), channel_id=1, source_target_pairs={{0,2},{2,0},{4,6},{6,4},{8,10},{10,8},{12,14},{14,12},{1,3},{3,1},... | collective-permute-start | bytes 98312 | tf_op jit(solution)/shard_map/ppermute | solution.py:158
  11.0 5.0 %collective-permute-start.2 = (bf16[64,128]{1,0:T(8,128)(2,1)S(1)}, bf16[64,128]{1,0:T(8,128)(2,1)S(1)}, u32[]{:S(2)}, u32[]{:S(2)}) collective-permute-start(bf16[64,128]{1,0:T(8,128)(2,1)S(1)} %pad_maximum_fusion.1), channel_id=1, source_target_pairs={{0,8},{2,10},{4,12},{6,14},{8,0},{10,2},{12,4},{14,6},{1,9},{3,11}... | collective-permute-start | bytes 49160 | tf_op jit(solution)/shard_map/ppermute | solution.py:158

commit v4 on v3

v4 whole, which is shorter than its diff:
```python
import functools

import jax
import jax.numpy as jnp
from jax import lax
from jax.experimental import pallas as pl
from jax.experimental.pallas import tpu as pltpu
from jax.sharding import PartitionSpec as P

F32 = jnp.float32
BF16 = jnp.bfloat16
NODE_AXES = ("leaf", "vec")
NT = (((1,), (1,)), ((), ()))
TN = (((0,), (0,)), ((), ()))
VMEM = pl.BlockSpec(memory_space=pltpu.VMEM)
HBM = pl.BlockSpec(memory_space=pltpu.HBM)
PARAMS = pltpu.CompilerParams(vmem_limit_bytes=24 << 20)


def bits_of(count):
    return count.bit_length() - 1


def reversed_bits(value, width):
    return sum(((value >> bit) & 1) << (width - 1 - bit) for bit in range(width))


def lane_half(shape):
    return lax.broadcasted_iota(jnp.int32, shape, 1) // (shape[1] // 2)


def in_hbm(x):
    return pltpu.with_memory_space_constraint(x, pltpu.HBM)


def side_by_side(stacked, rows):
    return jnp.concatenate([stacked[at : at + rows] for at in range(0, stacked.shape[0], rows)], axis=1)


def source_kernel(nodes, *refs):
    sources, (send_ref, keep_ref, adj_ref, *later), scratch = refs[:9], refs[9:16], refs[16:]
    dst_ref, out_ref, far_ref, up_ref, sums, sems = scratch
    copies = [
        pltpu.make_async_copy(there, here, sems.at[i])
        for i, (there, here) in enumerate(zip(sources, (dst_ref, adj_ref, out_ref, far_ref, up_ref, *later)))
    ]
    for copy in copies:
        copy.start()
    leaf_dev, vectors, _ = adj_ref.shape
    rank = out_ref.shape[1]
    far_count = dst_ref.shape[1]
    pairs = leaf_dev // 2
    wide = 2 * rank
    within = bits_of(leaf_dev)
    me = lax.axis_index(NODE_AXES)
    sums[...] = jnp.zeros_like(sums)
    half = lane_half((vectors, wide))
    for copy in copies[:3]:
        copy.wait()
    coefs = [
        lax.dot_general(adj_ref[j], out_ref[j], NT, preferred_element_type=F32).astype(BF16) for j in range(leaf_dev)
    ]
    copies[3].wait()
    for j in range(leaf_dev):
        contrib = jnp.dot(coefs[j], far_ref[j], preferred_element_type=F32)
        for g in range(far_count // 2):
            straight = contrib[:, g * wide : (g + 1) * wide]
            turned = pltpu.roll(straight, rank, 1)
            for h in range(2):
                target = dst_ref[j, 2 * g + h]
                place = ((target >> within) ^ me) * pairs + ((target & (leaf_dev - 1)) >> 1)
                side = target & 1
                value = jnp.where(jnp.full(half.shape, side) == h, straight, turned)
                sums[j, place] += jnp.where(half == side, value, 0.0)
    copies[4].wait()
    node = lax.dot_general(jnp.concatenate(coefs, axis=1), up_ref[0], NT, preferred_element_type=F32).astype(BF16)
    node = jnp.concatenate([node, node], axis=1)
    rows = pairs * vectors
    width = bits_of(nodes)
    for r in range(nodes):
        d = reversed_bits(r, width)
        block = sum(sums[j, d * pairs : (d + 1) * pairs] for j in range(leaf_dev)).reshape(rows, wide)
        if r < nodes // 2:
            keep_ref[r * rows : (r + 1) * rows] = block
        else:
            at = (r - nodes // 2) * rows
            send_ref[at : at + rows] = block.astype(BF16)
    send_ref[nodes // 2 * rows :] = node
    keep_ref[nodes // 2 * rows :] = node.astype(F32)
    for copy in copies[5:]:
        copy.wait()


def top_kernel(src_hbm, top_ref, down_ref, matrix_ref, src_ref, by_node, sem):
    copy = pltpu.make_async_copy(src_hbm, src_ref, sem.at[0])
    copy.start()
    rank = down_ref.shape[1]
    me = lax.axis_index(NODE_AXES)
    by_node[...] = jnp.zeros_like(by_node)
    through = lax.dot_general(top_ref[0], down_ref[0], TN, preferred_element_type=F32)
    copy.wait()
    for k in range(src_ref.shape[1]):
        by_node[src_ref[0, k] ^ me] += through[k * rank : (k + 1) * rank]
    matrix_ref[...] = by_node[...].reshape(matrix_ref.shape).astype(BF16)


def near_kernel(src_hbm, adj_ref, a_ref, b_ref, tiles_ref, near_ref, src_ref, around, sem):
    copy = pltpu.make_async_copy(src_hbm, src_ref, sem.at[0])
    copy.start()
    leaf_dev, vectors, cells = adj_ref.shape
    me = lax.axis_index(NODE_AXES)
    around[:leaf_dev] = adj_ref[...]
    around[leaf_dev : 2 * leaf_dev] = a_ref[...]
    around[2 * leaf_dev :] = b_ref[...]
    copy.wait()
    for j in range(leaf_dev):
        total = None
        for k in range(src_ref.shape[1]):
            source = src_ref[j, k]
            node = source // leaf_dev
            base = jnp.where(node == me, 0, jnp.where(node == (me ^ 1), leaf_dev, 2 * leaf_dev))
            block = around[base + source % leaf_dev]
            part = jnp.dot(block, tiles_ref[j, k * cells : (k + 1) * cells], preferred_element_type=F32)
            total = part if total is None else total + part
        near_ref[j] = total


def final_kernel(got_ref, kept_ref, matrix_ref, in_ref, near_ref, out_ref):
    leaf_dev, vectors, _ = near_ref.shape
    rank = in_ref.shape[1]
    rows = leaf_dev // 2 * vectors
    coefs = [side_by_side(kept_ref[rows:].astype(BF16), vectors), side_by_side(got_ref[rows:], vectors)]
    down = jnp.dot(jnp.concatenate(coefs, axis=1), matrix_ref[...], preferred_element_type=F32)
    leaf_in = side_by_side(kept_ref[:rows] + got_ref[:rows].astype(F32), vectors)
    mixed = (leaf_in + down).astype(BF16)
    for j in range(leaf_dev):
        far = jnp.dot(mixed[:, j * rank : (j + 1) * rank], in_ref[j], preferred_element_type=F32)
        out_ref[j] = near_ref[j] + far


def on_device(
    adjoint, leaf_basis_out, leaf_basis_in, transfer_up, transfer_down, far_coupling, top_coupling, near_tiles, near_src, far_dst, top_src
):
    leaf_dev, vectors, cells = adjoint.shape
    rank = leaf_basis_out.shape[1]
    wide = 2 * rank
    pairs = leaf_dev // 2
    rows = pairs * vectors
    nodes = lax.axis_size(NODE_AXES)
    steps = bits_of(nodes)

    cores = lax.axis_size("sub")

    def swapped(x, partner, flip):
        pairs = [(i * cores + c, partner(i) * cores + (cores - 1 - c if flip else c)) for i in range(nodes) for c in range(cores)]
        return lax.ppermute(x, NODE_AXES + ("sub",), pairs)

    def like(x):
        return jax.ShapeDtypeStruct(x.shape, x.dtype)

    later = (near_tiles, top_coupling, transfer_down, leaf_basis_in)
    send, keep, adjoint_v, tiles, top, down, basis_in = pl.pallas_call(
        functools.partial(source_kernel, nodes),
        out_shape=(
            jax.ShapeDtypeStruct((nodes // 2 * rows + vectors, wide), BF16),
            jax.ShapeDtypeStruct((nodes // 2 * rows + vectors, wide), F32),
            like(adjoint),
            *map(like, later),
        ),
        in_specs=[HBM] * 9,
        out_specs=(VMEM,) * 7,
        scratch_shapes=[
            pltpu.SMEM(far_dst.shape, jnp.int32),
            pltpu.VMEM(leaf_basis_out.shape, BF16),
            pltpu.VMEM(far_coupling.shape, BF16),
            pltpu.VMEM(transfer_up.shape, BF16),
            pltpu.VMEM((leaf_dev, nodes * pairs, vectors, wide), F32),
            pltpu.SemaphoreType.DMA((9,)),
        ],
        compiler_params=PARAMS,
        name="source",
    )(*map(in_hbm, (far_dst, adjoint, leaf_basis_out, far_coupling, transfer_up, *later)))

    matrix = pl.pallas_call(
        top_kernel,
        out_shape=jax.ShapeDtypeStruct((nodes * rank, leaf_dev * rank), BF16),
        in_specs=[HBM] + [VMEM] * 2,
        out_specs=VMEM,
        scratch_shapes=[
            pltpu.SMEM(top_src.shape, jnp.int32),
            pltpu.VMEM((nodes, rank, leaf_dev * rank), F32),
            pltpu.SemaphoreType.DMA((1,)),
        ],
        compiler_params=PARAMS,
        name="top",
    )(in_hbm(top_src), top, down)

    inner = [(i, i + 1 if i % 2 else i - 1) for i in range(1, nodes - 1)]
    other = [(i * cores + c, j * cores + c) for i, j in inner for c in range(cores)]
    other += [(i * cores + c, i * cores + (c + 1) % cores) for i in (0, nodes - 1) for c in range(cores)]
    a = swapped(adjoint_v, lambda i: i ^ 1, False)
    b = lax.ppermute(lax.optimization_barrier((adjoint_v, a, matrix))[0], NODE_AXES + ("sub",), other)

    coefs = None
    for step in range(steps):
        flip = step in (0, steps - 1)
        half = (nodes >> (step + 1)) * rows
        if step:
            send = jnp.concatenate([keep[half:].astype(BF16)] + coefs, axis=0)
            keep = keep[:half]
            if flip:
                keep = jnp.concatenate([keep] + [coef.astype(F32) for coef in coefs], axis=0)
        got = swapped(send, lambda i: i ^ (1 << step), flip)
        if flip:
            keep = swapped(keep, lambda i: i, True)
        if step == 0:
            coefs = [jnp.where(jnp.arange(wide) < rank, keep[half:].astype(BF16), got[half:])]
        elif step < steps - 1:
            coefs.append(got[half:])
        if step < steps - 1:
            keep = keep[:half] + got[:half].astype(F32)

    near = pl.pallas_call(
        near_kernel,
        out_shape=jax.ShapeDtypeStruct((leaf_dev, vectors, cells), F32),
        in_specs=[HBM] + [VMEM] * 4,
        out_specs=VMEM,
        scratch_shapes=[
            pltpu.SMEM(near_src.shape, jnp.int32),
            pltpu.VMEM((3 * leaf_dev, vectors, cells), BF16),
            pltpu.SemaphoreType.DMA((1,)),
        ],
        compiler_params=PARAMS,
        name="near",
    )(in_hbm(near_src), adjoint_v, a, b, tiles)

    return pl.pallas_call(
        final_kernel,
        out_shape=jax.ShapeDtypeStruct((leaf_dev, vectors, cells), F32),
        in_specs=[VMEM] * 5,
        out_specs=VMEM,
        compiler_params=PARAMS,
        name="final",
    )(got, keep, matrix, basis_in, near)


def solution(mesh):
    split = P(("design", "leaf", "vec"), None, None)
    in_specs = (P(("design", "leaf", "vec"), "sub", None),) + (split,) * 7 + (P(("design", "leaf", "vec"), None),) * 3
    out_specs = P(("design", "leaf", "vec"), "sub", None)
    return jax.shard_map(on_device, mesh=mesh, in_specs=in_specs, out_specs=out_specs, check_vma=False)
```

time: 17.2 us -> 16.1 us (0.936)
  starting transfers between devices: 10 us -> 7.97 us
  waiting for transfers between devices: 2.56 us -> 3.17 us
  Pallas kernels: 4.29 us -> 4.62 us
    ppermute x5 -> x7, starting transfers between devices: 10 us -> 7.97 us  [the longest x6 7.74 us: swapped(): return lax.ppermute(x, NODE_AXES + ('sub',), pairs)]
    ppermute x5 -> x7, waiting for transfers between devices: 2.56 us -> 3.17 us  [the longest x6 3.16 us: swapped(): return lax.ppermute(x, NODE_AXES + ('sub',), pairs)]
    pallas_call x1 -> x2, Pallas kernels: 1.3 us -> 1.85 us  [the longest x1 1.02 us: on_device(): pl.pallas_call(near_kernel, out_shape=jax.ShapeDtypeStruct((leaf_dev, vec...]
    pallas_call x1, Pallas kernels: 2.01 us -> 1.75 us  [on_device(): pl.pallas_call(functools.partial(source_kernel, nodes), out_shape=(jax.Sh...]
  transfers between devices with their start and end apart: 5 -> 7, of which waited for: 3 -> 3; matrix products, arithmetic and copies ran while one was open for 0% -> 0% of each run, Pallas kernels for 8% -> 12%
where the time goes in v4:
time: 16.1 us; the launch traced here: 15.9 us
  starting transfers between devices  7.97 us (50%)
  Pallas kernels  4.62 us (29%)
  waiting for transfers between devices  3.17 us (20%)
    ppermute x6, starting transfers between devices, swapped(): return lax.ppermute(x, NODE_AXES + ('sub',), pairs)  7.74 us
    ppermute x6, waiting for transfers between devices, swapped(): return lax.ppermute(x, NODE_AXES + ('sub',), pairs)  3.16 us
    pallas_call x1, Pallas kernels, on_device(): pl.pallas_call(functools.partial(source_kernel, nodes), out_shape=(jax.Sh...  1.75 us
    pallas_call x1, Pallas kernels, on_device(): pl.pallas_call(near_kernel, out_shape=jax.ShapeDtypeStruct((leaf_dev, vec...  1.02 us
    pallas_call x1, Pallas kernels, on_device(): pl.pallas_call(final_kernel, out_shape=jax.ShapeDtypeStruct((leaf_dev, ve...  1.01 us
    pallas_call x1, Pallas kernels, on_device(): pl.pallas_call(top_kernel, out_shape=jax.ShapeDtypeStruct((nodes * rank,...  0.84 us
  transfers between devices with their start and end apart: 7, of which 3 were waited for; matrix products, arithmetic and copies ran while one was open for 0% of the time, Pallas kernels for 12%

profile of v4, /device:TPU:0, one launch (start us, length us, event | category | flops | bytes accessed | tf_op | source)
XLA Modules:
  0.0 15.9 jit_solution(11968785711039678121)
XLA Ops:
  0.0 1.8 %source.1 = (bf16[144,128]{1,0:T(8,128)(2,1)S(1)}, f32[144,128]{1,0:T(8,128)S(1)}, bf16[4,16,256]{2,1,0:T(8,128)(2,1)S(1)}, bf16[4,768,256]{2,1,0:T(8,128)(2,1)S...) custom-call(s32[4,8]{1,0:T(4,128)} %refs_0_.1, ...), custom_call_target="tpu_custom_call" | custom-call | tf_op jit(solution)/shard_map/source/pallas_call | solution.py:162
  1.8 0.5 %collective-permute-start = (f32[144,128]{1,0:T(8,128)S(1)}, f32[144,128]{1,0:T(8,128)S(1)}, u32[]{:S(2)}, u32[]{:S(2)}) collective-permute-start(f32[144,128]{1,0:T(8,128)S(1)} %get-tuple-element.13), channel_id=1, source_target_pairs={{0,1},{1,0},{2,3},{3,2},{4,5},{5,4},{6,7},{7,6},{8,9},{9,8},{10,11... | collective-permute-start | bytes 221192 | tf_op jit(solution)/shard_map/ppermute | solution.py:156
  2.3 2.6 %collective-permute-start.1 = (bf16[144,128]{1,0:T(8,128)(2,1)S(1)}, bf16[144,128]{1,0:T(8,128)(2,1)S(1)}, u32[]{:S(2)}, u32[]{:S(2)}) collective-permute-start(bf16[144,128]{1,0:T(8,128)(2,1)S(1)} %get-tuple-element.14), channel_id=1, source_target_pairs={{0,3},{1,2},{2,1},{3,0},{4,7},{5,6},{6,5},{7,4},{8,11},{9,10},{10,... | collective-permute-start | bytes 110600 | tf_op jit(solution)/shard_map/ppermute | solution.py:156
  4.9 0.0 collective-permute-start.5
  4.9 1.7 %collective-permute-done.1 = bf16[144,128]{1,0:T(8,128)(2,1)S(1)} collective-permute-done((bf16[144,128]{1,0:T(8,128)(2,1)S(1)}, bf16[144,128]{1,0:T(8,128)(2,1)S(1)}, u32[]{:S(2)}, u32[]{:S(2)}) %collective-permute-start.1) | collective-permute-done | bytes 36896 | tf_op jit(solution)/shard_map/ppermute | solution.py:156
  6.7 0.0 collective-permute-done
  6.7 1.7 %collective-permute-start.2 = (bf16[80,128]{1,0:T(8,128)(2,1)S(1)}, bf16[80,128]{1,0:T(8,128)(2,1)S(1)}, u32[]{:S(2)}, u32[]{:S(2)}) collective-permute-start(bf16[80,128]{1,0:T(8,128)(2,1)S(1)} %pad_maximum_fusion.1), channel_id=1, source_target_pairs={{0,4},{1,5},{2,6},{3,7},{4,0},{5,1},{6,2},{7,3},{8,12},{9,13},{10,... | collective-permute-start | bytes 61448 | tf_op jit(solution)/shard_map/ppermute | solution.py:156
  8.4 0.8 %top.1.matrix_ref = bf16[512,256]{1,0:T(8,128)(2,1)S(1)} custom-call(s32[1,16]{1,0:T(1,128)} %src_hbm.2, bf16[1,64,1024]{2,1,0:T(8,128)(2,1)S(1)} %get-tuple-element.15.top_ref, bf16[1,64,256]{2,1,0:T(8,128)(2,1)S(1)} %get-tuple-element.16.down_ref), custom_call_target="tpu_custom_call" | custom-call | tf_op jit(solution)/shard_map/top/pallas_call | solution.py:184
  9.3 0.0 collective-permute-done.5.a_ref
  9.3 0.2 %collective-permute-start.6 = (bf16[4,16,256]{2,1,0:T(8,128)(2,1)S(1)}, bf16[4,16,256]{2,1,0:T(8,128)(2,1)S(1)}, u32[]{:S(2)}, u32[]{:S(2)}) collective-permute-start(bf16[4,16,256]{2,1,0:T(8,128)(2,1)S(1)} %get-tuple-element.19.adj_ref), channel_id=1, source_target_pairs={{2,4},{3,5},{4,2},{5,3},{6,8},{7,9},{8,6},{9,7},{10,12},{11,13},{1... | collective-permute-start | bytes 98312 | tf_op jit(solution)/shard_map/ppermute | solution.py:202
  9.5 1.0 %collective-permute-done.2 = bf16[80,128]{1,0:T(8,128)(2,1)S(1)} collective-permute-done((bf16[80,128]{1,0:T(8,128)(2,1)S(1)}, bf16[80,128]{1,0:T(8,128)(2,1)S(1)}, u32[]{:S(2)}, u32[]{:S(2)}) %collective-permute-start.2) | collective-permute-done | bytes 20512 | tf_op jit(solution)/shard_map/ppermute | solution.py:156
  10.6 0.1 collective-permute-start.4
  10.7 2.8 %collective-permute-start.3 = (bf16[64,128]{1,0:T(8,128)(2,1)S(1)}, bf16[64,128]{1,0:T(8,128)(2,1)S(1)}, u32[]{:S(2)}, u32[]{:S(2)}) collective-permute-start(bf16[64,128]{1,0:T(8,128)(2,1)S(1)} %pad_maximum_fusion.2), channel_id=1, source_target_pairs={{0,9},{1,8},{2,11},{3,10},{4,13},{5,12},{6,15},{7,14},{8,1},{9,0},... | collective-permute-start | bytes 49160 | tf_op jit(solution)/shard_map/ppermute | solution.py:156
  13.5 0.0 collective-permute-done.6.b_ref
  13.5 1.0 %near.1.near_ref = f32[4,16,256]{2,1,0:T(8,128)S(1)} custom-call(s32[4,3]{1,0:T(4,128)} %src_hbm.3, bf16[4,16,256]{2,1,0:T(8,128)(2,1)S(1)} %get-tuple-element.19.adj_ref, bf16[4,16,256]{2,1,0:T(8,128)(2,1)S(1)} %collective-permute-done.5.a_ref, bf16[4,16,256]{2,1,0:T(8,128)(2,1)S(1)} %collective-permute-done.6.b_ref, ...), custom_call_target="tpu_custom_call" | custom-call | tf_op jit(solution)/shard_map/near/pallas_call | solution.py:223
  14.5 0.4 %collective-permute-done.3.got_ref = bf16[64,128]{1,0:T(8,128)(2,1)S(1)} collective-permute-done((bf16[64,128]{1,0:T(8,128)(2,1)S(1)}, bf16[64,128]{1,0:T(8,128)(2,1)S(1)}, u32[]{:S(2)}, u32[]{:S(2)}) %collective-permute-start.3) | collective-permute-done | bytes 16416 | tf_op jit(solution)/shard_map/ppermute | solution.py:156
  14.9 0.0 collective-permute-done.4.kept_ref
  14.9 1.0 %final.1 = f32[4,16,256]{2,1,0:T(8,128)} custom-call(bf16[64,128]{1,0:T(8,128)(2,1)S(1)} %collective-permute-done.3.got_ref, f32[64,128]{1,0:T(8,128)S(1)} %collective-permute-done.4.kept_ref, bf16[512,256]{1,0:T(8,128)(2,1)S(1)} %top.1.matrix_ref, bf16[4,64,256]{2,1,0:T(8,128)(2,1)S(1)} %get-tuple-element.17.in_ref, f32[4,16,256]{2,1,0:T(8,128)S(1)} %near.1.near_ref), custom_call_target="tpu_custom_call" | custom-call | tf_op jit(solution)/shard_map/final/pallas_call | solution.py:237
  (11 shorter events, 0.1 us)
Async XLA Ops:
  1.8 4.9 %collective-permute-start = (f32[144,128]{1,0:T(8,128)S(1)}, f32[144,128]{1,0:T(8,128)S(1)}, u32[]{:S(2)}, u32[]{:S(2)}) collective-permute-start(f32[144,128]{1,0:T(8,128)S(1)} %get-tuple-element.13), channel_id=1, source_target_pairs={{0,1},{1,0},{2,3},{3,2},{4,5},{5,4},{6,7},{7,6},{8,9},{9,8},{10,11... | collective-permute-start | bytes 221192 | tf_op jit(solution)/shard_map/ppermute | solution.py:156
  2.3 4.4 %collective-permute-start.1 = (bf16[144,128]{1,0:T(8,128)(2,1)S(1)}, bf16[144,128]{1,0:T(8,128)(2,1)S(1)}, u32[]{:S(2)}, u32[]{:S(2)}) collective-permute-start(bf16[144,128]{1,0:T(8,128)(2,1)S(1)} %get-tuple-element.14), channel_id=1, source_target_pairs={{0,3},{1,2},{2,1},{3,0},{4,7},{5,6},{6,5},{7,4},{8,11},{9,10},{10,... | collective-permute-start | bytes 110600 | tf_op jit(solution)/shard_map/ppermute | solution.py:156
  4.9 4.4 %collective-permute-start.5 = (bf16[4,16,256]{2,1,0:T(8,128)(2,1)S(1)}, bf16[4,16,256]{2,1,0:T(8,128)(2,1)S(1)}, u32[]{:S(2)}, u32[]{:S(2)}) collective-permute-start(bf16[4,16,256]{2,1,0:T(8,128)(2,1)S(1)} %get-tuple-element.19.adj_ref), channel_id=1, source_target_pairs={{0,2},{1,3},{2,0},{3,1},{4,6},{5,7},{6,4},{7,5},{8,10},{9,11},{10,... | collective-permute-start | bytes 98312 | tf_op jit(solution)/shard_map/ppermute | solution.py:156
  6.7 3.8 %collective-permute-start.2 = (bf16[80,128]{1,0:T(8,128)(2,1)S(1)}, bf16[80,128]{1,0:T(8,128)(2,1)S(1)}, u32[]{:S(2)}, u32[]{:S(2)}) collective-permute-start(bf16[80,128]{1,0:T(8,128)(2,1)S(1)} %pad_maximum_fusion.1), channel_id=1, source_target_pairs={{0,4},{1,5},{2,6},{3,7},{4,0},{5,1},{6,2},{7,3},{8,12},{9,13},{10,... | collective-permute-start | bytes 61448 | tf_op jit(solution)/shard_map/ppermute | solution.py:156
  9.3 4.2 %collective-permute-start.6 = (bf16[4,16,256]{2,1,0:T(8,128)(2,1)S(1)}, bf16[4,16,256]{2,1,0:T(8,128)(2,1)S(1)}, u32[]{:S(2)}, u32[]{:S(2)}) collective-permute-start(bf16[4,16,256]{2,1,0:T(8,128)(2,1)S(1)} %get-tuple-element.19.adj_ref), channel_id=1, source_target_pairs={{2,4},{3,5},{4,2},{5,3},{6,8},{7,9},{8,6},{9,7},{10,12},{11,13},{1... | collective-permute-start | bytes 98312 | tf_op jit(solution)/shard_map/ppermute | solution.py:202
  10.6 4.3 %collective-permute-start.4 = (f32[64,128]{1,0:T(8,128)S(1)}, f32[64,128]{1,0:T(8,128)S(1)}, u32[]{:S(2)}, u32[]{:S(2)}) collective-permute-start(f32[64,128]{1,0:T(8,128)S(1)} %pad_maximum_fusion), channel_id=1, source_target_pairs={{0,1},{1,0},{2,3},{3,2},{4,5},{5,4},{6,7},{7,6},{8,9},{9,8},{10,11... | collective-permute-start | bytes 98312 | tf_op jit(solution)/shard_map/ppermute | solution.py:156
  10.7 4.2 %collective-permute-start.3 = (bf16[64,128]{1,0:T(8,128)(2,1)S(1)}, bf16[64,128]{1,0:T(8,128)(2,1)S(1)}, u32[]{:S(2)}, u32[]{:S(2)}) collective-permute-start(bf16[64,128]{1,0:T(8,128)(2,1)S(1)} %pad_maximum_fusion.2), channel_id=1, source_target_pairs={{0,9},{1,8},{2,11},{3,10},{4,13},{5,12},{6,15},{7,14},{8,1},{9,0},... | collective-permute-start | bytes 49160 | tf_op jit(solution)/shard_map/ppermute | solution.py:156

commit v5 on v4

--- a/solution.py
+++ b/solution.py
@@ -14,7 +14,7 @@
 TN = (((0,), (0,)), ((), ()))
 VMEM = pl.BlockSpec(memory_space=pltpu.VMEM)
 HBM = pl.BlockSpec(memory_space=pltpu.HBM)
-PARAMS = pltpu.CompilerParams(vmem_limit_bytes=24 << 20)
+PARAMS = pltpu.CompilerParams(vmem_limit_bytes=32 << 20)
 
 
 def bits_of(count):
@@ -38,8 +38,10 @@
 
 
 def source_kernel(nodes, *refs):
-    sources, (send_ref, keep_ref, adj_ref, *later), scratch = refs[:9], refs[9:16], refs[16:]
-    dst_ref, out_ref, far_ref, up_ref, sums, sems = scratch
+    sources, (send_ref, keep_ref, adj_ref, *later), scratch = refs[:8], refs[8:14], refs[14:]
+    dst_ref, out_ref, far_ref, up_ref, *sums, sems = scratch
+    first = later[2].shape[0]
+    sources = (*sources[:7], sources[7].at[:first])
     copies = [
         pltpu.make_async_copy(there, here, sems.at[i])
         for i, (there, here) in enumerate(zip(sources, (dst_ref, adj_ref, out_ref, far_ref, up_ref, *later)))
@@ -53,62 +55,70 @@
     wide = 2 * rank
     within = bits_of(leaf_dev)
     me = lax.axis_index(NODE_AXES)
-    sums[...] = jnp.zeros_like(sums)
+    rows = pairs * vectors
+    for one in sums:
+        one[...] = jnp.zeros_like(one)
     half = lane_half((vectors, wide))
     for copy in copies[:3]:
         copy.wait()
     coefs = [
         lax.dot_general(adj_ref[j], out_ref[j], NT, preferred_element_type=F32).astype(BF16) for j in range(leaf_dev)
     ]
-    copies[3].wait()
+    for copy in copies[3:5]:
+        copy.wait()
+    node = lax.dot_general(jnp.concatenate(coefs, axis=1), up_ref[0], NT, preferred_element_type=F32).astype(BF16)
+    node = jnp.concatenate([node, node], axis=1)
+    send_ref[nodes // 2 * rows :] = node
+    keep_ref[nodes // 2 * rows :] = node.astype(F32)
     for j in range(leaf_dev):
         contrib = jnp.dot(coefs[j], far_ref[j], preferred_element_type=F32)
-        for g in range(far_count // 2):
-            straight = contrib[:, g * wide : (g + 1) * wide]
-            turned = pltpu.roll(straight, rank, 1)
-            for h in range(2):
-                target = dst_ref[j, 2 * g + h]
-                place = ((target >> within) ^ me) * pairs + ((target & (leaf_dev - 1)) >> 1)
-                side = target & 1
-                value = jnp.where(jnp.full(half.shape, side) == h, straight, turned)
-                sums[j, place] += jnp.where(half == side, value, 0.0)
-    copies[4].wait()
-    node = lax.dot_general(jnp.concatenate(coefs, axis=1), up_ref[0], NT, preferred_element_type=F32).astype(BF16)
-    node = jnp.concatenate([node, node], axis=1)
-    rows = pairs * vectors
+        for k in range(far_count):
+            block = contrib[:, k // 2 * wide : (k // 2 + 1) * wide]
+            target = dst_ref[j, k]
+            place = ((target >> within) ^ me) * pairs + ((target & (leaf_dev - 1)) >> 1)
+            place += ((target ^ k) & 1) * (nodes * pairs)
+            sums[j][place] += jnp.where(half == k % 2, block, 0.0)
     width = bits_of(nodes)
     for r in range(nodes):
-        d = reversed_bits(r, width)
-        block = sum(sums[j, d * pairs : (d + 1) * pairs] for j in range(leaf_dev)).reshape(rows, wide)
-        if r < nodes // 2:
-            keep_ref[r * rows : (r + 1) * rows] = block
-        else:
-            at = (r - nodes // 2) * rows
-            send_ref[at : at + rows] = block.astype(BF16)
-    send_ref[nodes // 2 * rows :] = node
-    keep_ref[nodes // 2 * rows :] = node.astype(F32)
+        for p in range(pairs):
+            place = reversed_bits(r, width) * pairs + p
+            straight = sum(one[place] for one in sums)
+            turned = sum(one[nodes * pairs + place] for one in sums)
+            block = straight + pltpu.roll(turned, rank, 1)
+            at = (r % (nodes // 2)) * rows + p * vectors
+            if r < nodes // 2:
+                keep_ref[at : at + vectors] = block
+            else:
+                send_ref[at : at + vectors] = block.astype(BF16)
     for copy in copies[5:]:
         copy.wait()
 
 
-def top_kernel(src_hbm, top_ref, down_ref, matrix_ref, src_ref, by_node, sem):
-    copy = pltpu.make_async_copy(src_hbm, src_ref, sem.at[0])
-    copy.start()
+def top_kernel(src_hbm, top_ref, down_ref, tiles_hbm, in_hbm_ref, matrix_ref, tiles_ref, in_ref, src_ref, by_node, sems):
+    sources = (src_hbm, tiles_hbm.at[tiles_hbm.shape[0] - tiles_ref.shape[0] :], in_hbm_ref)
+    copies = [
+        pltpu.make_async_copy(there, here, sems.at[i]) for i, (there, here) in enumerate(zip(sources, (src_ref, tiles_ref, in_ref)))
+    ]
+    for copy in copies:
+        copy.start()
     rank = down_ref.shape[1]
     me = lax.axis_index(NODE_AXES)
     by_node[...] = jnp.zeros_like(by_node)
     through = lax.dot_general(top_ref[0], down_ref[0], TN, preferred_element_type=F32)
-    copy.wait()
+    copies[0].wait()
     for k in range(src_ref.shape[1]):
         by_node[src_ref[0, k] ^ me] += through[k * rank : (k + 1) * rank]
     matrix_ref[...] = by_node[...].reshape(matrix_ref.shape).astype(BF16)
-
-
-def near_kernel(src_hbm, adj_ref, a_ref, b_ref, tiles_ref, near_ref, src_ref, around, sem):
+    for copy in copies[1:]:
+        copy.wait()
+
+
+def near_kernel(src_hbm, adj_ref, a_ref, b_ref, tiles_ref, more_tiles_ref, near_ref, src_ref, around, sem):
     copy = pltpu.make_async_copy(src_hbm, src_ref, sem.at[0])
     copy.start()
     leaf_dev, vectors, cells = adj_ref.shape
     me = lax.axis_index(NODE_AXES)
+    first = tiles_ref.shape[0]
     around[:leaf_dev] = adj_ref[...]
     around[leaf_dev : 2 * leaf_dev] = a_ref[...]
     around[2 * leaf_dev :] = b_ref[...]
@@ -120,7 +130,8 @@
             node = source // leaf_dev
             base = jnp.where(node == me, 0, jnp.where(node == (me ^ 1), leaf_dev, 2 * leaf_dev))
             block = around[base + source % leaf_dev]
-            part = jnp.dot(block, tiles_ref[j, k * cells : (k + 1) * cells], preferred_element_type=F32)
+            tiles, at = (tiles_ref, j) if j < first else (more_tiles_ref, j - first)
+            part = jnp.dot(block, tiles[at, k * cells : (k + 1) * cells], preferred_element_type=F32)
             total = part if total is None else total + part
         near_ref[j] = total
 
@@ -158,48 +169,57 @@
     def like(x):
         return jax.ShapeDtypeStruct(x.shape, x.dtype)
 
-    later = (near_tiles, top_coupling, transfer_down, leaf_basis_in)
-    send, keep, adjoint_v, tiles, top, down, basis_in = pl.pallas_call(
+    first = leaf_dev // 2
+    tiles_shape = (first,) + near_tiles.shape[1:]
+    more_shape = (leaf_dev - first,) + near_tiles.shape[1:]
+    send, keep, adjoint_v, top, down, tiles = pl.pallas_call(
         functools.partial(source_kernel, nodes),
         out_shape=(
             jax.ShapeDtypeStruct((nodes // 2 * rows + vectors, wide), BF16),
             jax.ShapeDtypeStruct((nodes // 2 * rows + vectors, wide), F32),
             like(adjoint),
-            *map(like, later),
+            like(top_coupling),
+            like(transfer_down),
+            jax.ShapeDtypeStruct(tiles_shape, BF16),
         ),
-        in_specs=[HBM] * 9,
-        out_specs=(VMEM,) * 7,
+        in_specs=[HBM] * 8,
+        out_specs=(VMEM,) * 6,
         scratch_shapes=[
             pltpu.SMEM(far_dst.shape, jnp.int32),
             pltpu.VMEM(leaf_basis_out.shape, BF16),
             pltpu.VMEM(far_coupling.shape, BF16),
             pltpu.VMEM(transfer_up.shape, BF16),
-            pltpu.VMEM((leaf_dev, nodes * pairs, vectors, wide), F32),
-            pltpu.SemaphoreType.DMA((9,)),
+            *[pltpu.VMEM((2 * nodes * pairs, vectors, wide), F32)] * leaf_dev,
+            pltpu.SemaphoreType.DMA((8,)),
         ],
         compiler_params=PARAMS,
         name="source",
-    )(*map(in_hbm, (far_dst, adjoint, leaf_basis_out, far_coupling, transfer_up, *later)))
-
-    matrix = pl.pallas_call(
+    )(*map(in_hbm, (far_dst, adjoint, leaf_basis_out, far_coupling, transfer_up, top_coupling, transfer_down, near_tiles)))
+
+    matrix, more_tiles, basis_in = pl.pallas_call(
         top_kernel,
-        out_shape=jax.ShapeDtypeStruct((nodes * rank, leaf_dev * rank), BF16),
-        in_specs=[HBM] + [VMEM] * 2,
-        out_specs=VMEM,
+        out_shape=(
+            jax.ShapeDtypeStruct((nodes * rank, leaf_dev * rank), BF16),
+            jax.ShapeDtypeStruct(more_shape, BF16),
+            like(leaf_basis_in),
+        ),
+        in_specs=[HBM] + [VMEM] * 2 + [HBM] * 2,
+        out_specs=(VMEM,) * 3,
         scratch_shapes=[
             pltpu.SMEM(top_src.shape, jnp.int32),
             pltpu.VMEM((nodes, rank, leaf_dev * rank), F32),
-            pltpu.SemaphoreType.DMA((1,)),
+            pltpu.SemaphoreType.DMA((3,)),
         ],
         compiler_params=PARAMS,
         name="top",
-    )(in_hbm(top_src), top, down)
+    )(in_hbm(top_src), top, down, in_hbm(near_tiles), in_hbm(leaf_basis_in))
 
     inner = [(i, i + 1 if i % 2 else i - 1) for i in range(1, nodes - 1)]
     other = [(i * cores + c, j * cores + c) for i, j in inner for c in range(cores)]
     other += [(i * cores + c, i * cores + (c + 1) % cores) for i in (0, nodes - 1) for c in range(cores)]
-    a = swapped(adjoint_v, lambda i: i ^ 1, False)
-    b = lax.ppermute(lax.optimization_barrier((adjoint_v, a, matrix))[0], NODE_AXES + ("sub",), other)
+    send, _ = lax.optimization_barrier((send, keep))
+    a = swapped(lax.optimization_barrier((adjoint_v, send, keep))[0], lambda i: i ^ 1, False)
+    b = lax.ppermute(lax.optimization_barrier((adjoint_v, a))[0], NODE_AXES + ("sub",), other)
 
     coefs = None
     for step in range(steps):
@@ -214,6 +234,7 @@
         if flip:
             keep = swapped(keep, lambda i: i, True)
         if step == 0:
+            got, _ = lax.optimization_barrier((got, matrix))
             coefs = [jnp.where(jnp.arange(wide) < rank, keep[half:].astype(BF16), got[half:])]
         elif step < steps - 1:
             coefs.append(got[half:])
@@ -223,7 +244,7 @@
     near = pl.pallas_call(
         near_kernel,
         out_shape=jax.ShapeDtypeStruct((leaf_dev, vectors, cells), F32),
-        in_specs=[HBM] + [VMEM] * 4,
+        in_specs=[HBM] + [VMEM] * 5,
         out_specs=VMEM,
         scratch_shapes=[
             pltpu.SMEM(near_src.shape, jnp.int32),
@@ -232,7 +253,7 @@
         ],
         compiler_params=PARAMS,
         name="near",
-    )(in_hbm(near_src), adjoint_v, a, b, tiles)
+    )(in_hbm(near_src), adjoint_v, a, b, tiles, more_tiles)
 
     return pl.pallas_call(
         final_kernel,

time: 16.1 us -> 15.9 us (0.988)
  starting transfers between devices: 7.97 us -> 7.75 us
    pallas_call x1, Pallas kernels: 0.84 us -> 1.18 us  [on_device(): pl.pallas_call(top_kernel, out_shape=(jax.ShapeDtypeStruct((nodes * rank,...]
    pallas_call x1, Pallas kernels: 1.75 us -> 1.51 us  [on_device(): pl.pallas_call(functools.partial(source_kernel, nodes), out_shape=(jax.Sh...]
    ppermute x1, starting transfers between devices: 0.23 us -> 0.01 us  [on_device(): lax.ppermute(lax.optimization_barrier((adjoint_v, a))[0], NODE_AXES + ('s...]
  transfers between devices with their start and end apart: 7 -> 7, of which waited for: 3 -> 4; matrix products, arithmetic and copies ran while one was open for 0% -> 0% of each run, Pallas kernels for 12% -> 14%
where the time goes in v5:
time: 15.9 us; the launch traced here: 15.7 us
  starting transfers between devices  7.75 us (49%)
  Pallas kernels  4.72 us (30%)
  waiting for transfers between devices  3.06 us (19%)
    ppermute x6, starting transfers between devices, swapped(): return lax.ppermute(x, NODE_AXES + ('sub',), pairs)  7.75 us
    ppermute x6, waiting for transfers between devices, swapped(): return lax.ppermute(x, NODE_AXES + ('sub',), pairs)  3.06 us
    pallas_call x1, Pallas kernels, on_device(): pl.pallas_call(functools.partial(source_kernel, nodes), out_shape=(jax.Sh...  1.51 us
    pallas_call x1, Pallas kernels, on_device(): pl.pallas_call(top_kernel, out_shape=(jax.ShapeDtypeStruct((nodes * rank,...  1.18 us
    pallas_call x1, Pallas kernels, on_device(): pl.pallas_call(near_kernel, out_shape=jax.ShapeDtypeStruct((leaf_dev, vec...  1.02 us
    pallas_call x1, Pallas kernels, on_device(): pl.pallas_call(final_kernel, out_shape=jax.ShapeDtypeStruct((leaf_dev, ve...  1.01 us
  transfers between devices with their start and end apart: 7, of which 4 were waited for; matrix products, arithmetic and copies ran while one was open for 0% of the time, Pallas kernels for 14%

profile of v5, /device:TPU:0, one launch (start us, length us, event | category | flops | bytes accessed | tf_op | source)
XLA Modules:
  0.0 15.7 jit_solution(13911662626823323949)
XLA Ops:
  0.0 1.5 %source.1 = (bf16[144,128]{1,0:T(8,128)(2,1)S(1)}, f32[144,128]{1,0:T(8,128)S(1)}, bf16[4,16,256]{2,1,0:T(8,128)(2,1)S(1)}, bf16[1,64,1024]{2,1,0:T(8,128)(2,1)S...) custom-call(s32[4,8]{1,0:T(4,128)} %refs_0_.1, bf16[4,16,256]{2,1,0:T(8,128)(2,1)} %refs_1_.1, ...), custom_call_target="tpu_custom_call" | custom-call | tf_op jit(solution)/shard_map/source/pallas_call | solution.py:175
  1.5 0.5 %collective-permute-start = (f32[144,128]{1,0:T(8,128)S(1)}, f32[144,128]{1,0:T(8,128)S(1)}, u32[]{:S(2)}, u32[]{:S(2)}) collective-permute-start(f32[144,128]{1,0:T(8,128)S(1)} %get-tuple-element.18), channel_id=1, source_target_pairs={{0,1},{1,0},{2,3},{3,2},{4,5},{5,4},{6,7},{7,6},{8,9},{9,8},{10,11... | collective-permute-start | bytes 221192 | tf_op jit(solution)/shard_map/ppermute | solution.py:167
  2.0 2.6 %collective-permute-start.1 = (bf16[144,128]{1,0:T(8,128)(2,1)S(1)}, bf16[144,128]{1,0:T(8,128)(2,1)S(1)}, u32[]{:S(2)}, u32[]{:S(2)}) collective-permute-start(bf16[144,128]{1,0:T(8,128)(2,1)S(1)} %get-tuple-element.20), channel_id=1, source_target_pairs={{0,3},{1,2},{2,1},{3,0},{4,7},{5,6},{6,5},{7,4},{8,11},{9,10},{10,... | collective-permute-start | bytes 110600 | tf_op jit(solution)/shard_map/ppermute | solution.py:167
  4.7 0.0 collective-permute-start.5
  4.7 1.2 %top.1 = (bf16[512,256]{1,0:T(8,128)(2,1)S(1)}, bf16[2,768,256]{2,1,0:T(8,128)(2,1)S(1)}, bf16[4,64,256]{2,1,0:T(8,128)(2,1)S(1)}) custom-call(s32[1,16]{1,0:T(1,128)} %src_hbm.2, bf16[1,64,1024]{2,1,0:T(8,128)(2,1)S(1)} %get-tuple-element.21.top_ref, bf16[1,64,256]{2,1,0:T(8,128)(2,1)S(1)} %get-tuple-element.22.down_ref, bf16[4,768,256]{2,1,0:T(8,128)(2,1)} %tiles_hbm.1, ...), custom_call_target="tpu_custom_call" | custom-call | tf_op jit(solution)/shard_map/top/pallas_call | solution.py:199
  5.9 0.5 %collective-permute-done.1 = bf16[144,128]{1,0:T(8,128)(2,1)S(1)} collective-permute-done((bf16[144,128]{1,0:T(8,128)(2,1)S(1)}, bf16[144,128]{1,0:T(8,128)(2,1)S(1)}, u32[]{:S(2)}, u32[]{:S(2)}) %collective-permute-start.1) | collective-permute-done | bytes 36896 | tf_op jit(solution)/shard_map/ppermute | solution.py:167
  6.4 0.0 collective-permute-done
  6.5 1.7 %collective-permute-start.2 = (bf16[80,128]{1,0:T(8,128)(2,1)S(1)}, bf16[80,128]{1,0:T(8,128)(2,1)S(1)}, u32[]{:S(2)}, u32[]{:S(2)}) collective-permute-start(bf16[80,128]{1,0:T(8,128)(2,1)S(1)} %pad_maximum_fusion.1), channel_id=1, source_target_pairs={{0,4},{1,5},{2,6},{3,7},{4,0},{5,1},{6,2},{7,3},{8,12},{9,13},{10,... | collective-permute-start | bytes 61448 | tf_op jit(solution)/shard_map/ppermute | solution.py:167
  8.2 0.4 %collective-permute-done.5.a_ref = bf16[4,16,256]{2,1,0:T(8,128)(2,1)S(1)} collective-permute-done((bf16[4,16,256]{2,1,0:T(8,128)(2,1)S(1)}, bf16[4,16,256]{2,1,0:T(8,128)(2,1)S(1)}, u32[]{:S(2)}, u32[]{:S(2)}) %collective-permute-start.5) | collective-permute-done | bytes 32800 | tf_op jit(solution)/shard_map/ppermute | solution.py:167
  8.6 0.0 collective-permute-start.6
  8.6 1.7 %collective-permute-done.2 = bf16[80,128]{1,0:T(8,128)(2,1)S(1)} collective-permute-done((bf16[80,128]{1,0:T(8,128)(2,1)S(1)}, bf16[80,128]{1,0:T(8,128)(2,1)S(1)}, u32[]{:S(2)}, u32[]{:S(2)}) %collective-permute-start.2) | collective-permute-done | bytes 20512 | tf_op jit(solution)/shard_map/ppermute | solution.py:167
  10.4 0.1 collective-permute-start.4
  10.5 2.8 %collective-permute-start.3 = (bf16[64,128]{1,0:T(8,128)(2,1)S(1)}, bf16[64,128]{1,0:T(8,128)(2,1)S(1)}, u32[]{:S(2)}, u32[]{:S(2)}) collective-permute-start(bf16[64,128]{1,0:T(8,128)(2,1)S(1)} %pad_maximum_fusion.2), channel_id=1, source_target_pairs={{0,9},{1,8},{2,11},{3,10},{4,13},{5,12},{6,15},{7,14},{8,1},{9,0},... | collective-permute-start | bytes 49160 | tf_op jit(solution)/shard_map/ppermute | solution.py:167
  13.2 0.0 collective-permute-done.6.b_ref
  13.2 1.0 %near.1.near_ref = f32[4,16,256]{2,1,0:T(8,128)S(1)} custom-call(s32[4,3]{1,0:T(4,128)} %src_hbm.3, bf16[4,16,256]{2,1,0:T(8,128)(2,1)S(1)} %get-tuple-element.28.adj_ref, bf16[4,16,256]{2,1,0:T(8,128)(2,1)S(1)} %collective-permute-done.5.a_ref, bf16[4,16,256]{2,1,0:T(8,128)(2,1)S(1)} %collective-permute-done.6.b_ref, ...), custom_call_target="tpu_custom_call" | custom-call | tf_op jit(solution)/shard_map/near/pallas_call | solution.py:244
  14.3 0.4 %collective-permute-done.3.got_ref = bf16[64,128]{1,0:T(8,128)(2,1)S(1)} collective-permute-done((bf16[64,128]{1,0:T(8,128)(2,1)S(1)}, bf16[64,128]{1,0:T(8,128)(2,1)S(1)}, u32[]{:S(2)}, u32[]{:S(2)}) %collective-permute-start.3) | collective-permute-done | bytes 16416 | tf_op jit(solution)/shard_map/ppermute | solution.py:167
  14.7 0.0 collective-permute-done.4.kept_ref
  14.7 1.0 %final.1 = f32[4,16,256]{2,1,0:T(8,128)} custom-call(bf16[64,128]{1,0:T(8,128)(2,1)S(1)} %collective-permute-done.3.got_ref, f32[64,128]{1,0:T(8,128)S(1)} %collective-permute-done.4.kept_ref, bf16[512,256]{1,0:T(8,128)(2,1)S(1)} %get-tuple-element.23.matrix_ref, bf16[4,64,256]{2,1,0:T(8,128)(2,1)S(1)} %get-tuple-element.25.in_ref, ...), custom_call_target="tpu_custom_call" | custom-call | tf_op jit(solution)/shard_map/final/pallas_call | solution.py:258
  (11 shorter events, 0.1 us)
Async XLA Ops:
  1.5 4.9 %collective-permute-start = (f32[144,128]{1,0:T(8,128)S(1)}, f32[144,128]{1,0:T(8,128)S(1)}, u32[]{:S(2)}, u32[]{:S(2)}) collective-permute-start(f32[144,128]{1,0:T(8,128)S(1)} %get-tuple-element.18), channel_id=1, source_target_pairs={{0,1},{1,0},{2,3},{3,2},{4,5},{5,4},{6,7},{7,6},{8,9},{9,8},{10,11... | collective-permute-start | bytes 221192 | tf_op jit(solution)/shard_map/ppermute | solution.py:167
  2.0 4.4 %collective-permute-start.1 = (bf16[144,128]{1,0:T(8,128)(2,1)S(1)}, bf16[144,128]{1,0:T(8,128)(2,1)S(1)}, u32[]{:S(2)}, u32[]{:S(2)}) collective-permute-start(bf16[144,128]{1,0:T(8,128)(2,1)S(1)} %get-tuple-element.20), channel_id=1, source_target_pairs={{0,3},{1,2},{2,1},{3,0},{4,7},{5,6},{6,5},{7,4},{8,11},{9,10},{10,... | collective-permute-start | bytes 110600 | tf_op jit(solution)/shard_map/ppermute | solution.py:167
  4.7 3.9 %collective-permute-start.5 = (bf16[4,16,256]{2,1,0:T(8,128)(2,1)S(1)}, bf16[4,16,256]{2,1,0:T(8,128)(2,1)S(1)}, u32[]{:S(2)}, u32[]{:S(2)}) collective-permute-start(bf16[4,16,256]{2,1,0:T(8,128)(2,1)S(1)} %get-tuple-element.28.adj_ref), channel_id=1, source_target_pairs={{0,2},{1,3},{2,0},{3,1},{4,6},{5,7},{6,4},{7,5},{8,10},{9,11},{10,... | collective-permute-start | bytes 98312 | tf_op jit(solution)/shard_map/ppermute | solution.py:167
  6.5 3.8 %collective-permute-start.2 = (bf16[80,128]{1,0:T(8,128)(2,1)S(1)}, bf16[80,128]{1,0:T(8,128)(2,1)S(1)}, u32[]{:S(2)}, u32[]{:S(2)}) collective-permute-start(bf16[80,128]{1,0:T(8,128)(2,1)S(1)} %pad_maximum_fusion.1), channel_id=1, source_target_pairs={{0,4},{1,5},{2,6},{3,7},{4,0},{5,1},{6,2},{7,3},{8,12},{9,13},{10,... | collective-permute-start | bytes 61448 | tf_op jit(solution)/shard_map/ppermute | solution.py:167
  8.6 4.7 %collective-permute-start.6 = (bf16[4,16,256]{2,1,0:T(8,128)(2,1)S(1)}, bf16[4,16,256]{2,1,0:T(8,128)(2,1)S(1)}, u32[]{:S(2)}, u32[]{:S(2)}) collective-permute-start(bf16[4,16,256]{2,1,0:T(8,128)(2,1)S(1)} %get-tuple-element.28.adj_ref), channel_id=1, source_target_pairs={{2,4},{3,5},{4,2},{5,3},{6,8},{7,9},{8,6},{9,7},{10,12},{11,13},{1... | collective-permute-start | bytes 98312 | tf_op jit(solution)/shard_map/ppermute | solution.py:222
  10.4 4.3 %collective-permute-start.4 = (f32[64,128]{1,0:T(8,128)S(1)}, f32[64,128]{1,0:T(8,128)S(1)}, u32[]{:S(2)}, u32[]{:S(2)}) collective-permute-start(f32[64,128]{1,0:T(8,128)S(1)} %pad_maximum_fusion), channel_id=1, source_target_pairs={{0,1},{1,0},{2,3},{3,2},{4,5},{5,4},{6,7},{7,6},{8,9},{9,8},{10,11... | collective-permute-start | bytes 98312 | tf_op jit(solution)/shard_map/ppermute | solution.py:167
  10.5 4.2 %collective-permute-start.3 = (bf16[64,128]{1,0:T(8,128)(2,1)S(1)}, bf16[64,128]{1,0:T(8,128)(2,1)S(1)}, u32[]{:S(2)}, u32[]{:S(2)}) collective-permute-start(bf16[64,128]{1,0:T(8,128)(2,1)S(1)} %pad_maximum_fusion.2), channel_id=1, source_target_pairs={{0,9},{1,8},{2,11},{3,10},{4,13},{5,12},{6,15},{7,14},{8,1},{9,0},... | collective-permute-start | bytes 49160 | tf_op jit(solution)/shard_map/ppermute | solution.py:167

commit v6 on v5

--- a/solution.py
+++ b/solution.py
@@ -113,40 +113,51 @@
         copy.wait()
 
 
-def near_kernel(src_hbm, adj_ref, a_ref, b_ref, tiles_ref, more_tiles_ref, near_ref, src_ref, around, sem):
+def fold_kernel(matrix_ref, in_ref, folded_ref):
+    leaf_dev, rank, cells = in_ref.shape
+    known = matrix_ref.shape[0] - folded_ref.shape[0]
+    for j in range(leaf_dev):
+        block = matrix_ref[known:, j * rank : (j + 1) * rank]
+        folded_ref[:, j * cells : (j + 1) * cells] = jnp.dot(block, in_ref[j], preferred_element_type=F32).astype(BF16)
+
+
+def near_kernel(src_hbm, adj_ref, a_ref, b_ref, tiles_ref, more_tiles_ref, kept_ref, matrix_ref, in_ref, base_ref, src_ref, around, sem):
     copy = pltpu.make_async_copy(src_hbm, src_ref, sem.at[0])
     copy.start()
     leaf_dev, vectors, cells = adj_ref.shape
+    rank = in_ref.shape[1]
+    rows = leaf_dev // 2 * vectors
+    first = tiles_ref.shape[0]
     me = lax.axis_index(NODE_AXES)
-    first = tiles_ref.shape[0]
     around[:leaf_dev] = adj_ref[...]
     around[leaf_dev : 2 * leaf_dev] = a_ref[...]
     around[2 * leaf_dev :] = b_ref[...]
+    coefs = side_by_side(kept_ref[rows:].astype(BF16), vectors)
+    down = jnp.dot(coefs, matrix_ref[: coefs.shape[1]], preferred_element_type=F32)
+    mixed = (side_by_side(kept_ref[:rows], vectors) + down).astype(BF16)
     copy.wait()
     for j in range(leaf_dev):
-        total = None
+        total = jnp.dot(mixed[:, j * rank : (j + 1) * rank], in_ref[j], preferred_element_type=F32)
         for k in range(src_ref.shape[1]):
             source = src_ref[j, k]
             node = source // leaf_dev
             base = jnp.where(node == me, 0, jnp.where(node == (me ^ 1), leaf_dev, 2 * leaf_dev))
             block = around[base + source % leaf_dev]
             tiles, at = (tiles_ref, j) if j < first else (more_tiles_ref, j - first)
-            part = jnp.dot(block, tiles[at, k * cells : (k + 1) * cells], preferred_element_type=F32)
-            total = part if total is None else total + part
-        near_ref[j] = total
-
-
-def final_kernel(got_ref, kept_ref, matrix_ref, in_ref, near_ref, out_ref):
-    leaf_dev, vectors, _ = near_ref.shape
+            total += jnp.dot(block, tiles[at, k * cells : (k + 1) * cells], preferred_element_type=F32)
+        base_ref[j] = total
+
+
+def final_kernel(got_ref, folded_ref, in_ref, base_ref, out_ref):
+    leaf_dev, vectors, cells = base_ref.shape
     rank = in_ref.shape[1]
     rows = leaf_dev // 2 * vectors
-    coefs = [side_by_side(kept_ref[rows:].astype(BF16), vectors), side_by_side(got_ref[rows:], vectors)]
-    down = jnp.dot(jnp.concatenate(coefs, axis=1), matrix_ref[...], preferred_element_type=F32)
-    leaf_in = side_by_side(kept_ref[:rows] + got_ref[:rows].astype(F32), vectors)
-    mixed = (leaf_in + down).astype(BF16)
-    for j in range(leaf_dev):
+    coefs = side_by_side(got_ref[rows:], vectors)
+    mixed = side_by_side(got_ref[:rows], vectors)
+    for j in range(leaf_dev):
+        top = jnp.dot(coefs, folded_ref[:, j * cells : (j + 1) * cells], preferred_element_type=F32)
         far = jnp.dot(mixed[:, j * rank : (j + 1) * rank], in_ref[j], preferred_element_type=F32)
-        out_ref[j] = near_ref[j] + far
+        out_ref[j] = base_ref[j] + (top + far)
 
 
 def on_device(
@@ -214,12 +225,21 @@
         name="top",
     )(in_hbm(top_src), top, down, in_hbm(near_tiles), in_hbm(leaf_basis_in))
 
+    folded = pl.pallas_call(
+        fold_kernel,
+        out_shape=jax.ShapeDtypeStruct((nodes // 2 * rank, leaf_dev * cells), BF16),
+        in_specs=[VMEM] * 2,
+        out_specs=VMEM,
+        compiler_params=PARAMS,
+        name="fold",
+    )(matrix, basis_in)
+
     inner = [(i, i + 1 if i % 2 else i - 1) for i in range(1, nodes - 1)]
     other = [(i * cores + c, j * cores + c) for i, j in inner for c in range(cores)]
     other += [(i * cores + c, i * cores + (c + 1) % cores) for i in (0, nodes - 1) for c in range(cores)]
     send, _ = lax.optimization_barrier((send, keep))
     a = swapped(lax.optimization_barrier((adjoint_v, send, keep))[0], lambda i: i ^ 1, False)
-    b = lax.ppermute(lax.optimization_barrier((adjoint_v, a))[0], NODE_AXES + ("sub",), other)
+    b = lax.ppermute(lax.optimization_barrier((adjoint_v, a, folded))[0], NODE_AXES + ("sub",), other)
 
     coefs = None
     for step in range(steps):
@@ -241,10 +261,10 @@
         if step < steps - 1:
             keep = keep[:half] + got[:half].astype(F32)
 
-    near = pl.pallas_call(
+    base = pl.pallas_call(
         near_kernel,
         out_shape=jax.ShapeDtypeStruct((leaf_dev, vectors, cells), F32),
-        in_specs=[HBM] + [VMEM] * 5,
+        in_specs=[HBM] + [VMEM] * 8,
         out_specs=VMEM,
         scratch_shapes=[
             pltpu.SMEM(near_src.shape, jnp.int32),
@@ -253,16 +273,16 @@
         ],
         compiler_params=PARAMS,
         name="near",
-    )(in_hbm(near_src), adjoint_v, a, b, tiles, more_tiles)
+    )(in_hbm(near_src), adjoint_v, a, b, tiles, more_tiles, keep, matrix, basis_in)
 
     return pl.pallas_call(
         final_kernel,
         out_shape=jax.ShapeDtypeStruct((leaf_dev, vectors, cells), F32),
-        in_specs=[VMEM] * 5,
+        in_specs=[VMEM] * 4,
         out_specs=VMEM,
         compiler_params=PARAMS,
         name="final",
-    )(got, keep, matrix, basis_in, near)
+    )(got, folded, basis_in, base)
 
 
 def solution(mesh):

time: 15.9 us -> 15.8 us (level)
  waiting for transfers between devices: 3.06 us -> 2.51 us
  Pallas kernels: 4.72 us -> 4.96 us
  starting transfers between devices: 7.75 us -> 7.94 us
    ppermute x6, waiting for transfers between devices: 3.06 us -> 2.51 us  [swapped(): return lax.ppermute(x, NODE_AXES + ('sub',), pairs)]
    pallas_call x0 -> x1, Pallas kernels: none -> 0.32 us  [on_device(): pl.pallas_call(fold_kernel, out_shape=jax.ShapeDtypeStruct((nodes // 2 *...]
    ppermute x1, starting transfers between devices: 0.01 us -> 0.19 us  [on_device(): lax.ppermute(lax.optimization_barrier((adjoint_v, a, folded))[0], NODE_AX...]
  transfers between devices with their start and end apart: 7 -> 7, of which waited for: 4 -> 4; matrix products, arithmetic and copies ran while one was open for 0% -> 0% of each run, Pallas kernels for 14% -> 16%
where the time goes in v6:
time: 15.8 us; the launch traced here: 15.6 us
  starting transfers between devices  7.94 us (50%)
  Pallas kernels  4.96 us (31%)
  waiting for transfers between devices  2.51 us (16%)
    ppermute x6, starting transfers between devices, swapped(): return lax.ppermute(x, NODE_AXES + ('sub',), pairs)  7.75 us
    ppermute x6, waiting for transfers between devices, swapped(): return lax.ppermute(x, NODE_AXES + ('sub',), pairs)  2.51 us
    pallas_call x1, Pallas kernels, on_device(): pl.pallas_call(functools.partial(source_kernel, nodes), out_shape=(jax.Sh...  1.51 us
    pallas_call x1, Pallas kernels, on_device(): pl.pallas_call(top_kernel, out_shape=(jax.ShapeDtypeStruct((nodes * rank,...  1.18 us
    pallas_call x1, Pallas kernels, on_device(): pl.pallas_call(near_kernel, out_shape=jax.ShapeDtypeStruct((leaf_dev, vec...  1.06 us
    pallas_call x1, Pallas kernels, on_device(): pl.pallas_call(final_kernel, out_shape=jax.ShapeDtypeStruct((leaf_dev, ve...  0.89 us
    pallas_call x1, Pallas kernels, on_device(): pl.pallas_call(fold_kernel, out_shape=jax.ShapeDtypeStruct((nodes // 2 *...  0.32 us
  transfers between devices with their start and end apart: 7, of which 4 were waited for; matrix products, arithmetic and copies ran while one was open for 0% of the time, Pallas kernels for 16%

profile of v6, /device:TPU:0, one launch (start us, length us, event | category | flops | bytes accessed | tf_op | source)
XLA Modules:
  0.0 15.6 jit_solution(17644558776648240008)
XLA Ops:
  0.0 1.5 %source.1 = (bf16[144,128]{1,0:T(8,128)(2,1)S(1)}, f32[144,128]{1,0:T(8,128)S(1)}, bf16[4,16,256]{2,1,0:T(8,128)(2,1)S(1)}, bf16[1,64,1024]{2,1,0:T(8,128)(2,1)S...) custom-call(s32[4,8]{1,0:T(4,128)} %refs_0_.1, bf16[4,16,256]{2,1,0:T(8,128)(2,1)} %refs_1_.1, ...), custom_call_target="tpu_custom_call" | custom-call | tf_op jit(solution)/shard_map/source/pallas_call | solution.py:186
  1.5 0.5 %collective-permute-start = (f32[144,128]{1,0:T(8,128)S(1)}, f32[144,128]{1,0:T(8,128)S(1)}, u32[]{:S(2)}, u32[]{:S(2)}) collective-permute-start(f32[144,128]{1,0:T(8,128)S(1)} %get-tuple-element.18), channel_id=1, source_target_pairs={{0,1},{1,0},{2,3},{3,2},{4,5},{5,4},{6,7},{7,6},{8,9},{9,8},{10,11... | collective-permute-start | bytes 221192 | tf_op jit(solution)/shard_map/ppermute | solution.py:178
  2.0 2.6 %collective-permute-start.1 = (bf16[144,128]{1,0:T(8,128)(2,1)S(1)}, bf16[144,128]{1,0:T(8,128)(2,1)S(1)}, u32[]{:S(2)}, u32[]{:S(2)}) collective-permute-start(bf16[144,128]{1,0:T(8,128)(2,1)S(1)} %get-tuple-element.20), channel_id=1, source_target_pairs={{0,3},{1,2},{2,1},{3,0},{4,7},{5,6},{6,5},{7,4},{8,11},{9,10},{10,... | collective-permute-start | bytes 110600 | tf_op jit(solution)/shard_map/ppermute | solution.py:178
  4.7 0.0 collective-permute-start.4
  4.7 1.2 %top.1 = (bf16[512,256]{1,0:T(8,128)(2,1)S(1)}, bf16[2,768,256]{2,1,0:T(8,128)(2,1)S(1)}, bf16[4,64,256]{2,1,0:T(8,128)(2,1)S(1)}) custom-call(s32[1,16]{1,0:T(1,128)} %src_hbm.2, bf16[1,64,1024]{2,1,0:T(8,128)(2,1)S(1)} %get-tuple-element.21.top_ref, bf16[1,64,256]{2,1,0:T(8,128)(2,1)S(1)} %get-tuple-element.22.down_ref, bf16[4,768,256]{2,1,0:T(8,128)(2,1)} %tiles_hbm.1, ...), custom_call_target="tpu_custom_call" | custom-call | tf_op jit(solution)/shard_map/top/pallas_call | solution.py:210
  5.9 0.5 %collective-permute-done.1 = bf16[144,128]{1,0:T(8,128)(2,1)S(1)} collective-permute-done((bf16[144,128]{1,0:T(8,128)(2,1)S(1)}, bf16[144,128]{1,0:T(8,128)(2,1)S(1)}, u32[]{:S(2)}, u32[]{:S(2)}) %collective-permute-start.1) | collective-permute-done | bytes 36896 | tf_op jit(solution)/shard_map/ppermute | solution.py:178
  6.4 0.0 collective-permute-done
  6.5 1.7 %collective-permute-start.2 = (bf16[80,128]{1,0:T(8,128)(2,1)S(1)}, bf16[80,128]{1,0:T(8,128)(2,1)S(1)}, u32[]{:S(2)}, u32[]{:S(2)}) collective-permute-start(bf16[80,128]{1,0:T(8,128)(2,1)S(1)} %pad_maximum_fusion.1), channel_id=1, source_target_pairs={{0,4},{1,5},{2,6},{3,7},{4,0},{5,1},{6,2},{7,3},{8,12},{9,13},{10,... | collective-permute-start | bytes 61448 | tf_op jit(solution)/shard_map/ppermute | solution.py:178
  8.2 0.3 %fold.1.folded_ref = bf16[256,1024]{1,0:T(8,128)(2,1)S(1)} custom-call(bf16[512,256]{1,0:T(8,128)(2,1)S(1)} %get-tuple-element.23.matrix_ref, bf16[4,64,256]{2,1,0:T(8,128)(2,1)S(1)} %get-tuple-element.25.in_ref), custom_call_target="tpu_custom_call" | custom-call | tf_op jit(solution)/shard_map/fold/pallas_call | solution.py:228
  8.5 0.1 collective-permute-done.4.a_ref
  8.6 0.2 %collective-permute-start.5 = (bf16[4,16,256]{2,1,0:T(8,128)(2,1)S(1)}, bf16[4,16,256]{2,1,0:T(8,128)(2,1)S(1)}, u32[]{:S(2)}, u32[]{:S(2)}) collective-permute-start(bf16[4,16,256]{2,1,0:T(8,128)(2,1)S(1)} %get-tuple-element.28.adj_ref), channel_id=1, source_target_pairs={{2,4},{3,5},{4,2},{5,3},{6,8},{7,9},{8,6},{9,7},{10,12},{11,13},{1... | collective-permute-start | bytes 98312 | tf_op jit(solution)/shard_map/ppermute | solution.py:242
  8.8 1.6 %collective-permute-done.2 = bf16[80,128]{1,0:T(8,128)(2,1)S(1)} collective-permute-done((bf16[80,128]{1,0:T(8,128)(2,1)S(1)}, bf16[80,128]{1,0:T(8,128)(2,1)S(1)}, u32[]{:S(2)}, u32[]{:S(2)}) %collective-permute-start.2) | collective-permute-done | bytes 20512 | tf_op jit(solution)/shard_map/ppermute | solution.py:178
  10.4 0.1 collective-permute-start.6
  10.5 2.8 %collective-permute-start.3 = (bf16[64,128]{1,0:T(8,128)(2,1)S(1)}, bf16[64,128]{1,0:T(8,128)(2,1)S(1)}, u32[]{:S(2)}, u32[]{:S(2)}) collective-permute-start(bf16[64,128]{1,0:T(8,128)(2,1)S(1)} %pad_maximum_fusion.2), channel_id=1, source_target_pairs={{0,9},{1,8},{2,11},{3,10},{4,13},{5,12},{6,15},{7,14},{8,1},{9,0},... | collective-permute-start | bytes 49160 | tf_op jit(solution)/shard_map/ppermute | solution.py:178
  13.2 0.0 collective-permute-done.5.b_ref
  13.2 0.0 collective-permute-done.6.kept_ref
  13.2 1.1 %near.1.base_ref = f32[4,16,256]{2,1,0:T(8,128)S(1)} custom-call(s32[4,3]{1,0:T(4,128)} %src_hbm.3, bf16[4,16,256]{2,1,0:T(8,128)(2,1)S(1)} %get-tuple-element.28.adj_ref, bf16[4,16,256]{2,1,0:T(8,128)(2,1)S(1)} %collective-permute-done.4.a_ref, bf16[4,16,256]{2,1,0:T(8,128)(2,1)S(1)} %collective-permute-done.5.b_ref, ...), custom_call_target="tpu_custom_call" | custom-call | tf_op jit(solution)/shard_map/near/pallas_call | solution.py:264
  14.3 0.4 %collective-permute-done.3.got_ref = bf16[64,128]{1,0:T(8,128)(2,1)S(1)} collective-permute-done((bf16[64,128]{1,0:T(8,128)(2,1)S(1)}, bf16[64,128]{1,0:T(8,128)(2,1)S(1)}, u32[]{:S(2)}, u32[]{:S(2)}) %collective-permute-start.3) | collective-permute-done | bytes 16416 | tf_op jit(solution)/shard_map/ppermute | solution.py:178
  14.7 0.9 %final.1 = f32[4,16,256]{2,1,0:T(8,128)} custom-call(bf16[64,128]{1,0:T(8,128)(2,1)S(1)} %collective-permute-done.3.got_ref, bf16[256,1024]{1,0:T(8,128)(2,1)S(1)} %fold.1.folded_ref, bf16[4,64,256]{2,1,0:T(8,128)(2,1)S(1)} %get-tuple-element.25.in_ref, f32[4,16,256]{2,1,0:T(8,128)S(1)} %near.1.base_ref), custom_call_target="tpu_custom_call" | custom-call | tf_op jit(solution)/shard_map/final/pallas_call | solution.py:278
  (11 shorter events, 0.1 us)
Async XLA Ops:
  1.5 4.9 %collective-permute-start = (f32[144,128]{1,0:T(8,128)S(1)}, f32[144,128]{1,0:T(8,128)S(1)}, u32[]{:S(2)}, u32[]{:S(2)}) collective-permute-start(f32[144,128]{1,0:T(8,128)S(1)} %get-tuple-element.18), channel_id=1, source_target_pairs={{0,1},{1,0},{2,3},{3,2},{4,5},{5,4},{6,7},{7,6},{8,9},{9,8},{10,11... | collective-permute-start | bytes 221192 | tf_op jit(solution)/shard_map/ppermute | solution.py:178
  2.0 4.4 %collective-permute-start.1 = (bf16[144,128]{1,0:T(8,128)(2,1)S(1)}, bf16[144,128]{1,0:T(8,128)(2,1)S(1)}, u32[]{:S(2)}, u32[]{:S(2)}) collective-permute-start(bf16[144,128]{1,0:T(8,128)(2,1)S(1)} %get-tuple-element.20), channel_id=1, source_target_pairs={{0,3},{1,2},{2,1},{3,0},{4,7},{5,6},{6,5},{7,4},{8,11},{9,10},{10,... | collective-permute-start | bytes 110600 | tf_op jit(solution)/shard_map/ppermute | solution.py:178
  4.7 3.9 %collective-permute-start.4 = (bf16[4,16,256]{2,1,0:T(8,128)(2,1)S(1)}, bf16[4,16,256]{2,1,0:T(8,128)(2,1)S(1)}, u32[]{:S(2)}, u32[]{:S(2)}) collective-permute-start(bf16[4,16,256]{2,1,0:T(8,128)(2,1)S(1)} %get-tuple-element.28.adj_ref), channel_id=1, source_target_pairs={{0,2},{1,3},{2,0},{3,1},{4,6},{5,7},{6,4},{7,5},{8,10},{9,11},{10,... | collective-permute-start | bytes 98312 | tf_op jit(solution)/shard_map/ppermute | solution.py:178
  6.5 3.8 %collective-permute-start.2 = (bf16[80,128]{1,0:T(8,128)(2,1)S(1)}, bf16[80,128]{1,0:T(8,128)(2,1)S(1)}, u32[]{:S(2)}, u32[]{:S(2)}) collective-permute-start(bf16[80,128]{1,0:T(8,128)(2,1)S(1)} %pad_maximum_fusion.1), channel_id=1, source_target_pairs={{0,4},{1,5},{2,6},{3,7},{4,0},{5,1},{6,2},{7,3},{8,12},{9,13},{10,... | collective-permute-start | bytes 61448 | tf_op jit(solution)/shard_map/ppermute | solution.py:178
  8.6 4.7 %collective-permute-start.5 = (bf16[4,16,256]{2,1,0:T(8,128)(2,1)S(1)}, bf16[4,16,256]{2,1,0:T(8,128)(2,1)S(1)}, u32[]{:S(2)}, u32[]{:S(2)}) collective-permute-start(bf16[4,16,256]{2,1,0:T(8,128)(2,1)S(1)} %get-tuple-element.28.adj_ref), channel_id=1, source_target_pairs={{2,4},{3,5},{4,2},{5,3},{6,8},{7,9},{8,6},{9,7},{10,12},{11,13},{1... | collective-permute-start | bytes 98312 | tf_op jit(solution)/shard_map/ppermute | solution.py:242
  10.4 2.9 %collective-permute-start.6 = (f32[64,128]{1,0:T(8,128)S(1)}, f32[64,128]{1,0:T(8,128)S(1)}, u32[]{:S(2)}, u32[]{:S(2)}) collective-permute-start(f32[64,128]{1,0:T(8,128)S(1)} %pad_maximum_fusion), channel_id=1, source_target_pairs={{0,1},{1,0},{2,3},{3,2},{4,5},{5,4},{6,7},{7,6},{8,9},{9,8},{10,11... | collective-permute-start | bytes 98312 | tf_op jit(solution)/shard_map/ppermute | solution.py:178
  10.5 4.2 %collective-permute-start.3 = (bf16[64,128]{1,0:T(8,128)(2,1)S(1)}, bf16[64,128]{1,0:T(8,128)(2,1)S(1)}, u32[]{:S(2)}, u32[]{:S(2)}) collective-permute-start(bf16[64,128]{1,0:T(8,128)(2,1)S(1)} %pad_maximum_fusion.2), channel_id=1, source_target_pairs={{0,9},{1,8},{2,11},{3,10},{4,13},{5,12},{6,15},{7,14},{8,1},{9,0},... | collective-permute-start | bytes 49160 | tf_op jit(solution)/shard_map/ppermute | solution.py:178

commit v7 on v6

--- a/solution.py
+++ b/solution.py
@@ -66,10 +66,6 @@
     ]
     for copy in copies[3:5]:
         copy.wait()
-    node = lax.dot_general(jnp.concatenate(coefs, axis=1), up_ref[0], NT, preferred_element_type=F32).astype(BF16)
-    node = jnp.concatenate([node, node], axis=1)
-    send_ref[nodes // 2 * rows :] = node
-    keep_ref[nodes // 2 * rows :] = node.astype(F32)
     for j in range(leaf_dev):
         contrib = jnp.dot(coefs[j], far_ref[j], preferred_element_type=F32)
         for k in range(far_count):
@@ -78,6 +74,10 @@
             place = ((target >> within) ^ me) * pairs + ((target & (leaf_dev - 1)) >> 1)
             place += ((target ^ k) & 1) * (nodes * pairs)
             sums[j][place] += jnp.where(half == k % 2, block, 0.0)
+    node = lax.dot_general(jnp.concatenate(coefs, axis=1), up_ref[0], NT, preferred_element_type=F32).astype(BF16)
+    node = jnp.concatenate([node, node], axis=1)
+    send_ref[nodes // 2 * rows :] = node
+    keep_ref[nodes // 2 * rows :] = node.astype(F32)
     width = bits_of(nodes)
     for r in range(nodes):
         for p in range(pairs):
@@ -94,7 +94,7 @@
         copy.wait()
 
 
-def top_kernel(src_hbm, top_ref, down_ref, tiles_hbm, in_hbm_ref, matrix_ref, tiles_ref, in_ref, src_ref, by_node, sems):
+def top_kernel(src_hbm, top_ref, down_ref, tiles_hbm, in_hbm_ref, matrix_ref, rest_ref, tiles_ref, in_ref, src_ref, by_node, sems):
     sources = (src_hbm, tiles_hbm.at[tiles_hbm.shape[0] - tiles_ref.shape[0] :], in_hbm_ref)
     copies = [
         pltpu.make_async_copy(there, here, sems.at[i]) for i, (there, here) in enumerate(zip(sources, (src_ref, tiles_ref, in_ref)))
@@ -108,20 +108,24 @@
     copies[0].wait()
     for k in range(src_ref.shape[1]):
         by_node[src_ref[0, k] ^ me] += through[k * rank : (k + 1) * rank]
-    matrix_ref[...] = by_node[...].reshape(matrix_ref.shape).astype(BF16)
+    matrix = by_node[...].reshape(matrix_ref.shape)
+    rounded = matrix.astype(BF16)
+    matrix_ref[...] = rounded
+    rest_ref[...] = (matrix - rounded.astype(F32)).astype(BF16)
     for copy in copies[1:]:
         copy.wait()
 
 
-def fold_kernel(matrix_ref, in_ref, folded_ref):
+def fold_kernel(matrix_ref, rest_ref, in_ref, folded_ref):
     leaf_dev, rank, cells = in_ref.shape
     known = matrix_ref.shape[0] - folded_ref.shape[0]
     for j in range(leaf_dev):
-        block = matrix_ref[known:, j * rank : (j + 1) * rank]
-        folded_ref[:, j * cells : (j + 1) * cells] = jnp.dot(block, in_ref[j], preferred_element_type=F32).astype(BF16)
-
-
-def near_kernel(src_hbm, adj_ref, a_ref, b_ref, tiles_ref, more_tiles_ref, kept_ref, matrix_ref, in_ref, base_ref, src_ref, around, sem):
+        blocks = [ref[known:, j * rank : (j + 1) * rank] for ref in (matrix_ref, rest_ref)]
+        total = sum(jnp.dot(block, in_ref[j], preferred_element_type=F32) for block in blocks)
+        folded_ref[:, j * cells : (j + 1) * cells] = total.astype(BF16)
+
+
+def near_kernel(src_hbm, adj_ref, a_ref, b_ref, tiles_ref, more_tiles_ref, kept_ref, matrix_ref, rest_ref, in_ref, base_ref, src_ref, around, sem):
     copy = pltpu.make_async_copy(src_hbm, src_ref, sem.at[0])
     copy.start()
     leaf_dev, vectors, cells = adj_ref.shape
@@ -133,7 +137,7 @@
     around[leaf_dev : 2 * leaf_dev] = a_ref[...]
     around[2 * leaf_dev :] = b_ref[...]
     coefs = side_by_side(kept_ref[rows:].astype(BF16), vectors)
-    down = jnp.dot(coefs, matrix_ref[: coefs.shape[1]], preferred_element_type=F32)
+    down = sum(jnp.dot(coefs, ref[: coefs.shape[1]], preferred_element_type=F32) for ref in (matrix_ref, rest_ref))
     mixed = (side_by_side(kept_ref[:rows], vectors) + down).astype(BF16)
     copy.wait()
     for j in range(leaf_dev):
@@ -207,15 +211,16 @@
         name="source",
     )(*map(in_hbm, (far_dst, adjoint, leaf_basis_out, far_coupling, transfer_up, top_coupling, transfer_down, near_tiles)))
 
-    matrix, more_tiles, basis_in = pl.pallas_call(
+    matrix, rest, more_tiles, basis_in = pl.pallas_call(
         top_kernel,
         out_shape=(
+            jax.ShapeDtypeStruct((nodes * rank, leaf_dev * rank), BF16),
             jax.ShapeDtypeStruct((nodes * rank, leaf_dev * rank), BF16),
             jax.ShapeDtypeStruct(more_shape, BF16),
             like(leaf_basis_in),
         ),
         in_specs=[HBM] + [VMEM] * 2 + [HBM] * 2,
-        out_specs=(VMEM,) * 3,
+        out_specs=(VMEM,) * 4,
         scratch_shapes=[
             pltpu.SMEM(top_src.shape, jnp.int32),
             pltpu.VMEM((nodes, rank, leaf_dev * rank), F32),
@@ -228,11 +233,11 @@
     folded = pl.pallas_call(
         fold_kernel,
         out_shape=jax.ShapeDtypeStruct((nodes // 2 * rank, leaf_dev * cells), BF16),
-        in_specs=[VMEM] * 2,
+        in_specs=[VMEM] * 3,
         out_specs=VMEM,
         compiler_params=PARAMS,
         name="fold",
-    )(matrix, basis_in)
+    )(matrix, rest, basis_in)
 
     inner = [(i, i + 1 if i % 2 else i - 1) for i in range(1, nodes - 1)]
     other = [(i * cores + c, j * cores + c) for i, j in inner for c in range(cores)]
@@ -264,7 +269,7 @@
     base = pl.pallas_call(
         near_kernel,
         out_shape=jax.ShapeDtypeStruct((leaf_dev, vectors, cells), F32),
-        in_specs=[HBM] + [VMEM] * 8,
+        in_specs=[HBM] + [VMEM] * 9,
         out_specs=VMEM,
         scratch_shapes=[
             pltpu.SMEM(near_src.shape, jnp.int32),
@@ -273,7 +278,7 @@
         ],
         compiler_params=PARAMS,
         name="near",
-    )(in_hbm(near_src), adjoint_v, a, b, tiles, more_tiles, keep, matrix, basis_in)
+    )(in_hbm(near_src), adjoint_v, a, b, tiles, more_tiles, keep, matrix, rest, basis_in)
 
     return pl.pallas_call(
         final_kernel,

time: 15.8 us -> 15.7 us (level)
  waiting for transfers between devices: 2.51 us -> 2.31 us
    ppermute x6, waiting for transfers between devices: 2.51 us -> 2.31 us  [swapped(): return lax.ppermute(x, NODE_AXES + ('sub',), pairs)]
  transfers between devices with their start and end apart: 7 -> 7, of which waited for: 4 -> 3; matrix products, arithmetic and copies ran while one was open for 0% -> 0% of each run, Pallas kernels for 16% -> 17%
where the time goes in v7:
time: 15.7 us; the launch traced here: 15.5 us
  starting transfers between devices  7.98 us (51%)
  Pallas kernels  5.06 us (32%)
  waiting for transfers between devices  2.31 us (15%)
    ppermute x6, starting transfers between devices, swapped(): return lax.ppermute(x, NODE_AXES + ('sub',), pairs)  7.75 us
    ppermute x6, waiting for transfers between devices, swapped(): return lax.ppermute(x, NODE_AXES + ('sub',), pairs)  2.31 us
    pallas_call x1, Pallas kernels, on_device(): pl.pallas_call(functools.partial(source_kernel, nodes), out_shape=(jax.Sh...  1.47 us
    pallas_call x1, Pallas kernels, on_device(): pl.pallas_call(top_kernel, out_shape=(jax.ShapeDtypeStruct((nodes * rank,...  1.18 us
    pallas_call x1, Pallas kernels, on_device(): pl.pallas_call(near_kernel, out_shape=jax.ShapeDtypeStruct((leaf_dev, vec...  1.07 us
    pallas_call x1, Pallas kernels, on_device(): pl.pallas_call(final_kernel, out_shape=jax.ShapeDtypeStruct((leaf_dev, ve...  0.89 us
    pallas_call x1, Pallas kernels, on_device(): pl.pallas_call(fold_kernel, out_shape=jax.ShapeDtypeStruct((nodes // 2 *...  0.45 us
  transfers between devices with their start and end apart: 7, of which 3 were waited for; matrix products, arithmetic and copies ran while one was open for 0% of the time, Pallas kernels for 17%

profile of v7, /device:TPU:0, one launch (start us, length us, event | category | flops | bytes accessed | tf_op | source)
XLA Modules:
  0.0 15.5 jit_solution(17484128063440443283)
XLA Ops:
  0.0 1.5 %source.1 = (bf16[144,128]{1,0:T(8,128)(2,1)S(1)}, f32[144,128]{1,0:T(8,128)S(1)}, bf16[4,16,256]{2,1,0:T(8,128)(2,1)S(1)}, bf16[1,64,1024]{2,1,0:T(8,128)(2,1)S...) custom-call(s32[4,8]{1,0:T(4,128)} %refs_0_.1, bf16[4,16,256]{2,1,0:T(8,128)(2,1)} %refs_1_.1, ...), custom_call_target="tpu_custom_call" | custom-call | tf_op jit(solution)/shard_map/source/pallas_call | solution.py:190
  1.5 0.5 %collective-permute-start = (f32[144,128]{1,0:T(8,128)S(1)}, f32[144,128]{1,0:T(8,128)S(1)}, u32[]{:S(2)}, u32[]{:S(2)}) collective-permute-start(f32[144,128]{1,0:T(8,128)S(1)} %get-tuple-element.19), channel_id=1, source_target_pairs={{0,1},{1,0},{2,3},{3,2},{4,5},{5,4},{6,7},{7,6},{8,9},{9,8},{10,11... | collective-permute-start | bytes 221192 | tf_op jit(solution)/shard_map/ppermute | solution.py:182
  2.0 2.6 %collective-permute-start.1 = (bf16[144,128]{1,0:T(8,128)(2,1)S(1)}, bf16[144,128]{1,0:T(8,128)(2,1)S(1)}, u32[]{:S(2)}, u32[]{:S(2)}) collective-permute-start(bf16[144,128]{1,0:T(8,128)(2,1)S(1)} %get-tuple-element.21), channel_id=1, source_target_pairs={{0,3},{1,2},{2,1},{3,0},{4,7},{5,6},{6,5},{7,4},{8,11},{9,10},{10,... | collective-permute-start | bytes 110600 | tf_op jit(solution)/shard_map/ppermute | solution.py:182
  4.6 0.0 collective-permute-start.4
  4.7 1.2 %top.1 = (bf16[512,256]{1,0:T(8,128)(2,1)S(1)}, bf16[512,256]{1,0:T(8,128)(2,1)S(1)}, bf16[2,768,256]{2,1,0:T(8,128)(2,1)S(1)}, bf16[4,64,256]{2,1,0:T(8,128)(2,1)S(1)}) custom-call(s32[1,16]{1,0:T(1,128)} %src_hbm.2, bf16[1,64,1024]{2,1,0:T(8,128)(2,1)S(1)} %get-tuple-element.22.top_ref, bf16[1,64,256]{2,1,0:T(8,128)(2,1)S(1)} %get-tuple-element.23.down_ref, ...), custom_call_target="tpu_custom_call" | custom-call | tf_op jit(solution)/shard_map/top/pallas_call | solution.py:214
  5.8 0.5 %collective-permute-done.1 = bf16[144,128]{1,0:T(8,128)(2,1)S(1)} collective-permute-done((bf16[144,128]{1,0:T(8,128)(2,1)S(1)}, bf16[144,128]{1,0:T(8,128)(2,1)S(1)}, u32[]{:S(2)}, u32[]{:S(2)}) %collective-permute-start.1) | collective-permute-done | bytes 36896 | tf_op jit(solution)/shard_map/ppermute | solution.py:182
  6.4 0.0 collective-permute-done
  6.4 1.7 %collective-permute-start.2 = (bf16[80,128]{1,0:T(8,128)(2,1)S(1)}, bf16[80,128]{1,0:T(8,128)(2,1)S(1)}, u32[]{:S(2)}, u32[]{:S(2)}) collective-permute-start(bf16[80,128]{1,0:T(8,128)(2,1)S(1)} %pad_maximum_fusion.1), channel_id=1, source_target_pairs={{0,4},{1,5},{2,6},{3,7},{4,0},{5,1},{6,2},{7,3},{8,12},{9,13},{10,... | collective-permute-start | bytes 61448 | tf_op jit(solution)/shard_map/ppermute | solution.py:182
  8.2 0.5 %fold.1.folded_ref = bf16[256,1024]{1,0:T(8,128)(2,1)S(1)} custom-call(bf16[512,256]{1,0:T(8,128)(2,1)S(1)} %get-tuple-element.24.matrix_ref, bf16[512,256]{1,0:T(8,128)(2,1)S(1)} %get-tuple-element.26.rest_ref, bf16[4,64,256]{2,1,0:T(8,128)(2,1)S(1)} %get-tuple-element.27.in_ref), custom_call_target="tpu_custom_call" | custom-call | tf_op jit(solution)/shard_map/fold/pallas_call | solution.py:233
  8.6 0.0 collective-permute-done.4.a_ref
  8.6 0.2 %collective-permute-start.5 = (bf16[4,16,256]{2,1,0:T(8,128)(2,1)S(1)}, bf16[4,16,256]{2,1,0:T(8,128)(2,1)S(1)}, u32[]{:S(2)}, u32[]{:S(2)}) collective-permute-start(bf16[4,16,256]{2,1,0:T(8,128)(2,1)S(1)} %get-tuple-element.30.adj_ref), channel_id=1, source_target_pairs={{2,4},{3,5},{4,2},{5,3},{6,8},{7,9},{8,6},{9,7},{10,12},{11,13},{1... | collective-permute-start | bytes 98312 | tf_op jit(solution)/shard_map/ppermute | solution.py:247
  8.9 1.4 %collective-permute-done.2 = bf16[80,128]{1,0:T(8,128)(2,1)S(1)} collective-permute-done((bf16[80,128]{1,0:T(8,128)(2,1)S(1)}, bf16[80,128]{1,0:T(8,128)(2,1)S(1)}, u32[]{:S(2)}, u32[]{:S(2)}) %collective-permute-start.2) | collective-permute-done | bytes 20512 | tf_op jit(solution)/shard_map/ppermute | solution.py:182
  10.3 0.1 collective-permute-start.6
  10.4 2.8 %collective-permute-start.3 = (bf16[64,128]{1,0:T(8,128)(2,1)S(1)}, bf16[64,128]{1,0:T(8,128)(2,1)S(1)}, u32[]{:S(2)}, u32[]{:S(2)}) collective-permute-start(bf16[64,128]{1,0:T(8,128)(2,1)S(1)} %pad_maximum_fusion.2), channel_id=1, source_target_pairs={{0,9},{1,8},{2,11},{3,10},{4,13},{5,12},{6,15},{7,14},{8,1},{9,0},... | collective-permute-start | bytes 49160 | tf_op jit(solution)/shard_map/ppermute | solution.py:182
  13.2 0.0 collective-permute-done.5.b_ref
  13.2 0.0 collective-permute-done.6.kept_ref
  13.2 1.1 %near.1.base_ref = f32[4,16,256]{2,1,0:T(8,128)S(1)} custom-call(s32[4,3]{1,0:T(4,128)} %src_hbm.3, bf16[4,16,256]{2,1,0:T(8,128)(2,1)S(1)} %get-tuple-element.30.adj_ref, bf16[4,16,256]{2,1,0:T(8,128)(2,1)S(1)} %collective-permute-done.4.a_ref, bf16[4,16,256]{2,1,0:T(8,128)(2,1)S(1)} %collective-permute-done.5.b_ref, ...), custom_call_target="tpu_custom_call" | custom-call | tf_op jit(solution)/shard_map/near/pallas_call | solution.py:269
  14.3 0.4 %collective-permute-done.3.got_ref = bf16[64,128]{1,0:T(8,128)(2,1)S(1)} collective-permute-done((bf16[64,128]{1,0:T(8,128)(2,1)S(1)}, bf16[64,128]{1,0:T(8,128)(2,1)S(1)}, u32[]{:S(2)}, u32[]{:S(2)}) %collective-permute-start.3) | collective-permute-done | bytes 16416 | tf_op jit(solution)/shard_map/ppermute | solution.py:182
  14.6 0.9 %final.1 = f32[4,16,256]{2,1,0:T(8,128)} custom-call(bf16[64,128]{1,0:T(8,128)(2,1)S(1)} %collective-permute-done.3.got_ref, bf16[256,1024]{1,0:T(8,128)(2,1)S(1)} %fold.1.folded_ref, bf16[4,64,256]{2,1,0:T(8,128)(2,1)S(1)} %get-tuple-element.27.in_ref, f32[4,16,256]{2,1,0:T(8,128)S(1)} %near.1.base_ref), custom_call_target="tpu_custom_call" | custom-call | tf_op jit(solution)/shard_map/final/pallas_call | solution.py:283
  (11 shorter events, 0.1 us)
Async XLA Ops:
  1.5 4.9 %collective-permute-start = (f32[144,128]{1,0:T(8,128)S(1)}, f32[144,128]{1,0:T(8,128)S(1)}, u32[]{:S(2)}, u32[]{:S(2)}) collective-permute-start(f32[144,128]{1,0:T(8,128)S(1)} %get-tuple-element.19), channel_id=1, source_target_pairs={{0,1},{1,0},{2,3},{3,2},{4,5},{5,4},{6,7},{7,6},{8,9},{9,8},{10,11... | collective-permute-start | bytes 221192 | tf_op jit(solution)/shard_map/ppermute | solution.py:182
  2.0 4.4 %collective-permute-start.1 = (bf16[144,128]{1,0:T(8,128)(2,1)S(1)}, bf16[144,128]{1,0:T(8,128)(2,1)S(1)}, u32[]{:S(2)}, u32[]{:S(2)}) collective-permute-start(bf16[144,128]{1,0:T(8,128)(2,1)S(1)} %get-tuple-element.21), channel_id=1, source_target_pairs={{0,3},{1,2},{2,1},{3,0},{4,7},{5,6},{6,5},{7,4},{8,11},{9,10},{10,... | collective-permute-start | bytes 110600 | tf_op jit(solution)/shard_map/ppermute | solution.py:182
  4.6 4.0 %collective-permute-start.4 = (bf16[4,16,256]{2,1,0:T(8,128)(2,1)S(1)}, bf16[4,16,256]{2,1,0:T(8,128)(2,1)S(1)}, u32[]{:S(2)}, u32[]{:S(2)}) collective-permute-start(bf16[4,16,256]{2,1,0:T(8,128)(2,1)S(1)} %get-tuple-element.30.adj_ref), channel_id=1, source_target_pairs={{0,2},{1,3},{2,0},{3,1},{4,6},{5,7},{6,4},{7,5},{8,10},{9,11},{10,... | collective-permute-start | bytes 98312 | tf_op jit(solution)/shard_map/ppermute | solution.py:182
  6.4 3.8 %collective-permute-start.2 = (bf16[80,128]{1,0:T(8,128)(2,1)S(1)}, bf16[80,128]{1,0:T(8,128)(2,1)S(1)}, u32[]{:S(2)}, u32[]{:S(2)}) collective-permute-start(bf16[80,128]{1,0:T(8,128)(2,1)S(1)} %pad_maximum_fusion.1), channel_id=1, source_target_pairs={{0,4},{1,5},{2,6},{3,7},{4,0},{5,1},{6,2},{7,3},{8,12},{9,13},{10,... | collective-permute-start | bytes 61448 | tf_op jit(solution)/shard_map/ppermute | solution.py:182
  8.6 4.6 %collective-permute-start.5 = (bf16[4,16,256]{2,1,0:T(8,128)(2,1)S(1)}, bf16[4,16,256]{2,1,0:T(8,128)(2,1)S(1)}, u32[]{:S(2)}, u32[]{:S(2)}) collective-permute-start(bf16[4,16,256]{2,1,0:T(8,128)(2,1)S(1)} %get-tuple-element.30.adj_ref), channel_id=1, source_target_pairs={{2,4},{3,5},{4,2},{5,3},{6,8},{7,9},{8,6},{9,7},{10,12},{11,13},{1... | collective-permute-start | bytes 98312 | tf_op jit(solution)/shard_map/ppermute | solution.py:247
  10.3 2.9 %collective-permute-start.6 = (f32[64,128]{1,0:T(8,128)S(1)}, f32[64,128]{1,0:T(8,128)S(1)}, u32[]{:S(2)}, u32[]{:S(2)}) collective-permute-start(f32[64,128]{1,0:T(8,128)S(1)} %pad_maximum_fusion), channel_id=1, source_target_pairs={{0,1},{1,0},{2,3},{3,2},{4,5},{5,4},{6,7},{7,6},{8,9},{9,8},{10,11... | collective-permute-start | bytes 98312 | tf_op jit(solution)/shard_map/ppermute | solution.py:182
  10.4 4.2 %collective-permute-start.3 = (bf16[64,128]{1,0:T(8,128)(2,1)S(1)}, bf16[64,128]{1,0:T(8,128)(2,1)S(1)}, u32[]{:S(2)}, u32[]{:S(2)}) collective-permute-start(bf16[64,128]{1,0:T(8,128)(2,1)S(1)} %pad_maximum_fusion.2), channel_id=1, source_target_pairs={{0,9},{1,8},{2,11},{3,10},{4,13},{5,12},{6,15},{7,14},{8,1},{9,0},... | collective-permute-start | bytes 49160 | tf_op jit(solution)/shard_map/ppermute | solution.py:182

commit v8 on v7

--- a/solution.py
+++ b/solution.py
@@ -230,31 +230,29 @@
         name="top",
     )(in_hbm(top_src), top, down, in_hbm(near_tiles), in_hbm(leaf_basis_in))
 
-    folded = pl.pallas_call(
-        fold_kernel,
-        out_shape=jax.ShapeDtypeStruct((nodes // 2 * rank, leaf_dev * cells), BF16),
-        in_specs=[VMEM] * 3,
-        out_specs=VMEM,
-        compiler_params=PARAMS,
-        name="fold",
-    )(matrix, rest, basis_in)
-
     inner = [(i, i + 1 if i % 2 else i - 1) for i in range(1, nodes - 1)]
     other = [(i * cores + c, j * cores + c) for i, j in inner for c in range(cores)]
     other += [(i * cores + c, i * cores + (c + 1) % cores) for i in (0, nodes - 1) for c in range(cores)]
     send, _ = lax.optimization_barrier((send, keep))
     a = swapped(lax.optimization_barrier((adjoint_v, send, keep))[0], lambda i: i ^ 1, False)
-    b = lax.ppermute(lax.optimization_barrier((adjoint_v, a, folded))[0], NODE_AXES + ("sub",), other)
-
-    coefs = None
+
     for step in range(steps):
-        flip = step in (0, steps - 1)
+        flip = step in (0, 1)
         half = (nodes >> (step + 1)) * rows
         if step:
             send = jnp.concatenate([keep[half:].astype(BF16)] + coefs, axis=0)
-            keep = keep[:half]
-            if flip:
-                keep = jnp.concatenate([keep] + [coef.astype(F32) for coef in coefs], axis=0)
+            keep = jnp.concatenate([keep[:half]] + [coef.astype(F32) for coef in coefs], axis=0)
+        if step == 1:
+            b = lax.ppermute(lax.optimization_barrier((adjoint_v, send, keep))[0], NODE_AXES + ("sub",), other)
+        if step == steps - 1:
+            folded = pl.pallas_call(
+                fold_kernel,
+                out_shape=jax.ShapeDtypeStruct((nodes // 2 * rank, leaf_dev * cells), BF16),
+                in_specs=[VMEM] * 3,
+                out_specs=VMEM,
+                compiler_params=PARAMS,
+                name="fold",
+            )(lax.optimization_barrier((matrix, send))[0], rest, basis_in)
         got = swapped(send, lambda i: i ^ (1 << step), flip)
         if flip:
             keep = swapped(keep, lambda i: i, True)
@@ -262,7 +260,7 @@
             got, _ = lax.optimization_barrier((got, matrix))
             coefs = [jnp.where(jnp.arange(wide) < rank, keep[half:].astype(BF16), got[half:])]
         elif step < steps - 1:
-            coefs.append(got[half:])
+            coefs = [keep[half:].astype(BF16), got[half:]]
         if step < steps - 1:
             keep = keep[:half] + got[:half].astype(F32)
 

time: 15.7 us -> 15.6 us (level)
  waiting for transfers between devices: 2.31 us -> 1.91 us
  starting transfers between devices: 7.98 us -> 8.2 us
    ppermute x6, waiting for transfers between devices: 2.31 us -> 1.91 us  [swapped(): return lax.ppermute(x, NODE_AXES + ('sub',), pairs)]
    ppermute x1, starting transfers between devices: 0.23 us -> 0.45 us  [on_device(): lax.ppermute(lax.optimization_barrier((adjoint_v, send, keep))[0], NODE_A...]
  transfers between devices with their start and end apart: 7 -> 7, of which waited for: 3 -> 3; matrix products, arithmetic and copies ran while one was open for 0% -> 0% of each run, Pallas kernels for 17% -> 18%
where the time goes in v8:
time: 15.6 us; the launch traced here: 15.4 us
  starting transfers between devices  8.2 us (53%)
  Pallas kernels  5.07 us (32%)
  waiting for transfers between devices  1.91 us (12%)
    ppermute x6, starting transfers between devices, swapped(): return lax.ppermute(x, NODE_AXES + ('sub',), pairs)  7.75 us
    ppermute x6, waiting for transfers between devices, swapped(): return lax.ppermute(x, NODE_AXES + ('sub',), pairs)  1.91 us
    pallas_call x1, Pallas kernels, on_device(): pl.pallas_call(functools.partial(source_kernel, nodes), out_shape=(jax.Sh...  1.47 us
    pallas_call x1, Pallas kernels, on_device(): pl.pallas_call(top_kernel, out_shape=(jax.ShapeDtypeStruct((nodes * rank,...  1.18 us
    pallas_call x1, Pallas kernels, on_device(): pl.pallas_call(near_kernel, out_shape=jax.ShapeDtypeStruct((leaf_dev, vec...  1.07 us
    pallas_call x1, Pallas kernels, on_device(): pl.pallas_call(final_kernel, out_shape=jax.ShapeDtypeStruct((leaf_dev, ve...  0.89 us
    pallas_call x1, Pallas kernels, on_device(): pl.pallas_call(fold_kernel, out_shape=jax.ShapeDtypeStruct((nodes // 2 *...  0.45 us
    ppermute x1, starting transfers between devices, on_device(): lax.ppermute(lax.optimization_barrier((adjoint_v, send, keep))[0], NODE_A...  0.45 us
  transfers between devices with their start and end apart: 7, of which 3 were waited for; matrix products, arithmetic and copies ran while one was open for 0% of the time, Pallas kernels for 18%

profile of v8, /device:TPU:0, one launch (start us, length us, event | category | flops | bytes accessed | tf_op | source)
XLA Modules:
  0.0 15.4 jit_solution(15662038895569045317)
XLA Ops:
  0.0 1.5 %source.1 = (bf16[144,128]{1,0:T(8,128)(2,1)S(1)}, f32[144,128]{1,0:T(8,128)S(1)}, bf16[4,16,256]{2,1,0:T(8,128)(2,1)S(1)}, bf16[1,64,1024]{2,1,0:T(8,128)(2,1)S...) custom-call(s32[4,8]{1,0:T(4,128)} %refs_0_.1, bf16[4,16,256]{2,1,0:T(8,128)(2,1)} %refs_1_.1, ...), custom_call_target="tpu_custom_call" | custom-call | tf_op jit(solution)/shard_map/source/pallas_call | solution.py:190
  1.5 0.5 %collective-permute-start = (f32[144,128]{1,0:T(8,128)S(1)}, f32[144,128]{1,0:T(8,128)S(1)}, u32[]{:S(2)}, u32[]{:S(2)}) collective-permute-start(f32[144,128]{1,0:T(8,128)S(1)} %get-tuple-element.20), channel_id=1, source_target_pairs={{0,1},{1,0},{2,3},{3,2},{4,5},{5,4},{6,7},{7,6},{8,9},{9,8},{10,11... | collective-permute-start | bytes 221192 | tf_op jit(solution)/shard_map/ppermute | solution.py:182
  2.0 2.6 %collective-permute-start.1 = (bf16[144,128]{1,0:T(8,128)(2,1)S(1)}, bf16[144,128]{1,0:T(8,128)(2,1)S(1)}, u32[]{:S(2)}, u32[]{:S(2)}) collective-permute-start(bf16[144,128]{1,0:T(8,128)(2,1)S(1)} %get-tuple-element.22), channel_id=1, source_target_pairs={{0,3},{1,2},{2,1},{3,0},{4,7},{5,6},{6,5},{7,4},{8,11},{9,10},{10,... | collective-permute-start | bytes 110600 | tf_op jit(solution)/shard_map/ppermute | solution.py:182
  4.6 0.0 collective-permute-start.5
  4.7 1.2 %top.1 = (bf16[512,256]{1,0:T(8,128)(2,1)S(1)}, bf16[512,256]{1,0:T(8,128)(2,1)S(1)}, bf16[2,768,256]{2,1,0:T(8,128)(2,1)S(1)}, bf16[4,64,256]{2,1,0:T(8,128)(2,1)S(1)}) custom-call(s32[1,16]{1,0:T(1,128)} %src_hbm.2, bf16[1,64,1024]{2,1,0:T(8,128)(2,1)S(1)} %get-tuple-element.23.top_ref, bf16[1,64,256]{2,1,0:T(8,128)(2,1)S(1)} %get-tuple-element.24.down_ref, ...), custom_call_target="tpu_custom_call" | custom-call | tf_op jit(solution)/shard_map/top/pallas_call | solution.py:214
  5.8 0.5 %collective-permute-done.1 = bf16[144,128]{1,0:T(8,128)(2,1)S(1)} collective-permute-done((bf16[144,128]{1,0:T(8,128)(2,1)S(1)}, bf16[144,128]{1,0:T(8,128)(2,1)S(1)}, u32[]{:S(2)}, u32[]{:S(2)}) %collective-permute-start.1) | collective-permute-done | bytes 36896 | tf_op jit(solution)/shard_map/ppermute | solution.py:182
  6.4 0.0 collective-permute-done
  6.4 1.8 %collective-permute-start.3 = (bf16[80,128]{1,0:T(8,128)(2,1)S(1)}, bf16[80,128]{1,0:T(8,128)(2,1)S(1)}, u32[]{:S(2)}, u32[]{:S(2)}) collective-permute-start(bf16[80,128]{1,0:T(8,128)(2,1)S(1)} %pad_maximum_fusion.2), channel_id=1, source_target_pairs={{0,5},{1,4},{2,7},{3,6},{4,1},{5,0},{6,3},{7,2},{8,13},{9,12},{10,... | collective-permute-start | bytes 61448 | tf_op jit(solution)/shard_map/ppermute | solution.py:182
  8.2 0.1 collective-permute-start.2
  8.3 0.4 %collective-permute-start.6 = (bf16[4,16,256]{2,1,0:T(8,128)(2,1)S(1)}, bf16[4,16,256]{2,1,0:T(8,128)(2,1)S(1)}, u32[]{:S(2)}, u32[]{:S(2)}) collective-permute-start(bf16[4,16,256]{2,1,0:T(8,128)(2,1)S(1)} %get-tuple-element.32.adj_ref), channel_id=1, source_target_pairs={{2,4},{3,5},{4,2},{5,3},{6,8},{7,9},{8,6},{9,7},{10,12},{11,13},{1... | collective-permute-start | bytes 98312 | tf_op jit(solution)/shard_map/ppermute | solution.py:246
  8.7 1.0 %collective-permute-done.3 = bf16[80,128]{1,0:T(8,128)(2,1)S(1)} collective-permute-done((bf16[80,128]{1,0:T(8,128)(2,1)S(1)}, bf16[80,128]{1,0:T(8,128)(2,1)S(1)}, u32[]{:S(2)}, u32[]{:S(2)}) %collective-permute-start.3) | collective-permute-done | bytes 20512 | tf_op jit(solution)/shard_map/ppermute | solution.py:182
  9.7 0.0 collective-permute-done.2
  9.8 2.7 %collective-permute-start.4 = (bf16[64,128]{1,0:T(8,128)(2,1)S(1)}, bf16[64,128]{1,0:T(8,128)(2,1)S(1)}, u32[]{:S(2)}, u32[]{:S(2)}) collective-permute-start(bf16[64,128]{1,0:T(8,128)(2,1)S(1)} %pad_maximum_fusion.3), channel_id=1, source_target_pairs={{0,8},{1,9},{2,10},{3,11},{4,12},{5,13},{6,14},{7,15},{8,0},{9,1},... | collective-permute-start | bytes 49160 | tf_op jit(solution)/shard_map/ppermute | solution.py:182
  12.5 0.5 %fold.1.folded_ref = bf16[256,1024]{1,0:T(8,128)(2,1)S(1)} custom-call(bf16[512,256]{1,0:T(8,128)(2,1)S(1)} %get-tuple-element.27.matrix_ref, bf16[512,256]{1,0:T(8,128)(2,1)S(1)} %get-tuple-element.28.rest_ref, bf16[4,64,256]{2,1,0:T(8,128)(2,1)S(1)} %get-tuple-element.29.in_ref), custom_call_target="tpu_custom_call" | custom-call | tf_op jit(solution)/shard_map/fold/pallas_call | solution.py:248
  13.0 0.0 collective-permute-done.5.a_ref
  13.0 0.0 collective-permute-done.6.b_ref
  13.0 1.1 %near.1.base_ref = f32[4,16,256]{2,1,0:T(8,128)S(1)} custom-call(s32[4,3]{1,0:T(4,128)} %src_hbm.3, bf16[4,16,256]{2,1,0:T(8,128)(2,1)S(1)} %get-tuple-element.32.adj_ref, bf16[4,16,256]{2,1,0:T(8,128)(2,1)S(1)} %collective-permute-done.5.a_ref, bf16[4,16,256]{2,1,0:T(8,128)(2,1)S(1)} %collective-permute-done.6.b_ref, ...), custom_call_target="tpu_custom_call" | custom-call | tf_op jit(solution)/shard_map/near/pallas_call | solution.py:267
  14.1 0.4 %collective-permute-done.4.got_ref = bf16[64,128]{1,0:T(8,128)(2,1)S(1)} collective-permute-done((bf16[64,128]{1,0:T(8,128)(2,1)S(1)}, bf16[64,128]{1,0:T(8,128)(2,1)S(1)}, u32[]{:S(2)}, u32[]{:S(2)}) %collective-permute-start.4) | collective-permute-done | bytes 16416 | tf_op jit(solution)/shard_map/ppermute | solution.py:182
  14.5 0.9 %final.1 = f32[4,16,256]{2,1,0:T(8,128)} custom-call(bf16[64,128]{1,0:T(8,128)(2,1)S(1)} %collective-permute-done.4.got_ref, bf16[256,1024]{1,0:T(8,128)(2,1)S(1)} %fold.1.folded_ref, bf16[4,64,256]{2,1,0:T(8,128)(2,1)S(1)} %get-tuple-element.29.in_ref, f32[4,16,256]{2,1,0:T(8,128)S(1)} %near.1.base_ref), custom_call_target="tpu_custom_call" | custom-call | tf_op jit(solution)/shard_map/final/pallas_call | solution.py:281
  (14 shorter events, 0.1 us)
Async XLA Ops:
  1.5 4.9 %collective-permute-start = (f32[144,128]{1,0:T(8,128)S(1)}, f32[144,128]{1,0:T(8,128)S(1)}, u32[]{:S(2)}, u32[]{:S(2)}) collective-permute-start(f32[144,128]{1,0:T(8,128)S(1)} %get-tuple-element.20), channel_id=1, source_target_pairs={{0,1},{1,0},{2,3},{3,2},{4,5},{5,4},{6,7},{7,6},{8,9},{9,8},{10,11... | collective-permute-start | bytes 221192 | tf_op jit(solution)/shard_map/ppermute | solution.py:182
  2.0 4.4 %collective-permute-start.1 = (bf16[144,128]{1,0:T(8,128)(2,1)S(1)}, bf16[144,128]{1,0:T(8,128)(2,1)S(1)}, u32[]{:S(2)}, u32[]{:S(2)}) collective-permute-start(bf16[144,128]{1,0:T(8,128)(2,1)S(1)} %get-tuple-element.22), channel_id=1, source_target_pairs={{0,3},{1,2},{2,1},{3,0},{4,7},{5,6},{6,5},{7,4},{8,11},{9,10},{10,... | collective-permute-start | bytes 110600 | tf_op jit(solution)/shard_map/ppermute | solution.py:182
  4.6 8.4 %collective-permute-start.5 = (bf16[4,16,256]{2,1,0:T(8,128)(2,1)S(1)}, bf16[4,16,256]{2,1,0:T(8,128)(2,1)S(1)}, u32[]{:S(2)}, u32[]{:S(2)}) collective-permute-start(bf16[4,16,256]{2,1,0:T(8,128)(2,1)S(1)} %get-tuple-element.32.adj_ref), channel_id=1, source_target_pairs={{0,2},{1,3},{2,0},{3,1},{4,6},{5,7},{6,4},{7,5},{8,10},{9,11},{10,... | collective-permute-start | bytes 98312 | tf_op jit(solution)/shard_map/ppermute | solution.py:182
  6.4 3.3 %collective-permute-start.3 = (bf16[80,128]{1,0:T(8,128)(2,1)S(1)}, bf16[80,128]{1,0:T(8,128)(2,1)S(1)}, u32[]{:S(2)}, u32[]{:S(2)}) collective-permute-start(bf16[80,128]{1,0:T(8,128)(2,1)S(1)} %pad_maximum_fusion.2), channel_id=1, source_target_pairs={{0,5},{1,4},{2,7},{3,6},{4,1},{5,0},{6,3},{7,2},{8,13},{9,12},{10,... | collective-permute-start | bytes 61448 | tf_op jit(solution)/shard_map/ppermute | solution.py:182
  8.2 1.5 %collective-permute-start.2 = (f32[80,128]{1,0:T(8,128)S(1)}, f32[80,128]{1,0:T(8,128)S(1)}, u32[]{:S(2)}, u32[]{:S(2)}) collective-permute-start(f32[80,128]{1,0:T(8,128)S(1)} %pad_maximum_fusion), channel_id=1, source_target_pairs={{0,1},{1,0},{2,3},{3,2},{4,5},{5,4},{6,7},{7,6},{8,9},{9,8},{10,11... | collective-permute-start | bytes 122888 | tf_op jit(solution)/shard_map/ppermute | solution.py:182
  8.3 4.7 %collective-permute-start.6 = (bf16[4,16,256]{2,1,0:T(8,128)(2,1)S(1)}, bf16[4,16,256]{2,1,0:T(8,128)(2,1)S(1)}, u32[]{:S(2)}, u32[]{:S(2)}) collective-permute-start(bf16[4,16,256]{2,1,0:T(8,128)(2,1)S(1)} %get-tuple-element.32.adj_ref), channel_id=1, source_target_pairs={{2,4},{3,5},{4,2},{5,3},{6,8},{7,9},{8,6},{9,7},{10,12},{11,13},{1... | collective-permute-start | bytes 98312 | tf_op jit(solution)/shard_map/ppermute | solution.py:246
  9.8 4.7 %collective-permute-start.4 = (bf16[64,128]{1,0:T(8,128)(2,1)S(1)}, bf16[64,128]{1,0:T(8,128)(2,1)S(1)}, u32[]{:S(2)}, u32[]{:S(2)}) collective-permute-start(bf16[64,128]{1,0:T(8,128)(2,1)S(1)} %pad_maximum_fusion.3), channel_id=1, source_target_pairs={{0,8},{1,9},{2,10},{3,11},{4,12},{5,13},{6,14},{7,15},{8,0},{9,1},... | collective-permute-start | bytes 49160 | tf_op jit(solution)/shard_map/ppermute | solution.py:182

commit v9 on v8

--- a/solution.py
+++ b/solution.py
@@ -66,10 +66,10 @@
     ]
     for copy in copies[3:5]:
         copy.wait()
-    for j in range(leaf_dev):
-        contrib = jnp.dot(coefs[j], far_ref[j], preferred_element_type=F32)
-        for k in range(far_count):
-            block = contrib[:, k // 2 * wide : (k // 2 + 1) * wide]
+    contribs = [jnp.dot(coefs[j], far_ref[j], preferred_element_type=F32) for j in range(leaf_dev)]
+    for k in range(far_count):
+        for j in range(leaf_dev):
+            block = contribs[j][:, k // 2 * wide : (k // 2 + 1) * wide]
             target = dst_ref[j, k]
             place = ((target >> within) ^ me) * pairs + ((target & (leaf_dev - 1)) >> 1)
             place += ((target ^ k) & 1) * (nodes * pairs)

time: 15.6 us -> 15.6 us (level)
  no operation moved by 1% of the time
where the time goes in v9:
time: 15.6 us; the launch traced here: 15.4 us
  starting transfers between devices  8.2 us (53%)
  Pallas kernels  5.07 us (32%)
  waiting for transfers between devices  1.91 us (12%)
    ppermute x6, starting transfers between devices, swapped(): return lax.ppermute(x, NODE_AXES + ('sub',), pairs)  7.75 us
    ppermute x6, waiting for transfers between devices, swapped(): return lax.ppermute(x, NODE_AXES + ('sub',), pairs)  1.91 us
    pallas_call x1, Pallas kernels, on_device(): pl.pallas_call(functools.partial(source_kernel, nodes), out_shape=(jax.Sh...  1.47 us
    pallas_call x1, Pallas kernels, on_device(): pl.pallas_call(top_kernel, out_shape=(jax.ShapeDtypeStruct((nodes * rank,...  1.18 us
    pallas_call x1, Pallas kernels, on_device(): pl.pallas_call(near_kernel, out_shape=jax.ShapeDtypeStruct((leaf_dev, vec...  1.07 us
    pallas_call x1, Pallas kernels, on_device(): pl.pallas_call(final_kernel, out_shape=jax.ShapeDtypeStruct((leaf_dev, ve...  0.89 us
    pallas_call x1, Pallas kernels, on_device(): pl.pallas_call(fold_kernel, out_shape=jax.ShapeDtypeStruct((nodes // 2 *...  0.45 us
    ppermute x1, starting transfers between devices, on_device(): lax.ppermute(lax.optimization_barrier((adjoint_v, send, keep))[0], NODE_A...  0.45 us
  transfers between devices with their start and end apart: 7, of which 3 were waited for; matrix products, arithmetic and copies ran while one was open for 0% of the time, Pallas kernels for 18%

profile of v9, /device:TPU:0, one launch (start us, length us, event | category | flops | bytes accessed | tf_op | source)
XLA Modules:
  0.0 15.4 jit_solution(2992172724350792831)
XLA Ops:
  0.0 1.5 %source.1 = (bf16[144,128]{1,0:T(8,128)(2,1)S(1)}, f32[144,128]{1,0:T(8,128)S(1)}, bf16[4,16,256]{2,1,0:T(8,128)(2,1)S(1)}, bf16[1,64,1024]{2,1,0:T(8,128)(2,1)S...) custom-call(s32[4,8]{1,0:T(4,128)} %refs_0_.1, bf16[4,16,256]{2,1,0:T(8,128)(2,1)} %refs_1_.1, ...), custom_call_target="tpu_custom_call" | custom-call | tf_op jit(solution)/shard_map/source/pallas_call | solution.py:190
  1.5 0.5 %collective-permute-start = (f32[144,128]{1,0:T(8,128)S(1)}, f32[144,128]{1,0:T(8,128)S(1)}, u32[]{:S(2)}, u32[]{:S(2)}) collective-permute-start(f32[144,128]{1,0:T(8,128)S(1)} %get-tuple-element.20), channel_id=1, source_target_pairs={{0,1},{1,0},{2,3},{3,2},{4,5},{5,4},{6,7},{7,6},{8,9},{9,8},{10,11... | collective-permute-start | bytes 221192 | tf_op jit(solution)/shard_map/ppermute | solution.py:182
  2.0 2.6 %collective-permute-start.1 = (bf16[144,128]{1,0:T(8,128)(2,1)S(1)}, bf16[144,128]{1,0:T(8,128)(2,1)S(1)}, u32[]{:S(2)}, u32[]{:S(2)}) collective-permute-start(bf16[144,128]{1,0:T(8,128)(2,1)S(1)} %get-tuple-element.22), channel_id=1, source_target_pairs={{0,3},{1,2},{2,1},{3,0},{4,7},{5,6},{6,5},{7,4},{8,11},{9,10},{10,... | collective-permute-start | bytes 110600 | tf_op jit(solution)/shard_map/ppermute | solution.py:182
  4.6 0.0 collective-permute-start.5
  4.7 1.2 %top.1 = (bf16[512,256]{1,0:T(8,128)(2,1)S(1)}, bf16[512,256]{1,0:T(8,128)(2,1)S(1)}, bf16[2,768,256]{2,1,0:T(8,128)(2,1)S(1)}, bf16[4,64,256]{2,1,0:T(8,128)(2,1)S(1)}) custom-call(s32[1,16]{1,0:T(1,128)} %src_hbm.2, bf16[1,64,1024]{2,1,0:T(8,128)(2,1)S(1)} %get-tuple-element.23.top_ref, bf16[1,64,256]{2,1,0:T(8,128)(2,1)S(1)} %get-tuple-element.24.down_ref, ...), custom_call_target="tpu_custom_call" | custom-call | tf_op jit(solution)/shard_map/top/pallas_call | solution.py:214
  5.8 0.5 %collective-permute-done.1 = bf16[144,128]{1,0:T(8,128)(2,1)S(1)} collective-permute-done((bf16[144,128]{1,0:T(8,128)(2,1)S(1)}, bf16[144,128]{1,0:T(8,128)(2,1)S(1)}, u32[]{:S(2)}, u32[]{:S(2)}) %collective-permute-start.1) | collective-permute-done | bytes 36896 | tf_op jit(solution)/shard_map/ppermute | solution.py:182
  6.4 0.0 collective-permute-done
  6.4 1.8 %collective-permute-start.3 = (bf16[80,128]{1,0:T(8,128)(2,1)S(1)}, bf16[80,128]{1,0:T(8,128)(2,1)S(1)}, u32[]{:S(2)}, u32[]{:S(2)}) collective-permute-start(bf16[80,128]{1,0:T(8,128)(2,1)S(1)} %pad_maximum_fusion.2), channel_id=1, source_target_pairs={{0,5},{1,4},{2,7},{3,6},{4,1},{5,0},{6,3},{7,2},{8,13},{9,12},{10,... | collective-permute-start | bytes 61448 | tf_op jit(solution)/shard_map/ppermute | solution.py:182
  8.2 0.1 collective-permute-start.2
  8.3 0.4 %collective-permute-start.6 = (bf16[4,16,256]{2,1,0:T(8,128)(2,1)S(1)}, bf16[4,16,256]{2,1,0:T(8,128)(2,1)S(1)}, u32[]{:S(2)}, u32[]{:S(2)}) collective-permute-start(bf16[4,16,256]{2,1,0:T(8,128)(2,1)S(1)} %get-tuple-element.32.adj_ref), channel_id=1, source_target_pairs={{2,4},{3,5},{4,2},{5,3},{6,8},{7,9},{8,6},{9,7},{10,12},{11,13},{1... | collective-permute-start | bytes 98312 | tf_op jit(solution)/shard_map/ppermute | solution.py:246
  8.7 1.0 %collective-permute-done.3 = bf16[80,128]{1,0:T(8,128)(2,1)S(1)} collective-permute-done((bf16[80,128]{1,0:T(8,128)(2,1)S(1)}, bf16[80,128]{1,0:T(8,128)(2,1)S(1)}, u32[]{:S(2)}, u32[]{:S(2)}) %collective-permute-start.3) | collective-permute-done | bytes 20512 | tf_op jit(solution)/shard_map/ppermute | solution.py:182
  9.7 0.0 collective-permute-done.2
  9.8 2.7 %collective-permute-start.4 = (bf16[64,128]{1,0:T(8,128)(2,1)S(1)}, bf16[64,128]{1,0:T(8,128)(2,1)S(1)}, u32[]{:S(2)}, u32[]{:S(2)}) collective-permute-start(bf16[64,128]{1,0:T(8,128)(2,1)S(1)} %pad_maximum_fusion.3), channel_id=1, source_target_pairs={{0,8},{1,9},{2,10},{3,11},{4,12},{5,13},{6,14},{7,15},{8,0},{9,1},... | collective-permute-start | bytes 49160 | tf_op jit(solution)/shard_map/ppermute | solution.py:182
  12.5 0.5 %fold.1.folded_ref = bf16[256,1024]{1,0:T(8,128)(2,1)S(1)} custom-call(bf16[512,256]{1,0:T(8,128)(2,1)S(1)} %get-tuple-element.27.matrix_ref, bf16[512,256]{1,0:T(8,128)(2,1)S(1)} %get-tuple-element.28.rest_ref, bf16[4,64,256]{2,1,0:T(8,128)(2,1)S(1)} %get-tuple-element.29.in_ref), custom_call_target="tpu_custom_call" | custom-call | tf_op jit(solution)/shard_map/fold/pallas_call | solution.py:248
  13.0 0.0 collective-permute-done.5.a_ref
  13.0 0.0 collective-permute-done.6.b_ref
  13.0 1.1 %near.1.base_ref = f32[4,16,256]{2,1,0:T(8,128)S(1)} custom-call(s32[4,3]{1,0:T(4,128)} %src_hbm.3, bf16[4,16,256]{2,1,0:T(8,128)(2,1)S(1)} %get-tuple-element.32.adj_ref, bf16[4,16,256]{2,1,0:T(8,128)(2,1)S(1)} %collective-permute-done.5.a_ref, bf16[4,16,256]{2,1,0:T(8,128)(2,1)S(1)} %collective-permute-done.6.b_ref, ...), custom_call_target="tpu_custom_call" | custom-call | tf_op jit(solution)/shard_map/near/pallas_call | solution.py:267
  14.1 0.4 %collective-permute-done.4.got_ref = bf16[64,128]{1,0:T(8,128)(2,1)S(1)} collective-permute-done((bf16[64,128]{1,0:T(8,128)(2,1)S(1)}, bf16[64,128]{1,0:T(8,128)(2,1)S(1)}, u32[]{:S(2)}, u32[]{:S(2)}) %collective-permute-start.4) | collective-permute-done | bytes 16416 | tf_op jit(solution)/shard_map/ppermute | solution.py:182
  14.5 0.9 %final.1 = f32[4,16,256]{2,1,0:T(8,128)} custom-call(bf16[64,128]{1,0:T(8,128)(2,1)S(1)} %collective-permute-done.4.got_ref, bf16[256,1024]{1,0:T(8,128)(2,1)S(1)} %fold.1.folded_ref, bf16[4,64,256]{2,1,0:T(8,128)(2,1)S(1)} %get-tuple-element.29.in_ref, f32[4,16,256]{2,1,0:T(8,128)S(1)} %near.1.base_ref), custom_call_target="tpu_custom_call" | custom-call | tf_op jit(solution)/shard_map/final/pallas_call | solution.py:281
  (14 shorter events, 0.1 us)
Async XLA Ops:
  1.5 4.9 %collective-permute-start = (f32[144,128]{1,0:T(8,128)S(1)}, f32[144,128]{1,0:T(8,128)S(1)}, u32[]{:S(2)}, u32[]{:S(2)}) collective-permute-start(f32[144,128]{1,0:T(8,128)S(1)} %get-tuple-element.20), channel_id=1, source_target_pairs={{0,1},{1,0},{2,3},{3,2},{4,5},{5,4},{6,7},{7,6},{8,9},{9,8},{10,11... | collective-permute-start | bytes 221192 | tf_op jit(solution)/shard_map/ppermute | solution.py:182
  2.0 4.4 %collective-permute-start.1 = (bf16[144,128]{1,0:T(8,128)(2,1)S(1)}, bf16[144,128]{1,0:T(8,128)(2,1)S(1)}, u32[]{:S(2)}, u32[]{:S(2)}) collective-permute-start(bf16[144,128]{1,0:T(8,128)(2,1)S(1)} %get-tuple-element.22), channel_id=1, source_target_pairs={{0,3},{1,2},{2,1},{3,0},{4,7},{5,6},{6,5},{7,4},{8,11},{9,10},{10,... | collective-permute-start | bytes 110600 | tf_op jit(solution)/shard_map/ppermute | solution.py:182
  4.6 8.4 %collective-permute-start.5 = (bf16[4,16,256]{2,1,0:T(8,128)(2,1)S(1)}, bf16[4,16,256]{2,1,0:T(8,128)(2,1)S(1)}, u32[]{:S(2)}, u32[]{:S(2)}) collective-permute-start(bf16[4,16,256]{2,1,0:T(8,128)(2,1)S(1)} %get-tuple-element.32.adj_ref), channel_id=1, source_target_pairs={{0,2},{1,3},{2,0},{3,1},{4,6},{5,7},{6,4},{7,5},{8,10},{9,11},{10,... | collective-permute-start | bytes 98312 | tf_op jit(solution)/shard_map/ppermute | solution.py:182
  6.4 3.3 %collective-permute-start.3 = (bf16[80,128]{1,0:T(8,128)(2,1)S(1)}, bf16[80,128]{1,0:T(8,128)(2,1)S(1)}, u32[]{:S(2)}, u32[]{:S(2)}) collective-permute-start(bf16[80,128]{1,0:T(8,128)(2,1)S(1)} %pad_maximum_fusion.2), channel_id=1, source_target_pairs={{0,5},{1,4},{2,7},{3,6},{4,1},{5,0},{6,3},{7,2},{8,13},{9,12},{10,... | collective-permute-start | bytes 61448 | tf_op jit(solution)/shard_map/ppermute | solution.py:182
  8.2 1.5 %collective-permute-start.2 = (f32[80,128]{1,0:T(8,128)S(1)}, f32[80,128]{1,0:T(8,128)S(1)}, u32[]{:S(2)}, u32[]{:S(2)}) collective-permute-start(f32[80,128]{1,0:T(8,128)S(1)} %pad_maximum_fusion), channel_id=1, source_target_pairs={{0,1},{1,0},{2,3},{3,2},{4,5},{5,4},{6,7},{7,6},{8,9},{9,8},{10,11... | collective-permute-start | bytes 122888 | tf_op jit(solution)/shard_map/ppermute | solution.py:182
  8.3 4.7 %collective-permute-start.6 = (bf16[4,16,256]{2,1,0:T(8,128)(2,1)S(1)}, bf16[4,16,256]{2,1,0:T(8,128)(2,1)S(1)}, u32[]{:S(2)}, u32[]{:S(2)}) collective-permute-start(bf16[4,16,256]{2,1,0:T(8,128)(2,1)S(1)} %get-tuple-element.32.adj_ref), channel_id=1, source_target_pairs={{2,4},{3,5},{4,2},{5,3},{6,8},{7,9},{8,6},{9,7},{10,12},{11,13},{1... | collective-permute-start | bytes 98312 | tf_op jit(solution)/shard_map/ppermute | solution.py:246
  9.8 4.7 %collective-permute-start.4 = (bf16[64,128]{1,0:T(8,128)(2,1)S(1)}, bf16[64,128]{1,0:T(8,128)(2,1)S(1)}, u32[]{:S(2)}, u32[]{:S(2)}) collective-permute-start(bf16[64,128]{1,0:T(8,128)(2,1)S(1)} %pad_maximum_fusion.3), channel_id=1, source_target_pairs={{0,8},{1,9},{2,10},{3,11},{4,12},{5,13},{6,14},{7,15},{8,0},{9,1},... | collective-permute-start | bytes 49160 | tf_op jit(solution)/shard_map/ppermute | solution.py:182

commit v10 on v8

--- a/solution.py
+++ b/solution.py
@@ -158,10 +158,10 @@
     rows = leaf_dev // 2 * vectors
     coefs = side_by_side(got_ref[rows:], vectors)
     mixed = side_by_side(got_ref[:rows], vectors)
-    for j in range(leaf_dev):
-        top = jnp.dot(coefs, folded_ref[:, j * cells : (j + 1) * cells], preferred_element_type=F32)
+    top = jnp.dot(coefs, folded_ref[...], preferred_element_type=F32)
+    for j in range(leaf_dev):
         far = jnp.dot(mixed[:, j * rank : (j + 1) * rank], in_ref[j], preferred_element_type=F32)
-        out_ref[j] = base_ref[j] + (top + far)
+        out_ref[j] = base_ref[j] + (top[:, j * cells : (j + 1) * cells] + far)
 
 
 def on_device(

time: 15.6 us -> 15.5 us (level)
  no operation moved by 1% of the time
where the time goes in v10:
time: 15.5 us; the launch traced here: 15.3 us
  starting transfers between devices  8.2 us (53%)
  Pallas kernels  5.02 us (32%)
  waiting for transfers between devices  1.91 us (12%)
    ppermute x6, starting transfers between devices, swapped(): return lax.ppermute(x, NODE_AXES + ('sub',), pairs)  7.75 us
    ppermute x6, waiting for transfers between devices, swapped(): return lax.ppermute(x, NODE_AXES + ('sub',), pairs)  1.91 us
    pallas_call x1, Pallas kernels, on_device(): pl.pallas_call(functools.partial(source_kernel, nodes), out_shape=(jax.Sh...  1.47 us
    pallas_call x1, Pallas kernels, on_device(): pl.pallas_call(top_kernel, out_shape=(jax.ShapeDtypeStruct((nodes * rank,...  1.18 us
    pallas_call x1, Pallas kernels, on_device(): pl.pallas_call(near_kernel, out_shape=jax.ShapeDtypeStruct((leaf_dev, vec...  1.07 us
    pallas_call x1, Pallas kernels, on_device(): pl.pallas_call(final_kernel, out_shape=jax.ShapeDtypeStruct((leaf_dev, ve...  0.84 us
    pallas_call x1, Pallas kernels, on_device(): pl.pallas_call(fold_kernel, out_shape=jax.ShapeDtypeStruct((nodes // 2 *...  0.45 us
    ppermute x1, starting transfers between devices, on_device(): lax.ppermute(lax.optimization_barrier((adjoint_v, send, keep))[0], NODE_A...  0.45 us
  transfers between devices with their start and end apart: 7, of which 3 were waited for; matrix products, arithmetic and copies ran while one was open for 0% of the time, Pallas kernels for 18%

profile of v10, /device:TPU:0, one launch (start us, length us, event | category | flops | bytes accessed | tf_op | source)
XLA Modules:
  0.0 15.3 jit_solution(5507067044219293851)
XLA Ops:
  0.0 1.5 %source.1 = (bf16[144,128]{1,0:T(8,128)(2,1)S(1)}, f32[144,128]{1,0:T(8,128)S(1)}, bf16[4,16,256]{2,1,0:T(8,128)(2,1)S(1)}, bf16[1,64,1024]{2,1,0:T(8,128)(2,1)S...) custom-call(s32[4,8]{1,0:T(4,128)} %refs_0_.1, bf16[4,16,256]{2,1,0:T(8,128)(2,1)} %refs_1_.1, ...), custom_call_target="tpu_custom_call" | custom-call | tf_op jit(solution)/shard_map/source/pallas_call | solution.py:190
  1.5 0.5 %collective-permute-start = (f32[144,128]{1,0:T(8,128)S(1)}, f32[144,128]{1,0:T(8,128)S(1)}, u32[]{:S(2)}, u32[]{:S(2)}) collective-permute-start(f32[144,128]{1,0:T(8,128)S(1)} %get-tuple-element.20), channel_id=1, source_target_pairs={{0,1},{1,0},{2,3},{3,2},{4,5},{5,4},{6,7},{7,6},{8,9},{9,8},{10,11... | collective-permute-start | bytes 221192 | tf_op jit(solution)/shard_map/ppermute | solution.py:182
  2.0 2.6 %collective-permute-start.1 = (bf16[144,128]{1,0:T(8,128)(2,1)S(1)}, bf16[144,128]{1,0:T(8,128)(2,1)S(1)}, u32[]{:S(2)}, u32[]{:S(2)}) collective-permute-start(bf16[144,128]{1,0:T(8,128)(2,1)S(1)} %get-tuple-element.22), channel_id=1, source_target_pairs={{0,3},{1,2},{2,1},{3,0},{4,7},{5,6},{6,5},{7,4},{8,11},{9,10},{10,... | collective-permute-start | bytes 110600 | tf_op jit(solution)/shard_map/ppermute | solution.py:182
  4.6 0.0 collective-permute-start.5
  4.7 1.2 %top.1 = (bf16[512,256]{1,0:T(8,128)(2,1)S(1)}, bf16[512,256]{1,0:T(8,128)(2,1)S(1)}, bf16[2,768,256]{2,1,0:T(8,128)(2,1)S(1)}, bf16[4,64,256]{2,1,0:T(8,128)(2,1)S(1)}) custom-call(s32[1,16]{1,0:T(1,128)} %src_hbm.2, bf16[1,64,1024]{2,1,0:T(8,128)(2,1)S(1)} %get-tuple-element.23.top_ref, bf16[1,64,256]{2,1,0:T(8,128)(2,1)S(1)} %get-tuple-element.24.down_ref, ...), custom_call_target="tpu_custom_call" | custom-call | tf_op jit(solution)/shard_map/top/pallas_call | solution.py:214
  5.8 0.5 %collective-permute-done.1 = bf16[144,128]{1,0:T(8,128)(2,1)S(1)} collective-permute-done((bf16[144,128]{1,0:T(8,128)(2,1)S(1)}, bf16[144,128]{1,0:T(8,128)(2,1)S(1)}, u32[]{:S(2)}, u32[]{:S(2)}) %collective-permute-start.1) | collective-permute-done | bytes 36896 | tf_op jit(solution)/shard_map/ppermute | solution.py:182
  6.4 0.0 collective-permute-done
  6.4 1.8 %collective-permute-start.3 = (bf16[80,128]{1,0:T(8,128)(2,1)S(1)}, bf16[80,128]{1,0:T(8,128)(2,1)S(1)}, u32[]{:S(2)}, u32[]{:S(2)}) collective-permute-start(bf16[80,128]{1,0:T(8,128)(2,1)S(1)} %pad_maximum_fusion.2), channel_id=1, source_target_pairs={{0,5},{1,4},{2,7},{3,6},{4,1},{5,0},{6,3},{7,2},{8,13},{9,12},{10,... | collective-permute-start | bytes 61448 | tf_op jit(solution)/shard_map/ppermute | solution.py:182
  8.2 0.1 collective-permute-start.2
  8.3 0.4 %collective-permute-start.6 = (bf16[4,16,256]{2,1,0:T(8,128)(2,1)S(1)}, bf16[4,16,256]{2,1,0:T(8,128)(2,1)S(1)}, u32[]{:S(2)}, u32[]{:S(2)}) collective-permute-start(bf16[4,16,256]{2,1,0:T(8,128)(2,1)S(1)} %get-tuple-element.32.adj_ref), channel_id=1, source_target_pairs={{2,4},{3,5},{4,2},{5,3},{6,8},{7,9},{8,6},{9,7},{10,12},{11,13},{1... | collective-permute-start | bytes 98312 | tf_op jit(solution)/shard_map/ppermute | solution.py:246
  8.7 1.0 %collective-permute-done.3 = bf16[80,128]{1,0:T(8,128)(2,1)S(1)} collective-permute-done((bf16[80,128]{1,0:T(8,128)(2,1)S(1)}, bf16[80,128]{1,0:T(8,128)(2,1)S(1)}, u32[]{:S(2)}, u32[]{:S(2)}) %collective-permute-start.3) | collective-permute-done | bytes 20512 | tf_op jit(solution)/shard_map/ppermute | solution.py:182
  9.7 0.0 collective-permute-done.2
  9.8 2.7 %collective-permute-start.4 = (bf16[64,128]{1,0:T(8,128)(2,1)S(1)}, bf16[64,128]{1,0:T(8,128)(2,1)S(1)}, u32[]{:S(2)}, u32[]{:S(2)}) collective-permute-start(bf16[64,128]{1,0:T(8,128)(2,1)S(1)} %pad_maximum_fusion.3), channel_id=1, source_target_pairs={{0,8},{1,9},{2,10},{3,11},{4,12},{5,13},{6,14},{7,15},{8,0},{9,1},... | collective-permute-start | bytes 49160 | tf_op jit(solution)/shard_map/ppermute | solution.py:182
  12.5 0.5 %fold.1.folded_ref = bf16[256,1024]{1,0:T(8,128)(2,1)S(1)} custom-call(bf16[512,256]{1,0:T(8,128)(2,1)S(1)} %get-tuple-element.27.matrix_ref, bf16[512,256]{1,0:T(8,128)(2,1)S(1)} %get-tuple-element.28.rest_ref, bf16[4,64,256]{2,1,0:T(8,128)(2,1)S(1)} %get-tuple-element.29.in_ref), custom_call_target="tpu_custom_call" | custom-call | tf_op jit(solution)/shard_map/fold/pallas_call | solution.py:248
  13.0 0.0 collective-permute-done.5.a_ref
  13.0 0.0 collective-permute-done.6.b_ref
  13.0 1.1 %near.1.base_ref = f32[4,16,256]{2,1,0:T(8,128)S(1)} custom-call(s32[4,3]{1,0:T(4,128)} %src_hbm.3, bf16[4,16,256]{2,1,0:T(8,128)(2,1)S(1)} %get-tuple-element.32.adj_ref, bf16[4,16,256]{2,1,0:T(8,128)(2,1)S(1)} %collective-permute-done.5.a_ref, bf16[4,16,256]{2,1,0:T(8,128)(2,1)S(1)} %collective-permute-done.6.b_ref, ...), custom_call_target="tpu_custom_call" | custom-call | tf_op jit(solution)/shard_map/near/pallas_call | solution.py:267
  14.1 0.4 %collective-permute-done.4.got_ref = bf16[64,128]{1,0:T(8,128)(2,1)S(1)} collective-permute-done((bf16[64,128]{1,0:T(8,128)(2,1)S(1)}, bf16[64,128]{1,0:T(8,128)(2,1)S(1)}, u32[]{:S(2)}, u32[]{:S(2)}) %collective-permute-start.4) | collective-permute-done | bytes 16416 | tf_op jit(solution)/shard_map/ppermute | solution.py:182
  14.5 0.8 %final.1 = f32[4,16,256]{2,1,0:T(8,128)} custom-call(bf16[64,128]{1,0:T(8,128)(2,1)S(1)} %collective-permute-done.4.got_ref, bf16[256,1024]{1,0:T(8,128)(2,1)S(1)} %fold.1.folded_ref, bf16[4,64,256]{2,1,0:T(8,128)(2,1)S(1)} %get-tuple-element.29.in_ref, f32[4,16,256]{2,1,0:T(8,128)S(1)} %near.1.base_ref), custom_call_target="tpu_custom_call" | custom-call | tf_op jit(solution)/shard_map/final/pallas_call | solution.py:281
  (14 shorter events, 0.1 us)
Async XLA Ops:
  1.5 4.9 %collective-permute-start = (f32[144,128]{1,0:T(8,128)S(1)}, f32[144,128]{1,0:T(8,128)S(1)}, u32[]{:S(2)}, u32[]{:S(2)}) collective-permute-start(f32[144,128]{1,0:T(8,128)S(1)} %get-tuple-element.20), channel_id=1, source_target_pairs={{0,1},{1,0},{2,3},{3,2},{4,5},{5,4},{6,7},{7,6},{8,9},{9,8},{10,11... | collective-permute-start | bytes 221192 | tf_op jit(solution)/shard_map/ppermute | solution.py:182
  2.0 4.4 %collective-permute-start.1 = (bf16[144,128]{1,0:T(8,128)(2,1)S(1)}, bf16[144,128]{1,0:T(8,128)(2,1)S(1)}, u32[]{:S(2)}, u32[]{:S(2)}) collective-permute-start(bf16[144,128]{1,0:T(8,128)(2,1)S(1)} %get-tuple-element.22), channel_id=1, source_target_pairs={{0,3},{1,2},{2,1},{3,0},{4,7},{5,6},{6,5},{7,4},{8,11},{9,10},{10,... | collective-permute-start | bytes 110600 | tf_op jit(solution)/shard_map/ppermute | solution.py:182
  4.6 8.4 %collective-permute-start.5 = (bf16[4,16,256]{2,1,0:T(8,128)(2,1)S(1)}, bf16[4,16,256]{2,1,0:T(8,128)(2,1)S(1)}, u32[]{:S(2)}, u32[]{:S(2)}) collective-permute-start(bf16[4,16,256]{2,1,0:T(8,128)(2,1)S(1)} %get-tuple-element.32.adj_ref), channel_id=1, source_target_pairs={{0,2},{1,3},{2,0},{3,1},{4,6},{5,7},{6,4},{7,5},{8,10},{9,11},{10,... | collective-permute-start | bytes 98312 | tf_op jit(solution)/shard_map/ppermute | solution.py:182
  6.4 3.3 %collective-permute-start.3 = (bf16[80,128]{1,0:T(8,128)(2,1)S(1)}, bf16[80,128]{1,0:T(8,128)(2,1)S(1)}, u32[]{:S(2)}, u32[]{:S(2)}) collective-permute-start(bf16[80,128]{1,0:T(8,128)(2,1)S(1)} %pad_maximum_fusion.2), channel_id=1, source_target_pairs={{0,5},{1,4},{2,7},{3,6},{4,1},{5,0},{6,3},{7,2},{8,13},{9,12},{10,... | collective-permute-start | bytes 61448 | tf_op jit(solution)/shard_map/ppermute | solution.py:182
  8.2 1.5 %collective-permute-start.2 = (f32[80,128]{1,0:T(8,128)S(1)}, f32[80,128]{1,0:T(8,128)S(1)}, u32[]{:S(2)}, u32[]{:S(2)}) collective-permute-start(f32[80,128]{1,0:T(8,128)S(1)} %pad_maximum_fusion), channel_id=1, source_target_pairs={{0,1},{1,0},{2,3},{3,2},{4,5},{5,4},{6,7},{7,6},{8,9},{9,8},{10,11... | collective-permute-start | bytes 122888 | tf_op jit(solution)/shard_map/ppermute | solution.py:182
  8.3 4.7 %collective-permute-start.6 = (bf16[4,16,256]{2,1,0:T(8,128)(2,1)S(1)}, bf16[4,16,256]{2,1,0:T(8,128)(2,1)S(1)}, u32[]{:S(2)}, u32[]{:S(2)}) collective-permute-start(bf16[4,16,256]{2,1,0:T(8,128)(2,1)S(1)} %get-tuple-element.32.adj_ref), channel_id=1, source_target_pairs={{2,4},{3,5},{4,2},{5,3},{6,8},{7,9},{8,6},{9,7},{10,12},{11,13},{1... | collective-permute-start | bytes 98312 | tf_op jit(solution)/shard_map/ppermute | solution.py:246
  9.8 4.7 %collective-permute-start.4 = (bf16[64,128]{1,0:T(8,128)(2,1)S(1)}, bf16[64,128]{1,0:T(8,128)(2,1)S(1)}, u32[]{:S(2)}, u32[]{:S(2)}) collective-permute-start(bf16[64,128]{1,0:T(8,128)(2,1)S(1)} %pad_maximum_fusion.3), channel_id=1, source_target_pairs={{0,8},{1,9},{2,10},{3,11},{4,12},{5,13},{6,14},{7,15},{8,0},{9,1},... | collective-permute-start | bytes 49160 | tf_op jit(solution)/shard_map/ppermute | solution.py:182

commit v11 on v10

--- a/solution.py
+++ b/solution.py
@@ -152,16 +152,23 @@
         base_ref[j] = total
 
 
-def final_kernel(got_ref, folded_ref, in_ref, base_ref, out_ref):
+def final_kernel(got_ref, folded_ref, in_ref, base_ref, out_hbm, out_ref, sems):
     leaf_dev, vectors, cells = base_ref.shape
     rank = in_ref.shape[1]
     rows = leaf_dev // 2 * vectors
     coefs = side_by_side(got_ref[rows:], vectors)
     mixed = side_by_side(got_ref[:rows], vectors)
+    copies, half = [], leaf_dev // 2
     top = jnp.dot(coefs, folded_ref[...], preferred_element_type=F32)
     for j in range(leaf_dev):
         far = jnp.dot(mixed[:, j * rank : (j + 1) * rank], in_ref[j], preferred_element_type=F32)
         out_ref[j] = base_ref[j] + (top[:, j * cells : (j + 1) * cells] + far)
+        if j % half == half - 1:
+            part = slice(j + 1 - half, j + 1)
+            copies.append(pltpu.make_async_copy(out_ref.at[part], out_hbm.at[part], sems.at[j // half]))
+            copies[-1].start()
+    for copy in copies:
+        copy.wait()
 
 
 def on_device(
@@ -282,7 +289,8 @@
         final_kernel,
         out_shape=jax.ShapeDtypeStruct((leaf_dev, vectors, cells), F32),
         in_specs=[VMEM] * 4,
-        out_specs=VMEM,
+        out_specs=HBM,
+        scratch_shapes=[pltpu.VMEM((leaf_dev, vectors, cells), F32), pltpu.SemaphoreType.DMA((2,))],
         compiler_params=PARAMS,
         name="final",
     )(got, folded, basis_in, base)

time: 15.5 us -> 15.5 us (level)
  no operation moved by 1% of the time
where the time goes in v11:
time: 15.5 us; the launch traced here: 15.3 us
  starting transfers between devices  8.2 us (53%)
  Pallas kernels  5.02 us (32%)
  waiting for transfers between devices  1.91 us (12%)
    ppermute x6, starting transfers between devices, swapped(): return lax.ppermute(x, NODE_AXES + ('sub',), pairs)  7.75 us
    ppermute x6, waiting for transfers between devices, swapped(): return lax.ppermute(x, NODE_AXES + ('sub',), pairs)  1.91 us
    pallas_call x1, Pallas kernels, on_device(): pl.pallas_call(functools.partial(source_kernel, nodes), out_shape=(jax.Sh...  1.47 us
    pallas_call x1, Pallas kernels, on_device(): pl.pallas_call(top_kernel, out_shape=(jax.ShapeDtypeStruct((nodes * rank,...  1.18 us
    pallas_call x1, Pallas kernels, on_device(): pl.pallas_call(near_kernel, out_shape=jax.ShapeDtypeStruct((leaf_dev, vec...  1.07 us
    pallas_call x1, Pallas kernels, on_device(): pl.pallas_call(final_kernel, out_shape=jax.ShapeDtypeStruct((leaf_dev, ve...  0.84 us
    pallas_call x1, Pallas kernels, on_device(): pl.pallas_call(fold_kernel, out_shape=jax.ShapeDtypeStruct((nodes // 2 *...  0.45 us
    ppermute x1, starting transfers between devices, on_device(): lax.ppermute(lax.optimization_barrier((adjoint_v, send, keep))[0], NODE_A...  0.45 us
  transfers between devices with their start and end apart: 7, of which 3 were waited for; matrix products, arithmetic and copies ran while one was open for 0% of the time, Pallas kernels for 18%

profile of v11, /device:TPU:0, one launch (start us, length us, event | category | flops | bytes accessed | tf_op | source)
XLA Modules:
  0.0 15.3 jit_solution(13159370882540975423)
XLA Ops:
  0.0 1.5 %source.1 = (bf16[144,128]{1,0:T(8,128)(2,1)S(1)}, f32[144,128]{1,0:T(8,128)S(1)}, bf16[4,16,256]{2,1,0:T(8,128)(2,1)S(1)}, bf16[1,64,1024]{2,1,0:T(8,128)(2,1)S...) custom-call(s32[4,8]{1,0:T(4,128)} %refs_0_.1, bf16[4,16,256]{2,1,0:T(8,128)(2,1)} %refs_1_.1, ...), custom_call_target="tpu_custom_call" | custom-call | tf_op jit(solution)/shard_map/source/pallas_call | solution.py:197
  1.5 0.5 %collective-permute-start = (f32[144,128]{1,0:T(8,128)S(1)}, f32[144,128]{1,0:T(8,128)S(1)}, u32[]{:S(2)}, u32[]{:S(2)}) collective-permute-start(f32[144,128]{1,0:T(8,128)S(1)} %get-tuple-element.20), channel_id=1, source_target_pairs={{0,1},{1,0},{2,3},{3,2},{4,5},{5,4},{6,7},{7,6},{8,9},{9,8},{10,11... | collective-permute-start | bytes 221192 | tf_op jit(solution)/shard_map/ppermute | solution.py:189
  2.0 2.6 %collective-permute-start.1 = (bf16[144,128]{1,0:T(8,128)(2,1)S(1)}, bf16[144,128]{1,0:T(8,128)(2,1)S(1)}, u32[]{:S(2)}, u32[]{:S(2)}) collective-permute-start(bf16[144,128]{1,0:T(8,128)(2,1)S(1)} %get-tuple-element.22), channel_id=1, source_target_pairs={{0,3},{1,2},{2,1},{3,0},{4,7},{5,6},{6,5},{7,4},{8,11},{9,10},{10,... | collective-permute-start | bytes 110600 | tf_op jit(solution)/shard_map/ppermute | solution.py:189
  4.6 0.0 collective-permute-start.5
  4.7 1.2 %top.1 = (bf16[512,256]{1,0:T(8,128)(2,1)S(1)}, bf16[512,256]{1,0:T(8,128)(2,1)S(1)}, bf16[2,768,256]{2,1,0:T(8,128)(2,1)S(1)}, bf16[4,64,256]{2,1,0:T(8,128)(2,1)S(1)}) custom-call(s32[1,16]{1,0:T(1,128)} %src_hbm.2, bf16[1,64,1024]{2,1,0:T(8,128)(2,1)S(1)} %get-tuple-element.23.top_ref, bf16[1,64,256]{2,1,0:T(8,128)(2,1)S(1)} %get-tuple-element.24.down_ref, ...), custom_call_target="tpu_custom_call" | custom-call | tf_op jit(solution)/shard_map/top/pallas_call | solution.py:221
  5.8 0.5 %collective-permute-done.1 = bf16[144,128]{1,0:T(8,128)(2,1)S(1)} collective-permute-done((bf16[144,128]{1,0:T(8,128)(2,1)S(1)}, bf16[144,128]{1,0:T(8,128)(2,1)S(1)}, u32[]{:S(2)}, u32[]{:S(2)}) %collective-permute-start.1) | collective-permute-done | bytes 36896 | tf_op jit(solution)/shard_map/ppermute | solution.py:189
  6.4 0.0 collective-permute-done
  6.4 1.8 %collective-permute-start.3 = (bf16[80,128]{1,0:T(8,128)(2,1)S(1)}, bf16[80,128]{1,0:T(8,128)(2,1)S(1)}, u32[]{:S(2)}, u32[]{:S(2)}) collective-permute-start(bf16[80,128]{1,0:T(8,128)(2,1)S(1)} %pad_maximum_fusion.2), channel_id=1, source_target_pairs={{0,5},{1,4},{2,7},{3,6},{4,1},{5,0},{6,3},{7,2},{8,13},{9,12},{10,... | collective-permute-start | bytes 61448 | tf_op jit(solution)/shard_map/ppermute | solution.py:189
  8.2 0.1 collective-permute-start.2
  8.3 0.4 %collective-permute-start.6 = (bf16[4,16,256]{2,1,0:T(8,128)(2,1)S(1)}, bf16[4,16,256]{2,1,0:T(8,128)(2,1)S(1)}, u32[]{:S(2)}, u32[]{:S(2)}) collective-permute-start(bf16[4,16,256]{2,1,0:T(8,128)(2,1)S(1)} %get-tuple-element.32.adj_ref), channel_id=1, source_target_pairs={{2,4},{3,5},{4,2},{5,3},{6,8},{7,9},{8,6},{9,7},{10,12},{11,13},{1... | collective-permute-start | bytes 98312 | tf_op jit(solution)/shard_map/ppermute | solution.py:253
  8.7 1.0 %collective-permute-done.3 = bf16[80,128]{1,0:T(8,128)(2,1)S(1)} collective-permute-done((bf16[80,128]{1,0:T(8,128)(2,1)S(1)}, bf16[80,128]{1,0:T(8,128)(2,1)S(1)}, u32[]{:S(2)}, u32[]{:S(2)}) %collective-permute-start.3) | collective-permute-done | bytes 20512 | tf_op jit(solution)/shard_map/ppermute | solution.py:189
  9.7 0.0 collective-permute-done.2
  9.8 2.7 %collective-permute-start.4 = (bf16[64,128]{1,0:T(8,128)(2,1)S(1)}, bf16[64,128]{1,0:T(8,128)(2,1)S(1)}, u32[]{:S(2)}, u32[]{:S(2)}) collective-permute-start(bf16[64,128]{1,0:T(8,128)(2,1)S(1)} %pad_maximum_fusion.3), channel_id=1, source_target_pairs={{0,8},{1,9},{2,10},{3,11},{4,12},{5,13},{6,14},{7,15},{8,0},{9,1},... | collective-permute-start | bytes 49160 | tf_op jit(solution)/shard_map/ppermute | solution.py:189
  12.5 0.5 %fold.1.folded_ref = bf16[256,1024]{1,0:T(8,128)(2,1)S(1)} custom-call(bf16[512,256]{1,0:T(8,128)(2,1)S(1)} %get-tuple-element.27.matrix_ref, bf16[512,256]{1,0:T(8,128)(2,1)S(1)} %get-tuple-element.28.rest_ref, bf16[4,64,256]{2,1,0:T(8,128)(2,1)S(1)} %get-tuple-element.29.in_ref), custom_call_target="tpu_custom_call" | custom-call | tf_op jit(solution)/shard_map/fold/pallas_call | solution.py:255
  13.0 0.0 collective-permute-done.5.a_ref
  13.0 0.0 collective-permute-done.6.b_ref
  13.0 1.1 %near.1.base_ref = f32[4,16,256]{2,1,0:T(8,128)S(1)} custom-call(s32[4,3]{1,0:T(4,128)} %src_hbm.3, bf16[4,16,256]{2,1,0:T(8,128)(2,1)S(1)} %get-tuple-element.32.adj_ref, bf16[4,16,256]{2,1,0:T(8,128)(2,1)S(1)} %collective-permute-done.5.a_ref, bf16[4,16,256]{2,1,0:T(8,128)(2,1)S(1)} %collective-permute-done.6.b_ref, ...), custom_call_target="tpu_custom_call" | custom-call | tf_op jit(solution)/shard_map/near/pallas_call | solution.py:274
  14.1 0.4 %collective-permute-done.4.got_ref = bf16[64,128]{1,0:T(8,128)(2,1)S(1)} collective-permute-done((bf16[64,128]{1,0:T(8,128)(2,1)S(1)}, bf16[64,128]{1,0:T(8,128)(2,1)S(1)}, u32[]{:S(2)}, u32[]{:S(2)}) %collective-permute-start.4) | collective-permute-done | bytes 16416 | tf_op jit(solution)/shard_map/ppermute | solution.py:189
  14.5 0.8 %final.1 = f32[4,16,256]{2,1,0:T(8,128)} custom-call(bf16[64,128]{1,0:T(8,128)(2,1)S(1)} %collective-permute-done.4.got_ref, bf16[256,1024]{1,0:T(8,128)(2,1)S(1)} %fold.1.folded_ref, bf16[4,64,256]{2,1,0:T(8,128)(2,1)S(1)} %get-tuple-element.29.in_ref, f32[4,16,256]{2,1,0:T(8,128)S(1)} %near.1.base_ref), custom_call_target="tpu_custom_call" | custom-call | tf_op jit(solution)/shard_map/final/pallas_call | solution.py:288
  (14 shorter events, 0.1 us)
Async XLA Ops:
  1.5 4.9 %collective-permute-start = (f32[144,128]{1,0:T(8,128)S(1)}, f32[144,128]{1,0:T(8,128)S(1)}, u32[]{:S(2)}, u32[]{:S(2)}) collective-permute-start(f32[144,128]{1,0:T(8,128)S(1)} %get-tuple-element.20), channel_id=1, source_target_pairs={{0,1},{1,0},{2,3},{3,2},{4,5},{5,4},{6,7},{7,6},{8,9},{9,8},{10,11... | collective-permute-start | bytes 221192 | tf_op jit(solution)/shard_map/ppermute | solution.py:189
  2.0 4.4 %collective-permute-start.1 = (bf16[144,128]{1,0:T(8,128)(2,1)S(1)}, bf16[144,128]{1,0:T(8,128)(2,1)S(1)}, u32[]{:S(2)}, u32[]{:S(2)}) collective-permute-start(bf16[144,128]{1,0:T(8,128)(2,1)S(1)} %get-tuple-element.22), channel_id=1, source_target_pairs={{0,3},{1,2},{2,1},{3,0},{4,7},{5,6},{6,5},{7,4},{8,11},{9,10},{10,... | collective-permute-start | bytes 110600 | tf_op jit(solution)/shard_map/ppermute | solution.py:189
  4.6 8.4 %collective-permute-start.5 = (bf16[4,16,256]{2,1,0:T(8,128)(2,1)S(1)}, bf16[4,16,256]{2,1,0:T(8,128)(2,1)S(1)}, u32[]{:S(2)}, u32[]{:S(2)}) collective-permute-start(bf16[4,16,256]{2,1,0:T(8,128)(2,1)S(1)} %get-tuple-element.32.adj_ref), channel_id=1, source_target_pairs={{0,2},{1,3},{2,0},{3,1},{4,6},{5,7},{6,4},{7,5},{8,10},{9,11},{10,... | collective-permute-start | bytes 98312 | tf_op jit(solution)/shard_map/ppermute | solution.py:189
  6.4 3.3 %collective-permute-start.3 = (bf16[80,128]{1,0:T(8,128)(2,1)S(1)}, bf16[80,128]{1,0:T(8,128)(2,1)S(1)}, u32[]{:S(2)}, u32[]{:S(2)}) collective-permute-start(bf16[80,128]{1,0:T(8,128)(2,1)S(1)} %pad_maximum_fusion.2), channel_id=1, source_target_pairs={{0,5},{1,4},{2,7},{3,6},{4,1},{5,0},{6,3},{7,2},{8,13},{9,12},{10,... | collective-permute-start | bytes 61448 | tf_op jit(solution)/shard_map/ppermute | solution.py:189
  8.2 1.5 %collective-permute-start.2 = (f32[80,128]{1,0:T(8,128)S(1)}, f32[80,128]{1,0:T(8,128)S(1)}, u32[]{:S(2)}, u32[]{:S(2)}) collective-permute-start(f32[80,128]{1,0:T(8,128)S(1)} %pad_maximum_fusion), channel_id=1, source_target_pairs={{0,1},{1,0},{2,3},{3,2},{4,5},{5,4},{6,7},{7,6},{8,9},{9,8},{10,11... | collective-permute-start | bytes 122888 | tf_op jit(solution)/shard_map/ppermute | solution.py:189
  8.3 4.7 %collective-permute-start.6 = (bf16[4,16,256]{2,1,0:T(8,128)(2,1)S(1)}, bf16[4,16,256]{2,1,0:T(8,128)(2,1)S(1)}, u32[]{:S(2)}, u32[]{:S(2)}) collective-permute-start(bf16[4,16,256]{2,1,0:T(8,128)(2,1)S(1)} %get-tuple-element.32.adj_ref), channel_id=1, source_target_pairs={{2,4},{3,5},{4,2},{5,3},{6,8},{7,9},{8,6},{9,7},{10,12},{11,13},{1... | collective-permute-start | bytes 98312 | tf_op jit(solution)/shard_map/ppermute | solution.py:253
  9.8 4.7 %collective-permute-start.4 = (bf16[64,128]{1,0:T(8,128)(2,1)S(1)}, bf16[64,128]{1,0:T(8,128)(2,1)S(1)}, u32[]{:S(2)}, u32[]{:S(2)}) collective-permute-start(bf16[64,128]{1,0:T(8,128)(2,1)S(1)} %pad_maximum_fusion.3), channel_id=1, source_target_pairs={{0,8},{1,9},{2,10},{3,11},{4,12},{5,13},{6,14},{7,15},{8,0},{9,1},... | collective-permute-start | bytes 49160 | tf_op jit(solution)/shard_map/ppermute | solution.py:189
